TPU v7x, 32 devices: a whole 2x2x4 slice. The times are simulated.
32 devices in a mesh: region: 4 (over x, core), sub: 8 (over z, y).
Axes of the slice: x: 2, y: 2, z: 4, core: 2. Of those that a mesh axis runs over, the one named last changes fastest.
Arguments:
- features: bfloat16 [256, 128, 256], P(('region', 'sub')), may hold values from -30 to 30
- voxel_mask: int32 [256, 128], P(('region', 'sub')), may hold values 0 or 1
- counts: int32 [32], replicated, may hold values from 4 to 8, as said below
- neighbors: int32 [256, 27], P(('region', 'sub')), may hold values from -1 to 255, as said below
- w_first: bfloat16 [6912, 256], replicated, may hold values from -0.15625 to 0.15625
- w_second: bfloat16 [6912, 256], replicated, may hold values from -0.15625 to 0.15625
- gain_first: float32 [256], replicated, may hold values from 0.1 to 1.9
- bias_first: float32 [256], replicated, may hold values from -3 to 3
- gain_second: float32 [256], replicated, may hold values from 0.1 to 1.9
- bias_second: float32 [256], replicated, may hold values from -3 to 3
- cotangent: bfloat16 [256, 128, 256], P(('region', 'sub')), may hold values from -30 to 30
Outputs:
- output: bfloat16 [256, 128, 256], P(('region', 'sub'))
- grad_features: bfloat16 [256, 128, 256], P(('region', 'sub'))
Inputs may be any that keep to these rules, and one draw needn't show every extreme that they name: `counts`: every device has at least one more live brick than 3; some device has 8 and some 3 + 1. `neighbors`: entry 13 of a live slot's row is the slot itself; a slot at or beyond its device's count has -1 in every entry. Slot b names slot c at offset o exactly when c names b at offset 26 - o. Every named slot is live and lies on the same device or on the device just before or just after it in the order of region+sub; a slot on the device after lies among that device's first 3 slots, a slot on the device before among its last 3 live slots.
All inputs are finite; a program needn't handle non-finite values. No bound on the sum of `voxel_mask` on one device may be relied on, other than what follows from the above.
Results may differ from a plain program's by a relative error of at most 0.003.
The roundings to bfloat16 on the way count: a program that leaves them out, or rounds other values in their place, can miss the bound.
Values may be sent and summed in bfloat16 or wider, within the bound.
No kernel may reach another device: no remote copies, remote signals or barrier semaphores. Data moves between devices by JAX's collectives and lax.ppermute only.
A program may use at most 128 MiB of HBM per device.

v0:
```python
import functools

import jax
import jax.numpy as jnp
from jax import lax
from jax.experimental import pallas as pl
from jax.experimental.pallas import tpu as pltpu
from jax.sharding import PartitionSpec as P

GC = 8
EDGE = 3
AXES = ("region", "sub")
eps_norm = 1e-05
MARK = 2.0**100
MARK_LIMIT = 2.0**90
VMEM_LIMIT = 56 * 2**20
f32 = jnp.float32
bf16 = jnp.bfloat16


def vmem():
    return pl.BlockSpec(memory_space=pltpu.VMEM)


def smem():
    return pl.BlockSpec(memory_space=pltpu.SMEM)


def hbm():
    return pl.BlockSpec(memory_space=pl.ANY)


def call(kernel, name, in_specs, outs, scratch=()):
    return pl.pallas_call(
        kernel,
        name=name,
        in_specs=in_specs,
        out_specs=[vmem() for _ in outs],
        out_shape=[jax.ShapeDtypeStruct(*o) for o in outs],
        scratch_shapes=list(scratch),
        compiler_params=pltpu.CompilerParams(vmem_limit_bytes=VMEM_LIMIT),
    )


def lane_of(shape):
    return lax.broadcasted_iota(jnp.int32, shape, len(shape) - 1) % GC


def spread_first(x):
    x = jnp.where(lane_of(x.shape) == 0, x, 0.0)
    for s in (1, 2, 4):
        x = x + pltpu.roll(x, s, 1)
    return x


def group_total(x):
    for s in (1, 2, 4):
        x = x + pltpu.roll(x, 128 - s, 1)
    return spread_first(x)


def halves(x):
    return x[:, :128], x[:, 128:]


def pack_row(values):
    lane = lane_of((1, 128))
    row = jnp.zeros((1, 128), f32)
    for k, value in enumerate(values):
        row = jnp.where(lane == k, value, row)
    return row


def unpack_row(rows, k):
    return spread_first(pltpu.roll(rows, 128 - k, 1) if k else rows)


def join(pair):
    return jnp.concatenate(pair, axis=1)


def column_sum(x):
    return jnp.sum(x, axis=0, keepdims=True)


def moments_row(sum_row, count_row, second_pass):
    sums = [group_total(h) for h in halves(sum_row)]
    count = count_row * float(GC)
    safe = jnp.maximum(count, 1.0)
    mean = join([s / safe for s in sums])
    squares = [group_total(h) for h in halves(second_pass(mean))]
    return pack_row([sums[0], sums[1], squares[0], squares[1], count])


def combine_moments(rows):
    count = unpack_row(rows, 4)
    total = column_sum(count)
    safe = jnp.maximum(count, 1.0)
    means, scales = [], []
    for k in (0, 1):
        sums = unpack_row(rows, k)
        mean = column_sum(sums) / total
        apart = sums / safe - mean
        spread = column_sum(unpack_row(rows, 2 + k) + count * (apart * apart)) / total
        means.append(mean)
        scales.append(lax.rsqrt(spread + eps_norm))
    return join(means), join(scales), join([total, total])


def combine_pairs(rows, total):
    summed = column_sum(rows)
    first = join([unpack_row(summed, 0), unpack_row(summed, 1)]) / total
    second = join([unpack_row(summed, 2), unpack_row(summed, 3)]) / total
    return first, second


def pairs_row(first, second):
    return pack_row([group_total(h) for h in (*halves(first), *halves(second))])


def eight_rows(x):
    return jnp.sum(x.reshape(16, 8, x.shape[-1]), axis=0)


def put_slot(source, slot, values):
    tile = values.reshape(16, 8, 256)
    source[1, slot] = tile
    source[0, slot] = pltpu.roll(tile, 1, 1)
    source[2, slot] = pltpu.roll(tile, 7, 1)


def build(index, brick, source, windows):
    z = lax.broadcasted_iota(jnp.int32, (1, 8, 256), 1)
    for slab in range(6):
        dx, x = (0, 3) if slab == 0 else (2, 0) if slab == 5 else (1, slab - 1)
        for l in range(3):
            parts = []
            for dy, y, n in ((0, 3, 1), (1, 0, 4), (2, 0, 1)):
                at = pl.ds(x * 4 + y, n)
                part = source[l, index[brick, dx * 9 + dy * 3 + 1], at]
                if l != 1:
                    edge = source[l, index[brick, dx * 9 + dy * 3 + l], at]
                    part = jnp.where(z == (0 if l == 0 else 7), edge, part)
                parts.append(part)
            columns = jnp.concatenate(parts, axis=0)
            for j in range(3):
                windows[j * 3 + l, slab * 32 : slab * 32 + 32, :] = (
                    columns[j : j + 4].reshape(32, 256).astype(bf16)
                )


def product(windows, weights, backward):
    total = None
    for i in range(3):
        for j in range(3):
            for l in range(3):
                o = i * 9 + j * 3 + l
                taken = windows[j * 3 + l, i * 32 : i * 32 + 128, :]
                if backward:
                    part = lax.dot_general(
                        taken, weights[26 - o], (((1,), (1,)), ((), ())), preferred_element_type=f32
                    )
                else:
                    part = jnp.dot(taken, weights[o], preferred_element_type=f32)
                total = part if total is None else total + part
    return total


def conv(index, source, window_pair, weights, backward, capacity, finish, carry):
    even, odd = window_pair
    build(index, 0, source, even)

    def two(step, carry):
        first = 2 * step
        build(index, first + 1, source, odd)
        carry = finish(first, product(even, weights, backward), carry)
        build(index, jnp.minimum(first + 2, capacity - 1), source, even)
        return finish(first + 1, product(odd, weights, backward), carry)

    return lax.fori_loop(0, capacity // 2, two, carry)


def conv_scratch(slots):
    return [
        pltpu.VMEM((3, slots, 16, 8, 256), f32),
        pltpu.VMEM((9, 192, 256), bf16),
        pltpu.VMEM((9, 192, 256), bf16),
        pltpu.VMEM((27, 256, 256), bf16),
        pltpu.SemaphoreType.DMA,
    ]


def each_slot(own, before, after, body):
    capacity = own[0].shape[0]

    def run(refs, start, count):
        def step(k, _):
            body(refs, k, start + k)
            return 0

        lax.fori_loop(0, count, step, 0)

    run(own, 0, capacity)
    run(before, capacity, EDGE)
    run(after, capacity + EDGE, EDGE)


def sigmoid(x):
    return 1.0 / (1.0 + jnp.exp(-x))


def start_kernel(counts, features, mask, cotangent, row, marked, feat_up, feat_down, cot_up, cot_down):
    capacity = features.shape[0]
    live = counts[0]

    def first_pass(b, carry):
        total, count = carry
        wide = jnp.broadcast_to(mask[pl.ds(b, 1), :].astype(f32), (128, 128)).T
        wide = wide * jnp.where(b < live, 1.0, 0.0)
        values = features[b].astype(f32)
        on = join([wide, wide])
        marked[b] = jnp.where(on > 0.5, values, MARK).astype(bf16)
        return total + eight_rows(values * on), count + eight_rows(wide)

    total, count = lax.fori_loop(
        0, capacity, first_pass, (jnp.zeros((8, 256), f32), jnp.zeros((8, 128), f32))
    )
    for k in range(EDGE):
        up = live - EDGE + k
        feat_up[k] = marked[up]
        feat_down[k] = marked[k]
        cot_up[k] = jnp.where(marked[up].astype(f32) < MARK_LIMIT, cotangent[up].astype(f32), 0.0).astype(bf16)
        cot_down[k] = jnp.where(marked[k].astype(f32) < MARK_LIMIT, cotangent[k].astype(f32), 0.0).astype(bf16)

    def second_pass(mean):
        def step(b, carry):
            values = marked[b].astype(f32)
            apart = jnp.where(values < MARK_LIMIT, values - mean, 0.0)
            return carry + eight_rows(apart * apart)

        return column_sum(lax.fori_loop(0, capacity, step, jnp.zeros((8, 256), f32)))

    packed = moments_row(column_sum(total), column_sum(count), second_pass)
    row[...] = jnp.broadcast_to(packed, row.shape)


def grad_conv_kernel(
    index, counts, cotangent, marked, before, after, weights_hbm, grad, up, down, source, even, odd, weights, sem
):
    capacity = cotangent.shape[0]
    fetch = pltpu.make_async_copy(weights_hbm, weights, sem)
    fetch.start()

    def own_slot(b, _):
        values = cotangent[b].astype(f32)
        put_slot(source, b, jnp.where(marked[b].astype(f32) < MARK_LIMIT, values, 0.0))
        return 0

    lax.fori_loop(0, capacity, own_slot, 0)
    for k in range(EDGE):
        put_slot(source, capacity + k, before[k].astype(f32))
        put_slot(source, capacity + EDGE + k, after[k].astype(f32))
    put_slot(source, capacity + 2 * EDGE, jnp.zeros((128, 256), f32))
    fetch.wait()

    def finish(b, total, carry):
        grad[b] = total
        return carry

    conv(index, source, (even, odd), weights, True, capacity, finish, 0)
    for k in range(EDGE):
        up[k] = grad[counts[0] - EDGE + k].astype(bf16)
        down[k] = grad[k].astype(bf16)


def first_conv_kernel(
    index, counts, rows, marked, before, after, gain, bias, weights_hbm,
    hidden, row, up, down, stats, source, even, odd, weights, sem,
):
    capacity = marked.shape[0]
    fetch = pltpu.make_async_copy(weights_hbm, weights, sem)
    fetch.start()
    mean, inv_scale, voxel_total = combine_moments(rows[...])
    stats[...] = jnp.concatenate(
        [mean, inv_scale, voxel_total, jnp.zeros((5, 256), f32)], axis=0
    )
    slope = inv_scale * gain[...]
    shift = bias[...] - mean * slope

    def prepare(refs, k, slot):
        values = refs[0][k].astype(f32)
        pre = values * slope + shift
        put_slot(source, slot, jnp.where(values < MARK_LIMIT, pre * sigmoid(pre), 0.0))

    each_slot((marked,), (before,), (after,), prepare)
    put_slot(source, capacity + 2 * EDGE, jnp.zeros((128, 256), f32))
    fetch.wait()

    def finish(b, total, carry):
        sums, count = carry
        on = marked[b].astype(f32) < MARK_LIMIT
        rounded = total.astype(bf16).astype(f32)
        hidden[b] = jnp.where(on, rounded, MARK).astype(bf16)
        kept = jnp.where(on, rounded, 0.0)
        ones = jnp.where(on, 1.0, 0.0)
        return sums + eight_rows(kept), count + eight_rows(ones)

    sums, count = conv(
        index, source, (even, odd), weights, False, capacity, finish,
        (jnp.zeros((8, 256), f32), jnp.zeros((8, 256), f32)),
    )
    for k in range(EDGE):
        up[k] = hidden[counts[0] - EDGE + k]
        down[k] = hidden[k]

    def second_pass(mean):
        def step(b, carry):
            values = hidden[b].astype(f32)
            apart = jnp.where(values < MARK_LIMIT, values - mean, 0.0)
            return carry + eight_rows(apart * apart)

        return column_sum(lax.fori_loop(0, capacity, step, jnp.zeros((8, 256), f32)))

    packed = moments_row(column_sum(sums), column_sum(count)[:, :128], second_pass)
    row[...] = jnp.broadcast_to(packed, row.shape)


def slope_of(pre):
    part = sigmoid(pre)
    return part * (1.0 + pre * (1.0 - part))


def second_sums_kernel(rows, hidden, grad, gain, bias, row, stats):
    capacity = hidden.shape[0]
    mean, inv_scale, voxel_total = combine_moments(rows[...])
    stats[...] = jnp.concatenate(
        [mean, inv_scale, voxel_total, jnp.zeros((5, 256), f32)], axis=0
    )
    gains, biases = gain[...], bias[...]

    def step(b, carry):
        values = hidden[b].astype(f32)
        normed = (values - mean) * inv_scale
        scaled = grad[b] * slope_of(normed * gains + biases) * gains
        on = values < MARK_LIMIT
        scaled = jnp.where(on, scaled, 0.0)
        normed = jnp.where(on, normed, 0.0)
        return carry[0] + eight_rows(scaled), carry[1] + eight_rows(scaled * normed)

    zero = jnp.zeros((8, 256), f32)
    first, second = lax.fori_loop(0, capacity, step, (zero, zero))
    row[...] = jnp.broadcast_to(pairs_row(column_sum(first), column_sum(second)), row.shape)


def second_conv_kernel(
    index, hidden, before, after, stats, gain, bias, marked, weights_hbm,
    out, source, even, odd, weights, sem,
):
    capacity = hidden.shape[0]
    fetch = pltpu.make_async_copy(weights_hbm, weights, sem)
    fetch.start()
    slope = stats[1:2, :] * gain[...]
    shift = bias[...] - stats[0:1, :] * slope

    def prepare(refs, k, slot):
        values = refs[0][k].astype(f32)
        pre = values * slope + shift
        put_slot(source, slot, jnp.where(values < MARK_LIMIT, pre * sigmoid(pre), 0.0))

    each_slot((hidden,), (before,), (after,), prepare)
    put_slot(source, capacity + 2 * EDGE, jnp.zeros((128, 256), f32))
    fetch.wait()

    def finish(b, total, carry):
        inputs = marked[b].astype(f32)
        out[b] = jnp.where(inputs < MARK_LIMIT, inputs + total, 0.0).astype(bf16)
        return carry

    conv(index, source, (even, odd), weights, False, capacity, finish, 0)


def back_conv_kernel(
    index, rows, hidden, hid_before, hid_after, grad, grad_before, grad_after,
    stats_second, gain_second, bias_second, marked, stats_first, gain_first, bias_first, weights_hbm,
    scaled_out, row, source, even, odd, weights, sem,
):
    capacity = hidden.shape[0]
    fetch = pltpu.make_async_copy(weights_hbm, weights, sem)
    fetch.start()
    mean, inv_scale, voxel_total = (stats_second[k : k + 1, :] for k in range(3))
    first, second = combine_pairs(rows[...], voxel_total)
    gains, biases = gain_second[...], bias_second[...]

    def prepare(refs, k, slot):
        values = refs[0][k].astype(f32)
        normed = (values - mean) * inv_scale
        scaled = refs[1][k].astype(f32) * slope_of(normed * gains + biases) * gains
        result = inv_scale * (scaled - first - normed * second)
        put_slot(source, slot, jnp.where(values < MARK_LIMIT, result, 0.0))

    each_slot((hidden, grad), (hid_before, grad_before), (hid_after, grad_after), prepare)
    put_slot(source, capacity + 2 * EDGE, jnp.zeros((128, 256), f32))
    fetch.wait()
    mean_first, inv_first = stats_first[0:1, :], stats_first[1:2, :]
    gains_first, biases_first = gain_first[...], bias_first[...]

    def finish(b, total, carry):
        values = marked[b].astype(f32)
        normed = (values - mean_first) * inv_first
        on = values < MARK_LIMIT
        scaled = total * slope_of(normed * gains_first + biases_first) * gains_first
        scaled = jnp.where(on, scaled, 0.0)
        normed = jnp.where(on, normed, 0.0)
        scaled_out[b] = scaled
        return carry[0] + eight_rows(scaled), carry[1] + eight_rows(scaled * normed)

    zero = jnp.zeros((8, 256), f32)
    sums = conv(index, source, (even, odd), weights, True, capacity, finish, (zero, zero))
    row[...] = jnp.broadcast_to(pairs_row(column_sum(sums[0]), column_sum(sums[1])), row.shape)


def end_kernel(rows, scaled, marked, stats, cotangent, out):
    capacity = marked.shape[0]
    mean, inv_scale, voxel_total = (stats[k : k + 1, :] for k in range(3))
    first, second = combine_pairs(rows[...], voxel_total)

    def step(b, carry):
        values = marked[b].astype(f32)
        normed = (values - mean) * inv_scale
        result = cotangent[b].astype(f32) + inv_scale * (scaled[b] - first - normed * second)
        out[b] = jnp.where(values < MARK_LIMIT, result, 0.0).astype(bf16)
        return carry

    lax.fori_loop(0, capacity, step, 0)


def on_device(
    features, voxel_mask, counts, neighbors, w_first, w_second,
    gain_first, bias_first, gain_second, bias_second, cotangent,
):
    capacity, voxels, channels = features.shape
    devices = counts.shape[0]
    device = lax.axis_index(AXES)
    live = counts[device][None]
    live_before = counts[jnp.maximum(device - 1, 0)]

    owner = neighbors // capacity
    within = neighbors % capacity
    index = jnp.where(
        owner == device,
        within,
        jnp.where(
            owner == device - 1,
            capacity + within - (live_before - EDGE),
            capacity + EDGE + within,
        ),
    )
    index = jnp.where(neighbors < 0, capacity + 2 * EDGE, index).astype(jnp.int32)

    vectors = [v.reshape(1, channels) for v in (gain_first, bias_first, gain_second, bias_second)]
    gain_first, bias_first, gain_second, bias_second = vectors
    w_first = w_first.reshape(27, channels, channels)
    w_second = w_second.reshape(27, channels, channels)

    def shift_up(x):
        return lax.ppermute(x, AXES, [(i, i + 1) for i in range(devices - 1)])

    def shift_down(x):
        return lax.ppermute(x, AXES, [(i + 1, i) for i in range(devices - 1)])

    def exchange(row):
        return lax.all_to_all(row, AXES, 0, 0, tiled=True)

    whole = ((capacity, voxels, channels), bf16)
    whole_wide = ((capacity, voxels, channels), f32)
    edge = ((EDGE, voxels, channels), bf16)
    packed = ((devices, 128), f32)
    vector = ((8, channels), f32)
    slots = capacity + 2 * EDGE + 1

    row, marked, feat_up, feat_down, cot_up, cot_down = call(
        start_kernel, "start", [smem(), vmem(), vmem(), vmem()], [packed, whole, edge, edge, edge, edge]
    )(live, features, voxel_mask, cotangent)
    feat_before, feat_after = shift_up(feat_up), shift_down(feat_down)
    rows_first = exchange(row)

    hidden, row, hid_up, hid_down, stats_first = call(
        first_conv_kernel, "first_conv", [smem(), smem()] + [vmem()] * 6 + [hbm()],
        [whole, packed, edge, edge, vector], conv_scratch(slots),
    )(index, live, rows_first, marked, feat_before, feat_after, gain_first, bias_first, w_first)
    cot_before, cot_after = shift_up(cot_up), shift_down(cot_down)
    hid_before, hid_after = shift_up(hid_up), shift_down(hid_down)
    rows_second = exchange(row)

    grad, grad_up, grad_down = call(
        grad_conv_kernel, "grad_conv", [smem(), smem()] + [vmem()] * 4 + [hbm()],
        [whole_wide, edge, edge], conv_scratch(slots),
    )(index, live, cotangent, marked, cot_before, cot_after, w_second)
    grad_before, grad_after = shift_up(grad_up), shift_down(grad_down)

    row, stats_second = call(second_sums_kernel, "second_sums", [vmem()] * 5, [packed, vector])(
        rows_second, hidden, grad, gain_second, bias_second
    )
    rows_third = exchange(row)

    (output,) = call(
        second_conv_kernel, "second_conv", [smem()] + [vmem()] * 7 + [hbm()], [whole], conv_scratch(slots)
    )(index, hidden, hid_before, hid_after, stats_second, gain_second, bias_second, marked, w_second)

    scaled, row = call(
        back_conv_kernel, "back_conv", [smem()] + [vmem()] * 14 + [hbm()],
        [whole_wide, packed], conv_scratch(slots),
    )(
        index, rows_third, hidden, hid_before, hid_after, grad, grad_before, grad_after,
        stats_second, gain_second, bias_second, marked, stats_first, gain_first, bias_first, w_first,
    )
    rows_fourth = exchange(row)

    (grad_features,) = call(end_kernel, "end", [vmem()] * 5, [whole])(
        rows_fourth, scaled, marked, stats_first, cotangent
    )
    return (output, grad_features)


def solution(mesh):
    split = P(AXES, None, None)
    placed = (split, P(AXES, None), P(), P(AXES, None), P(), P(), P(), P(), P(), P(), split)
    return jax.shard_map(
        on_device, mesh=mesh, in_specs=placed, out_specs=(split, split), check_vma=False
    )
```

profile of v0, /device:TPU:0, one launch (start us, length us, event | category | flops | bytes accessed | tf_op | source)
XLA Modules:
  0.0 132.9 jit_solution(8845034507598239550)
XLA Ops:
  0.6 1.4 %fusion.1 = (s32[1]{0:T(128)}, s32[1]{0:T(128)}) fusion(s32[32]{0:T(128)} %param.13, s32[]{:T(128)S(6)} %select_n.31, s32[]{:T(128)S(6)} %max.3), kind=kLoop, calls=%fused_computation.8 | loop fusion | bytes 24 | tf_op jit(solution)/shard_map/dynamic_slice | solution.py:444
  2.0 4.6 %start.1 = (f32[32,128]{1,0:T(8,128)}, bf16[8,128,256]{2,1,0:T(8,128)(2,1)}, bf16[3,128,256]{2,1,0:T(8,128)(2,1)}, bf16[3,128,256]{2,1,0:T(8,128)(2,1)}, bf16[3,...) custom-call(s32[1]{0:T(128)} %get-tuple-element.38.counts, bf16[8,128,256]{2,1,0:T(8,128)(2,1)} %features.1, ...), custom_call_target="tpu_custom_call" | custom-call | tf_op jit(solution)/shard_map/start/pallas_call | solution.py:481
  6.6 7.3 %all-to-all-start = ((f32[32,1,128]{2,1,0:T(1,128)}), f32[32,1,128]{2,1,0:T(1,128)S(1)}, u32[]{:S(2)}, u32[]{:S(2)}) async-start(f32[32,1,128]{2,1,0:T(1,128)} %bitcast.32), calls=%async_computation | async-start | bytes 32768 | tf_op jit(solution)/shard_map/all_to_all | solution.py:472
  13.9 3.7 %collective-permute-start = (bf16[3,128,256]{2,1,0:T(8,128)(2,1)}, bf16[3,128,256]{2,1,0:T(8,128)(2,1)S(1)}, u32[]{:S(2)}, u32[]{:S(2)}) collective-permute-start(bf16[3,128,256]{2,1,0:T(8,128)(2,1)} %get-tuple-element.22), channel_id=1, source_target_pairs={{0,1},{1,2},{2,3},{3,4},{4,5},{5,6},{6,7},{7,8},{8,9},{9,10},{10,1... | collective-permute-start | bytes 589832 | tf_op jit(solution)/shard_map/ppermute | solution.py:466
  17.6 1.3 collective-permute-start.1
  18.9 4.6 %collective-permute-start.4 = (bf16[3,128,256]{2,1,0:T(8,128)(2,1)}, bf16[3,128,256]{2,1,0:T(8,128)(2,1)S(1)}, u32[]{:S(2)}, u32[]{:S(2)}) collective-permute-start(bf16[3,128,256]{2,1,0:T(8,128)(2,1)} %get-tuple-element.28), channel_id=1, source_target_pairs={{0,1},{1,2},{2,3},{3,4},{4,5},{5,6},{6,7},{7,8},{8,9},{9,10},{10,1... | collective-permute-start | bytes 589832 | tf_op jit(solution)/shard_map/ppermute | solution.py:466
  23.5 1.3 collective-permute-start.5
  25.4 1.3 select_select_fusion.index
  26.7 0.0 all-to-all-done
  26.7 0.0 copy-start.8
  26.7 0.0 collective-permute-done.before
  26.7 0.0 copy-start.4
  26.7 1.7 %collective-permute-done.1.after = bf16[3,128,256]{2,1,0:T(8,128)(2,1)S(1)} collective-permute-done((bf16[3,128,256]{2,1,0:T(8,128)(2,1)}, bf16[3,128,256]{2,1,0:T(8,128)(2,1)S(1)}, u32[]{:S(2)}, u32[]{:S(2)}) %collective-permute-start.1) | collective-permute-done | bytes 196640 | tf_op jit(solution)/shard_map/ppermute | solution.py:469
  28.4 0.0 copy-start.5
  28.4 0.0 copy-done.8
  28.4 0.0 copy-done.4
  28.4 0.7 copy-done.5
  29.1 10.1 %first_conv.1 = (bf16[8,128,256]{2,1,0:T(8,128)(2,1)}, f32[32,128]{1,0:T(8,128)}, bf16[3,128,256]{2,1,0:T(8,128)(2,1)}, bf16[3,128,256]{2,1,0:T(8,128)(2,1)}, f32[8,256]{1,0:T(8,128)}) custom-call(s32[8,27]{1,0:T(8,128)} %select_select_fusion.index, s32[1]{0:T(128)} %get-tuple-element.38.counts, f32[32,128]{1,0:T(8,128)} %bitcast.27, ...), custom_call_target="tpu_custom_call" | custom-call | tf_op jit(solution)/shard_map/first_conv/pallas_call | solution.py:487
  39.3 0.0 copy-start.10
  39.3 3.2 %collective-permute-start.2 = (bf16[3,128,256]{2,1,0:T(8,128)(2,1)}, bf16[3,128,256]{2,1,0:T(8,128)(2,1)S(1)}, u32[]{:S(2)}, u32[]{:S(2)}) collective-permute-start(bf16[3,128,256]{2,1,0:T(8,128)(2,1)} %get-tuple-element.25), channel_id=1, source_target_pairs={{0,1},{1,2},{2,3},{3,4},{4,5},{5,6},{6,7},{7,8},{8,9},{9,10},{10,1... | collective-permute-start | bytes 589832 | tf_op jit(solution)/shard_map/ppermute | solution.py:466
  42.5 1.3 collective-permute-start.3
  43.8 0.0 collective-permute-done.4.before
  43.8 0.0 copy-start.2
  43.8 0.0 collective-permute-done.5.after
  43.8 0.0 copy-start.3
  43.8 0.6 copy-done.2
  44.5 0.1 copy-done.3
  44.6 14.7 %grad_conv.1 = (f32[8,128,256]{2,1,0:T(8,128)}, bf16[3,128,256]{2,1,0:T(8,128)(2,1)}, bf16[3,128,256]{2,1,0:T(8,128)(2,1)}) custom-call(s32[8,27]{1,0:T(8,128)} %select_select_fusion.index, s32[1]{0:T(128)} %get-tuple-element.38.counts, bf16[8,128,256]{2,1,0:T(8,128)(2,1)} %cotangent.5, bf16[8,128,256]{2,1,0:T(8,128)(2,1)} %get-tuple-element.21.marked, ...), custom_call_target="tpu_custom_call" | custom-call | tf_op jit(solution)/shard_map/grad_conv/pallas_call | solution.py:495
  59.2 8.4 %collective-permute-start.6 = (bf16[3,128,256]{2,1,0:T(8,128)(2,1)}, bf16[3,128,256]{2,1,0:T(8,128)(2,1)S(1)}, u32[]{:S(2)}, u32[]{:S(2)}) collective-permute-start(bf16[3,128,256]{2,1,0:T(8,128)(2,1)} %get-tuple-element.33), channel_id=1, source_target_pairs={{0,1},{1,2},{2,3},{3,4},{4,5},{5,6},{6,7},{7,8},{8,9},{9,10},{10,1... | collective-permute-start | bytes 589832 | tf_op jit(solution)/shard_map/ppermute | solution.py:466
  67.7 1.3 collective-permute-start.7
  69.0 0.0 copy-done.10
  69.0 19.4 %all_to_all.44 = f32[32,1,128]{2,1,0:T(1,128)} all-to-all(f32[32,1,128]{2,1,0:T(1,128)S(1)} %bitcast.31), channel_id=1, replica_groups=mesh['region'=4,'sub'=8] {'region','sub'}, dimensions={0} | all-to-all | bytes 32768 | tf_op jit(solution)/shard_map/all_to_all | solution.py:472
  88.4 3.7 %second_sums.1 = (f32[32,128]{1,0:T(8,128)}, f32[8,256]{1,0:T(8,128)}) custom-call(f32[32,128]{1,0:T(8,128)} %bitcast.30, bf16[8,128,256]{2,1,0:T(8,128)(2,1)} %get-tuple-element.24.hidden, f32[8,128,256]{2,1,0:T(8,128)} %get-tuple-element.30.grad, f32[1,256]{1,0:T(1,128)} %bitcast.35, f32[1,256]{1,0:T(1,128)} %bitcast.38), custom_call_target="tpu_custom_call" | custom-call | tf_op jit(solution)/shard_map/second_sums/pallas_call | solution.py:501
  92.1 10.1 %all_to_all.45 = f32[32,1,128]{2,1,0:T(1,128)} all-to-all(f32[32,1,128]{2,1,0:T(1,128)} %bitcast.34), channel_id=1, replica_groups=mesh['region'=4,'sub'=8] {'region','sub'}, dimensions={0} | all-to-all | bytes 32768 | tf_op jit(solution)/shard_map/all_to_all | solution.py:472
  102.2 0.0 collective-permute-done.2.before.hid_before
  102.2 0.0 copy-start
  102.2 0.0 collective-permute-done.3.after.hid_after
  102.2 0.0 copy-start.1
  102.3 0.0 collective-permute-done.6.grad_before
  102.3 0.0 copy-start.6
  102.3 0.0 collective-permute-done.7.grad_after
  102.3 0.0 copy-start.7
  102.3 0.6 copy-done
  102.9 0.1 copy-done.1
  103.0 0.1 copy-done.6
  103.0 0.1 copy-done.7
  103.1 14.8 %back_conv.1 = (f32[8,128,256]{2,1,0:T(8,128)}, f32[32,128]{1,0:T(8,128)}) custom-call(s32[8,27]{1,0:T(8,128)} %select_select_fusion.index, f32[32,128]{1,0:T(8,128)} %bitcast.28, bf16[8,128,256]{2,1,0:T(8,128)(2,1)} %get-tuple-element.24.hidden, bf16[3,128,256]{2,1,0:T(8,128)(2,1)} %copy-done, bf16[3,128,256]{2,1,0:T(8,128)(2,1)} %copy-done.1, ...), custom_call_target="tpu_custom_call" | custom-call | tf_op jit(solution)/shard_map/back_conv/pallas_call | solution.py:510
  117.9 2.6 %all-to-all-start.3 = ((f32[32,1,128]{2,1,0:T(1,128)}), f32[32,1,128]{2,1,0:T(1,128)S(1)}, u32[]{:S(2)}, u32[]{:S(2)}) async-start(f32[32,1,128]{2,1,0:T(1,128)} %bitcast.33), calls=%async_computation.3 | async-start | bytes 32768 | tf_op jit(solution)/shard_map/all_to_all | solution.py:472
  120.5 8.7 %second_conv.1 = bf16[8,128,256]{2,1,0:T(8,128)(2,1)} custom-call(s32[8,27]{1,0:T(8,128)} %select_select_fusion.index, bf16[8,128,256]{2,1,0:T(8,128)(2,1)} %get-tuple-element.24.hidden, bf16[3,128,256]{2,1,0:T(8,128)(2,1)} %copy-done, bf16[3,128,256]{2,1,0:T(8,128)(2,1)} %copy-done.1, f32[8,256]{1,0:T(8,128)} %get-tuple-element.31.stats.stats_second, ...), custom_call_target="tpu_custom_call" | custom-call | tf_op jit(solution)/shard_map/second_conv/pallas_call | solution.py:506
  129.2 0.0 all-to-all-done.3
  129.2 0.0 copy-start.9
  129.3 0.6 copy-done.9
  129.8 3.1 %end.1 = bf16[8,128,256]{2,1,0:T(8,128)(2,1)} custom-call(f32[32,128]{1,0:T(8,128)} %bitcast.29, f32[8,128,256]{2,1,0:T(8,128)} %get-tuple-element.37.scaled, bf16[8,128,256]{2,1,0:T(8,128)(2,1)} %get-tuple-element.21.marked, f32[8,256]{1,0:T(8,128)} %get-tuple-element.35.stats_first.stats, bf16[8,128,256]{2,1,0:T(8,128)(2,1)} %cotangent.5), custom_call_target="tpu_custom_call" | custom-call | tf_op jit(solution)/shard_map/end/pallas_call | solution.py:519
Async XLA Ops:
  6.6 20.1 %all-to-all-start = ((f32[32,1,128]{2,1,0:T(1,128)}), f32[32,1,128]{2,1,0:T(1,128)S(1)}, u32[]{:S(2)}, u32[]{:S(2)}) async-start(f32[32,1,128]{2,1,0:T(1,128)} %bitcast.32), calls=%async_computation | async-start | bytes 32768 | tf_op jit(solution)/shard_map/all_to_all | solution.py:472
  13.9 12.8 %collective-permute-start = (bf16[3,128,256]{2,1,0:T(8,128)(2,1)}, bf16[3,128,256]{2,1,0:T(8,128)(2,1)S(1)}, u32[]{:S(2)}, u32[]{:S(2)}) collective-permute-start(bf16[3,128,256]{2,1,0:T(8,128)(2,1)} %get-tuple-element.22), channel_id=1, source_target_pairs={{0,1},{1,2},{2,3},{3,4},{4,5},{5,6},{6,7},{7,8},{8,9},{9,10},{10,1... | collective-permute-start | bytes 589832 | tf_op jit(solution)/shard_map/ppermute | solution.py:466
  17.6 10.8 %collective-permute-start.1 = (bf16[3,128,256]{2,1,0:T(8,128)(2,1)}, bf16[3,128,256]{2,1,0:T(8,128)(2,1)S(1)}, u32[]{:S(2)}, u32[]{:S(2)}) collective-permute-start(bf16[3,128,256]{2,1,0:T(8,128)(2,1)} %get-tuple-element.23), channel_id=1, source_target_pairs={{1,0},{2,1},{3,2},{4,3},{5,4},{6,5},{7,6},{8,7},{9,8},{10,9},{11,1... | collective-permute-start | bytes 589832 | tf_op jit(solution)/shard_map/ppermute | solution.py:469
  18.9 24.9 %collective-permute-start.4 = (bf16[3,128,256]{2,1,0:T(8,128)(2,1)}, bf16[3,128,256]{2,1,0:T(8,128)(2,1)S(1)}, u32[]{:S(2)}, u32[]{:S(2)}) collective-permute-start(bf16[3,128,256]{2,1,0:T(8,128)(2,1)} %get-tuple-element.28), channel_id=1, source_target_pairs={{0,1},{1,2},{2,3},{3,4},{4,5},{5,6},{6,7},{7,8},{8,9},{9,10},{10,1... | collective-permute-start | bytes 589832 | tf_op jit(solution)/shard_map/ppermute | solution.py:466
  23.5 20.4 %collective-permute-start.5 = (bf16[3,128,256]{2,1,0:T(8,128)(2,1)}, bf16[3,128,256]{2,1,0:T(8,128)(2,1)S(1)}, u32[]{:S(2)}, u32[]{:S(2)}) collective-permute-start(bf16[3,128,256]{2,1,0:T(8,128)(2,1)} %get-tuple-element.29), channel_id=1, source_target_pairs={{1,0},{2,1},{3,2},{4,3},{5,4},{6,5},{7,6},{8,7},{9,8},{10,9},{11,1... | collective-permute-start | bytes 589832 | tf_op jit(solution)/shard_map/ppermute | solution.py:469
  26.7 1.8 %copy-start.8 = (f32[32,1,128]{2,1,0:T(1,128)}, f32[32,1,128]{2,1,0:T(1,128)S(1)}, u32[]{:S(2)}) copy-start(f32[32,1,128]{2,1,0:T(1,128)S(1)} %all-to-all-done) | copy-start | bytes 49156
  26.7 1.8 %copy-start.4 = (bf16[3,128,256]{2,1,0:T(8,128)(2,1)}, bf16[3,128,256]{2,1,0:T(8,128)(2,1)S(1)}, u32[]{:S(2)}) copy-start(bf16[3,128,256]{2,1,0:T(8,128)(2,1)S(1)} %collective-permute-done.before) | copy-start | bytes 589828
  28.4 0.7 copy-start.5
  39.3 29.7 %copy-start.10 = (f32[32,128]{1,0:T(8,128)S(1)}, f32[32,128]{1,0:T(8,128)}, u32[]{:S(2)}) copy-start(f32[32,128]{1,0:T(8,128)} %get-tuple-element.27) | copy-start | bytes 49156
  39.3 62.9 %collective-permute-start.2 = (bf16[3,128,256]{2,1,0:T(8,128)(2,1)}, bf16[3,128,256]{2,1,0:T(8,128)(2,1)S(1)}, u32[]{:S(2)}, u32[]{:S(2)}) collective-permute-start(bf16[3,128,256]{2,1,0:T(8,128)(2,1)} %get-tuple-element.25), channel_id=1, source_target_pairs={{0,1},{1,2},{2,3},{3,4},{4,5},{5,6},{6,7},{7,8},{8,9},{9,10},{10,1... | collective-permute-start | bytes 589832 | tf_op jit(solution)/shard_map/ppermute | solution.py:466
  42.5 59.7 %collective-permute-start.3 = (bf16[3,128,256]{2,1,0:T(8,128)(2,1)}, bf16[3,128,256]{2,1,0:T(8,128)(2,1)S(1)}, u32[]{:S(2)}, u32[]{:S(2)}) collective-permute-start(bf16[3,128,256]{2,1,0:T(8,128)(2,1)} %get-tuple-element.26), channel_id=1, source_target_pairs={{1,0},{2,1},{3,2},{4,3},{5,4},{6,5},{7,6},{8,7},{9,8},{10,9},{11,1... | collective-permute-start | bytes 589832 | tf_op jit(solution)/shard_map/ppermute | solution.py:469
  43.8 0.7 copy-start.2
  43.8 0.7 copy-start.3
  59.2 43.0 %collective-permute-start.6 = (bf16[3,128,256]{2,1,0:T(8,128)(2,1)}, bf16[3,128,256]{2,1,0:T(8,128)(2,1)S(1)}, u32[]{:S(2)}, u32[]{:S(2)}) collective-permute-start(bf16[3,128,256]{2,1,0:T(8,128)(2,1)} %get-tuple-element.33), channel_id=1, source_target_pairs={{0,1},{1,2},{2,3},{3,4},{4,5},{5,6},{6,7},{7,8},{8,9},{9,10},{10,1... | collective-permute-start | bytes 589832 | tf_op jit(solution)/shard_map/ppermute | solution.py:466
  67.7 34.6 %collective-permute-start.7 = (bf16[3,128,256]{2,1,0:T(8,128)(2,1)}, bf16[3,128,256]{2,1,0:T(8,128)(2,1)S(1)}, u32[]{:S(2)}, u32[]{:S(2)}) collective-permute-start(bf16[3,128,256]{2,1,0:T(8,128)(2,1)} %get-tuple-element.34), channel_id=1, source_target_pairs={{1,0},{2,1},{3,2},{4,3},{5,4},{6,5},{7,6},{8,7},{9,8},{10,9},{11,1... | collective-permute-start | bytes 589832 | tf_op jit(solution)/shard_map/ppermute | solution.py:469
  102.2 0.7 copy-start
  102.2 0.7 copy-start.1
  102.3 0.8 copy-start.6
  102.3 0.8 copy-start.7
  117.9 11.3 %all-to-all-start.3 = ((f32[32,1,128]{2,1,0:T(1,128)}), f32[32,1,128]{2,1,0:T(1,128)S(1)}, u32[]{:S(2)}, u32[]{:S(2)}) async-start(f32[32,1,128]{2,1,0:T(1,128)} %bitcast.33), calls=%async_computation.3 | async-start | bytes 32768 | tf_op jit(solution)/shard_map/all_to_all | solution.py:472
  129.2 0.6 copy-start.9
where the time goes:
time: 134 us; the launch traced here: 133 us
  Pallas kernels  59.7 us (45%)
  starting transfers between devices  34.9 us (26%)
  blocking collectives  29.5 us (22%)
  local copies, waits for them, and re-layouts  4.2 us (3%)
  waiting for transfers between devices  1.76 us (1%)
  between operations  1.51 us (1%)
    all_to_all x2, blocking collectives, exchange(): return lax.all_to_all(row, AXES, 0, 0, tiled=True)  29.5 us
    ppermute x4, starting transfers between devices, shift_up(): return lax.ppermute(x, AXES, [(i, i + 1) for i in range(devices - 1)])  19.9 us
    pallas_call x1, Pallas kernels, on_device(): call(back_conv_kernel, 'back_conv', [smem()] + [vmem()] * 14 + [hbm()], [...  14.8 us
    pallas_call x1, Pallas kernels, on_device(): call(grad_conv_kernel, 'grad_conv', [smem(), smem()] + [vmem()] * 4 + [hb...  14.7 us
    pallas_call x1, Pallas kernels, on_device(): call(first_conv_kernel, 'first_conv', [smem(), smem()] + [vmem()] * 6 + [...  10.1 us
    all_to_all x2, starting transfers between devices, exchange(): return lax.all_to_all(row, AXES, 0, 0, tiled=True)  9.87 us
    pallas_call x1, Pallas kernels, on_device(): call(second_conv_kernel, 'second_conv', [smem()] + [vmem()] * 7 + [hbm()]...  8.71 us
    ppermute x4, starting transfers between devices, shift_down(): return lax.ppermute(x, AXES, [(i + 1, i) for i in range(devices - 1)])  5.17 us
  transfers between devices with their start and end apart: 10, of which 1 were waited for; matrix products, arithmetic and copies ran while one was open for 1% of the time, Pallas kernels for 28%

commit v1 on v0

v1 whole, which is shorter than its diff:
```python
import functools

import jax
import jax.numpy as jnp
from jax import lax
from jax.experimental import pallas as pl
from jax.experimental.pallas import tpu as pltpu
from jax.sharding import PartitionSpec as P

GC = 8
EDGE = 3
AXES = ("region", "sub")
eps_norm = 1e-05
MARK = 2.0**100
MARK_LIMIT = 2.0**90
VMEM_LIMIT = 20 * 2**20
COSTS = {"second_sums": 50, "second_conv": 8}
f32 = jnp.float32
bf16 = jnp.bfloat16


def vmem():
    return pl.BlockSpec(memory_space=pltpu.VMEM)


def smem():
    return pl.BlockSpec(memory_space=pltpu.SMEM)


def hbm():
    return pl.BlockSpec(memory_space=pltpu.HBM)


def call(kernel, name, in_specs, outs, scratch=()):
    made = pl.pallas_call(
        kernel,
        name=name,
        in_specs=in_specs,
        out_specs=[vmem() for _ in outs],
        out_shape=[jax.ShapeDtypeStruct(*o) for o in outs],
        scratch_shapes=list(scratch),
        cost_estimate=pl.CostEstimate(flops=int(COSTS[name] * 1.15e9), bytes_accessed=0, transcendentals=0)
        if name in COSTS
        else None,
        compiler_params=pltpu.CompilerParams(vmem_limit_bytes=VMEM_LIMIT),
    )

    def run(*operands):
        return made(
            *(
                pltpu.with_memory_space_constraint(x, pltpu.HBM)
                if spec.memory_space == pltpu.HBM
                else x
                for spec, x in zip(in_specs, operands)
            )
        )

    return run


class Fetched:
    def __init__(self, source, target, sem):
        self.copy = pltpu.make_async_copy(source, target, sem)
        self.copy.start()
        self.target = target

    def ready(self):
        self.copy.wait()
        return self.target


def lane_of(shape):
    return lax.broadcasted_iota(jnp.int32, shape, len(shape) - 1) % GC


def spread_first(x):
    x = jnp.where(lane_of(x.shape) == 0, x, 0.0)
    for s in (1, 2, 4):
        x = x + pltpu.roll(x, s, 1)
    return x


def group_total(x):
    for s in (1, 2, 4):
        x = x + pltpu.roll(x, 128 - s, 1)
    return spread_first(x)


def halves(x):
    return x[:, :128], x[:, 128:]


def pack_row(values):
    lane = lane_of((1, 128))
    row = jnp.zeros((1, 128), f32)
    for k, value in enumerate(values):
        row = jnp.where(lane == k, value, row)
    return row


def unpack_row(rows, k):
    return spread_first(pltpu.roll(rows, 128 - k, 1) if k else rows)


def join(pair):
    return jnp.concatenate(pair, axis=1)


def column_sum(x):
    return jnp.sum(x, axis=0, keepdims=True)


def moments_row(sum_row, count_row, second_pass):
    sums = [group_total(h) for h in halves(sum_row)]
    count = count_row * float(GC)
    safe = jnp.maximum(count, 1.0)
    mean = join([s / safe for s in sums])
    squares = [group_total(h) for h in halves(second_pass(mean))]
    return pack_row([sums[0], sums[1], squares[0], squares[1], count])


def combine_moments(rows):
    count = unpack_row(rows, 4)
    total = column_sum(count)
    safe = jnp.maximum(count, 1.0)
    means, scales = [], []
    for k in (0, 1):
        sums = unpack_row(rows, k)
        mean = column_sum(sums) / total
        apart = sums / safe - mean
        spread = column_sum(unpack_row(rows, 2 + k) + count * (apart * apart)) / total
        means.append(mean)
        scales.append(lax.rsqrt(spread + eps_norm))
    return join(means), join(scales), join([total, total])


def combine_pairs(rows, total):
    summed = column_sum(rows)
    first = join([unpack_row(summed, 0), unpack_row(summed, 1)]) / total
    second = join([unpack_row(summed, 2), unpack_row(summed, 3)]) / total
    return first, second


def pairs_row(first, second):
    return pack_row([group_total(h) for h in (*halves(first), *halves(second))])


def eight_rows(x):
    return jnp.sum(x.reshape(16, 8, x.shape[-1]), axis=0)


def put_slot(source, slot, values):
    tile = values.reshape(16, 8, 256)
    source[1, slot] = tile
    source[0, slot] = pltpu.roll(tile, 1, 1)
    source[2, slot] = pltpu.roll(tile, 7, 1)


def build(index, brick, source, windows):
    z = lax.broadcasted_iota(jnp.int32, (1, 8, 256), 1)
    for slab in range(6):
        dx, x = (0, 3) if slab == 0 else (2, 0) if slab == 5 else (1, slab - 1)
        for l in range(3):
            parts = []
            for dy, y, n in ((0, 3, 1), (1, 0, 4), (2, 0, 1)):
                at = pl.ds(x * 4 + y, n)
                part = source[l, index[brick, dx * 9 + dy * 3 + 1], at]
                if l != 1:
                    edge = source[l, index[brick, dx * 9 + dy * 3 + l], at]
                    part = jnp.where(z == (0 if l == 0 else 7), edge, part)
                parts.append(part)
            columns = jnp.concatenate(parts, axis=0)
            for j in range(3):
                windows[j * 3 + l, slab * 32 : slab * 32 + 32, :] = (
                    columns[j : j + 4].reshape(32, 256).astype(bf16)
                )


def product(pair, weights, backward):
    total = None
    for i in range(3):
        for j in range(3):
            for l in range(3):
                o = i * 9 + j * 3 + l
                taken = jnp.concatenate(
                    [pair[k, j * 3 + l, i * 32 : i * 32 + 128, :] for k in range(2)], axis=0
                )
                if backward:
                    part = lax.dot_general(
                        taken, weights[26 - o], (((1,), (1,)), ((), ())), preferred_element_type=f32
                    )
                else:
                    part = jnp.dot(taken, weights[o], preferred_element_type=f32)
                total = part if total is None else total + part
    return total


def conv(index, source, pairs, weights, backward, capacity, finish, carry):
    def build_pair(first, pair):
        first = jnp.minimum(first, capacity - 2)
        for k in range(2):
            build(index, first + k, source, pair.at[k])

    def finish_pair(first, pair, carry):
        both = product(pair, weights, backward)
        carry = finish(first, both[:128], carry)
        return finish(first + 1, both[128:], carry)

    even, odd = pairs
    build_pair(0, even)

    def four(step, carry):
        first = 4 * step
        build_pair(first + 2, odd)
        carry = finish_pair(first, even, carry)
        build_pair(first + 4, even)
        return finish_pair(first + 2, odd, carry)

    return lax.fori_loop(0, capacity // 4, four, carry)


def conv_scratch(slots):
    return [
        pltpu.VMEM((3, slots, 16, 8, 256), f32),
        pltpu.VMEM((2, 9, 192, 256), bf16),
        pltpu.VMEM((2, 9, 192, 256), bf16),
        pltpu.VMEM((27, 256, 256), bf16),
        pltpu.SemaphoreType.DMA,
    ]


def each_slot(capacity, own, before, after, body):
    def run(refs, start, count):
        def step(k, _):
            body(refs, k, start + k)
            return 0

        lax.fori_loop(0, count, step, 0)

    run(before, capacity, EDGE)
    run(after, capacity + EDGE, EDGE)
    run([x.ready() if isinstance(x, Fetched) else x for x in own], 0, capacity)


def sigmoid(x):
    return 1.0 / (1.0 + jnp.exp(-x))


def mark_kernel(
    counts, features, mask, gain_first, bias_first, gain_second, bias_second,
    marked, up, down, vectors, stage, mask_stage, vector_stage, feature_sem, small_sem,
):
    capacity = marked.shape[0]
    small = [pltpu.make_async_copy(mask, mask_stage, small_sem.at[0])]
    for k, vector in enumerate((gain_first, bias_first, gain_second, bias_second)):
        small.append(pltpu.make_async_copy(vector, vector_stage.at[k], small_sem.at[k + 1]))
    bricks = [
        pltpu.make_async_copy(features.at[b], stage.at[b], feature_sem.at[b]) for b in range(capacity)
    ]
    for copy in small + bricks:
        copy.start()
    live = counts[lax.axis_index(AXES)]
    small[0].wait()
    for b in range(capacity):
        wide = jnp.broadcast_to(mask_stage[b : b + 1, :].astype(f32), (128, 128)).T
        wide = wide * jnp.where(b < live, 1.0, 0.0)
        bricks[b].wait()
        marked[b] = jnp.where(join([wide, wide]) > 0.5, stage[b].astype(f32), MARK).astype(bf16)
    for k in range(EDGE):
        up[k] = marked[live - EDGE + k]
        down[k] = marked[k]
    for copy in small[1:]:
        copy.wait()
    for k in range(4):
        vectors[k : k + 1, :] = vector_stage[k]
    vectors[4:8, :] = jnp.zeros((4, 256), f32)


def first_sums_kernel(counts, marked_hbm, cotangent, row, up, down, stage, sems, marked, marked_sem):
    marked = Fetched(marked_hbm, marked, marked_sem)
    live = counts[lax.axis_index(AXES)]
    copies = []
    for k in range(EDGE):
        copies.append(pltpu.make_async_copy(cotangent.at[live - EDGE + k], stage.at[k], sems.at[k]))
        copies.append(pltpu.make_async_copy(cotangent.at[k], stage.at[EDGE + k], sems.at[EDGE + k]))
    for copy in copies:
        copy.start()
    marked = marked.ready()
    capacity = marked.shape[0]

    total = jnp.zeros((8, 256), f32)
    count = jnp.zeros((8, 128), f32)
    for b in range(capacity):
        values = marked[b].astype(f32)
        on = values < MARK_LIMIT
        total = total + eight_rows(jnp.where(on, values, 0.0))
        count = count + eight_rows(jnp.where(on[:, :128], 1.0, 0.0))

    def second_pass(mean):
        squares = jnp.zeros((8, 256), f32)
        for b in range(capacity):
            values = marked[b].astype(f32)
            apart = jnp.where(values < MARK_LIMIT, values - mean, 0.0)
            squares = squares + eight_rows(apart * apart)
        return column_sum(squares)

    packed = moments_row(column_sum(total), column_sum(count), second_pass)
    row[...] = jnp.broadcast_to(packed, row.shape)
    for copy in copies:
        copy.wait()
    for k in range(EDGE):
        for out, at, brick in ((up, k, live - EDGE + k), (down, EDGE + k, k)):
            on = marked[brick].astype(f32) < MARK_LIMIT
            out[k] = jnp.where(on, stage[at].astype(f32), 0.0).astype(bf16)


def grad_conv_kernel(
    index, counts, cotangent, marked_hbm, hidden, before, after, weights_hbm,
    grad, up, down, source, even, odd, weights, sem, stage, stage_sem, marked, marked_sem, edge_sem,
):
    capacity = marked.shape[0]
    live = counts[lax.axis_index(AXES)]
    edges = [
        pltpu.make_async_copy(hidden.at[pl.ds(live - EDGE, EDGE)], up.at[pl.ds(0, EDGE)], edge_sem.at[0]),
        pltpu.make_async_copy(hidden.at[pl.ds(0, EDGE)], down.at[pl.ds(0, EDGE)], edge_sem.at[1]),
    ]
    for copy in edges:
        copy.start()
    own = Fetched(cotangent, stage, stage_sem)
    marked = Fetched(marked_hbm, marked, marked_sem)
    fetch = pltpu.make_async_copy(weights_hbm, weights, sem)
    fetch.start()
    for k in range(EDGE):
        put_slot(source, capacity + k, before[k].astype(f32))
        put_slot(source, capacity + EDGE + k, after[k].astype(f32))
    put_slot(source, capacity + 2 * EDGE, jnp.zeros((128, 256), f32))
    marked, stage = marked.ready(), own.ready()

    def own_slot(b, _):
        values = stage[b].astype(f32)
        put_slot(source, b, jnp.where(marked[b].astype(f32) < MARK_LIMIT, values, 0.0))
        return 0

    lax.fori_loop(0, capacity, own_slot, 0)
    fetch.wait()

    def finish(b, total, carry):
        grad[b] = total
        return carry

    conv(index, source, (even, odd), weights, True, capacity, finish, 0)
    for copy in edges:
        copy.wait()
    for k in range(EDGE):
        up[EDGE + k] = grad[live - EDGE + k].astype(bf16)
        down[EDGE + k] = grad[k].astype(bf16)


def first_conv_kernel(
    index, rows, marked_hbm, before, after, vectors, weights_hbm,
    hidden, row, stats, source, even, odd, weights, sem, marked_stage, marked_sem,
):
    capacity = hidden.shape[0]
    marked = Fetched(marked_hbm, marked_stage, marked_sem)
    fetch = pltpu.make_async_copy(weights_hbm, weights, sem)
    fetch.start()
    mean, inv_scale, voxel_total = combine_moments(rows[...])
    stats[...] = jnp.concatenate(
        [mean, inv_scale, voxel_total, jnp.zeros((5, 256), f32)], axis=0
    )
    slope = inv_scale * vectors[0:1, :]
    shift = vectors[1:2, :] - mean * slope

    def prepare(refs, k, slot):
        values = refs[0][k].astype(f32)
        pre = values * slope + shift
        put_slot(source, slot, jnp.where(values < MARK_LIMIT, pre * sigmoid(pre), 0.0))

    each_slot(capacity, (marked,), (before,), (after,), prepare)
    put_slot(source, capacity + 2 * EDGE, jnp.zeros((128, 256), f32))
    fetch.wait()

    def finish(b, total, carry):
        sums, count = carry
        on = marked_stage[b].astype(f32) < MARK_LIMIT
        rounded = total.astype(bf16).astype(f32)
        hidden[b] = jnp.where(on, rounded, MARK).astype(bf16)
        kept = jnp.where(on, rounded, 0.0)
        ones = jnp.where(on, 1.0, 0.0)
        return sums + eight_rows(kept), count + eight_rows(ones)

    sums, count = conv(
        index, source, (even, odd), weights, False, capacity, finish,
        (jnp.zeros((8, 256), f32), jnp.zeros((8, 256), f32)),
    )
    def second_pass(mean):
        def step(b, carry):
            values = hidden[b].astype(f32)
            apart = jnp.where(values < MARK_LIMIT, values - mean, 0.0)
            return carry + eight_rows(apart * apart)

        return column_sum(lax.fori_loop(0, capacity, step, jnp.zeros((8, 256), f32)))

    packed = moments_row(column_sum(sums), column_sum(count)[:, :128], second_pass)
    row[...] = jnp.broadcast_to(packed, row.shape)


def slope_of(pre):
    part = sigmoid(pre)
    return part * (1.0 + pre * (1.0 - part))


def second_sums_kernel(rows, hidden_hbm, grad, vectors, row, stats, hidden, hidden_sem):
    capacity = hidden.shape[0]
    fetch = Fetched(hidden_hbm, hidden, hidden_sem)
    mean, inv_scale, voxel_total = combine_moments(rows[...])
    stats[...] = jnp.concatenate(
        [mean, inv_scale, voxel_total, jnp.zeros((5, 256), f32)], axis=0
    )
    gains, biases = vectors[2:3, :], vectors[3:4, :]

    def step(b, carry):
        values = hidden[b].astype(f32)
        normed = (values - mean) * inv_scale
        scaled = grad[b] * slope_of(normed * gains + biases) * gains
        on = values < MARK_LIMIT
        scaled = jnp.where(on, scaled, 0.0)
        normed = jnp.where(on, normed, 0.0)
        return carry[0] + eight_rows(scaled), carry[1] + eight_rows(scaled * normed)

    zero = jnp.zeros((8, 256), f32)
    fetch.ready()
    first, second = lax.fori_loop(0, capacity, step, (zero, zero), unroll=2)
    row[...] = jnp.broadcast_to(pairs_row(column_sum(first), column_sum(second)), row.shape)


def second_conv_kernel(
    index, hidden_hbm, before, after, stats, vectors, marked_hbm, weights_hbm,
    out, source, even, odd, weights, sem, hidden_stage, hidden_sem, marked, marked_sem,
):
    capacity = marked.shape[0]
    hidden = Fetched(hidden_hbm, hidden_stage, hidden_sem)
    marking = Fetched(marked_hbm, marked, marked_sem)
    fetch = pltpu.make_async_copy(weights_hbm, weights, sem)
    fetch.start()
    slope = stats[1:2, :] * vectors[2:3, :]
    shift = vectors[3:4, :] - stats[0:1, :] * slope

    def prepare(refs, k, slot):
        values = refs[0][k].astype(f32)
        pre = values * slope + shift
        put_slot(source, slot, jnp.where(values < MARK_LIMIT, pre * sigmoid(pre), 0.0))

    each_slot(capacity, (hidden,), (before,), (after,), prepare)
    put_slot(source, capacity + 2 * EDGE, jnp.zeros((128, 256), f32))
    marking.ready()
    fetch.wait()

    def finish(b, total, carry):
        inputs = marked[b].astype(f32)
        out[b] = jnp.where(inputs < MARK_LIMIT, inputs + total, 0.0).astype(bf16)
        return carry

    conv(index, source, (even, odd), weights, False, capacity, finish, 0)


def back_conv_kernel(
    index, rows, hidden_hbm, grad, before, after,
    stats_second, marked_hbm, stats_first, vectors, weights_hbm,
    scaled_out, row, source, even, odd, weights, sem, hidden_stage, hidden_sem, marked, marked_sem,
):
    capacity = marked.shape[0]
    hidden = Fetched(hidden_hbm, hidden_stage, hidden_sem)
    marking = Fetched(marked_hbm, marked, marked_sem)
    fetch = pltpu.make_async_copy(weights_hbm, weights, sem)
    fetch.start()
    mean, inv_scale, voxel_total = (stats_second[k : k + 1, :] for k in range(3))
    first, second = combine_pairs(rows[...], voxel_total)
    gains, biases = vectors[2:3, :], vectors[3:4, :]

    def prepare(refs, k, slot):
        values = refs[0][k].astype(f32)
        normed = (values - mean) * inv_scale
        scaled = refs[1][k].astype(f32) * slope_of(normed * gains + biases) * gains
        result = inv_scale * (scaled - first - normed * second)
        put_slot(source, slot, jnp.where(values < MARK_LIMIT, result, 0.0))

    halo = [(x.at[pl.ds(0, EDGE)], x.at[pl.ds(EDGE, EDGE)]) for x in (before, after)]
    each_slot(capacity, (hidden, grad), *halo, prepare)
    put_slot(source, capacity + 2 * EDGE, jnp.zeros((128, 256), f32))
    marking.ready()
    fetch.wait()
    mean_first, inv_first = stats_first[0:1, :], stats_first[1:2, :]
    gains_first, biases_first = vectors[0:1, :], vectors[1:2, :]

    def finish(b, total, carry):
        values = marked[b].astype(f32)
        normed = (values - mean_first) * inv_first
        on = values < MARK_LIMIT
        scaled = total * slope_of(normed * gains_first + biases_first) * gains_first
        scaled = jnp.where(on, scaled, 0.0)
        normed = jnp.where(on, normed, 0.0)
        scaled_out[b] = scaled
        return carry[0] + eight_rows(scaled), carry[1] + eight_rows(scaled * normed)

    zero = jnp.zeros((8, 256), f32)
    sums = conv(index, source, (even, odd), weights, True, capacity, finish, (zero, zero))
    row[...] = jnp.broadcast_to(pairs_row(column_sum(sums[0]), column_sum(sums[1])), row.shape)


def end_kernel(rows, scaled, marked_hbm, stats, cotangent, out, stage, sem, marked, marked_sem):
    capacity = marked.shape[0]
    own = Fetched(cotangent, stage, sem)
    marking = Fetched(marked_hbm, marked, marked_sem)
    mean, inv_scale, voxel_total = (stats[k : k + 1, :] for k in range(3))
    first, second = combine_pairs(rows[...], voxel_total)
    own.ready()
    marking.ready()

    def step(b, carry):
        values = marked[b].astype(f32)
        normed = (values - mean) * inv_scale
        result = stage[b].astype(f32) + inv_scale * (scaled[b] - first - normed * second)
        out[b] = jnp.where(values < MARK_LIMIT, result, 0.0).astype(bf16)
        return carry

    lax.fori_loop(0, capacity, step, 0, unroll=2)


def on_device(
    features, voxel_mask, counts, neighbors, w_first, w_second,
    gain_first, bias_first, gain_second, bias_second, cotangent,
):
    capacity, voxels, channels = features.shape
    devices = counts.shape[0]
    device = lax.axis_index(AXES)
    live_before = counts[jnp.maximum(device - 1, 0)]

    owner = neighbors // capacity
    within = neighbors % capacity
    index = jnp.where(
        owner == device,
        within,
        jnp.where(
            owner == device - 1,
            capacity + within - (live_before - EDGE),
            capacity + EDGE + within,
        ),
    )
    index = jnp.where(neighbors < 0, capacity + 2 * EDGE, index).astype(jnp.int32)

    vectors = [v.reshape(1, channels) for v in (gain_first, bias_first, gain_second, bias_second)]
    gain_first, bias_first, gain_second, bias_second = vectors
    w_first = w_first.reshape(27, channels, channels)
    w_second = w_second.reshape(27, channels, channels)

    def shift_up(x):
        return lax.ppermute(x, AXES, [(i, (i + 1) % devices) for i in range(devices)])

    def shift_down(x):
        return lax.ppermute(x, AXES, [((i + 1) % devices, i) for i in range(devices)])

    def exchange(row):
        return lax.all_to_all(row, AXES, 0, 0, tiled=True)

    whole = ((capacity, voxels, channels), bf16)
    whole_wide = ((capacity, voxels, channels), f32)
    two_edges = ((2 * EDGE, voxels, channels), bf16)
    edge = ((EDGE, voxels, channels), bf16)
    packed = ((devices, 128), f32)
    vector = ((8, channels), f32)
    slots = capacity + 2 * EDGE + 1

    dma = pltpu.SemaphoreType.DMA
    marked, feat_up, feat_down, vectors = call(
        mark_kernel, "mark", [smem()] + [hbm()] * 6, [whole, edge, edge, vector],
        [
            pltpu.VMEM(*whole), pltpu.VMEM((capacity, voxels), jnp.int32),
            pltpu.VMEM((4, 1, channels), f32),
            dma((capacity,)), dma((5,)),
        ],
    )(counts, features, voxel_mask, gain_first, bias_first, gain_second, bias_second)
    feat_before, feat_after = shift_up(feat_up), shift_down(feat_down)
    row, cot_up, cot_down = call(
        first_sums_kernel, "first_sums", [smem(), hbm(), hbm()], [packed, edge, edge],
        [pltpu.VMEM((2 * EDGE, voxels, channels), bf16), dma((2 * EDGE,)), pltpu.VMEM(*whole), dma],
    )(counts, marked, cotangent)
    rows_first = exchange(row)
    cot_before, cot_after = shift_up(cot_up), shift_down(cot_down)

    hidden, row, stats_first = call(
        first_conv_kernel, "first_conv", [smem(), vmem(), hbm(), vmem(), vmem(), vmem(), hbm()],
        [whole, packed, vector], conv_scratch(slots) + [pltpu.VMEM(*whole), dma],
    )(index, rows_first, marked, feat_before, feat_after, vectors, w_first)
    rows_second = exchange(row)

    grad, up, down = call(
        grad_conv_kernel, "grad_conv", [smem(), smem(), hbm(), hbm(), hbm(), vmem(), vmem(), hbm()],
        [whole_wide, two_edges, two_edges],
        conv_scratch(slots) + [pltpu.VMEM(*whole), dma, pltpu.VMEM(*whole), dma, dma((2,))],
    )(index, counts, cotangent, marked, hidden, cot_before, cot_after, w_second)
    before, after = shift_up(up), shift_down(down)

    row, stats_second = call(
        second_sums_kernel, "second_sums", [vmem(), hbm(), vmem(), vmem()], [packed, vector],
        [pltpu.VMEM(*whole), dma],
    )(rows_second, hidden, grad, vectors)
    rows_third = exchange(row)

    (output,) = call(
        second_conv_kernel, "second_conv", [smem(), hbm(), vmem(), vmem(), vmem(), vmem(), hbm(), hbm()],
        [whole],
        conv_scratch(slots) + [pltpu.VMEM(*whole), dma, pltpu.VMEM(*whole), dma],
    )(index, hidden, before, after, stats_second, vectors, marked, w_second)

    scaled, row = call(
        back_conv_kernel, "back_conv", [smem(), vmem(), hbm()] + [vmem()] * 4 + [hbm(), vmem(), vmem(), hbm()],
        [whole_wide, packed],
        conv_scratch(slots) + [pltpu.VMEM(*whole), dma, pltpu.VMEM(*whole), dma],
    )(
        index, rows_third, hidden, grad, before, after,
        stats_second, marked, stats_first, vectors, w_first,
    )
    rows_fourth = exchange(row)

    (grad_features,) = call(
        end_kernel, "end", [vmem(), vmem(), hbm(), vmem(), hbm()], [whole],
        [pltpu.VMEM(*whole), dma, pltpu.VMEM(*whole), dma],
    )(rows_fourth, scaled, marked, stats_first, cotangent)
    return (output, grad_features)


def solution(mesh):
    split = P(AXES, None, None)
    placed = (split, P(AXES, None), P(), P(AXES, None), P(), P(), P(), P(), P(), P(), split)
    return jax.shard_map(
        on_device, mesh=mesh, in_specs=placed, out_specs=(split, split), check_vma=False
    )
```

time: 134 us -> 90.9 us (0.68)
  blocking collectives: 29.5 us -> 13.6 us
  Pallas kernels: 59.7 us -> 44.1 us
  starting transfers between devices: 34.9 us -> 27 us
  waiting for transfers between devices: 1.76 us -> 0.02 us
    all_to_all x2 -> x1, blocking collectives: 29.5 us -> 13.6 us  [exchange(): return lax.all_to_all(row, AXES, 0, 0, tiled=True)]
    pallas_call x7 -> x8, Pallas kernels: 59.7 us -> 44.1 us  [run(): made(*(pltpu.with_memory_space_constraint(x, pltpu.HBM) if spec.memory_sp...]
    ppermute x8 -> x6, starting transfers between devices: 25 us -> 17.2 us  [the longest x3 10.6 us: shift_down(): lax.ppermute(x, AXES, [((i + 1) % devices, i) for i in range(devices)])]
    ppermute x8 -> x6, waiting for transfers between devices: 1.76 us -> 0.02 us  [the longest x3 0.01 us: shift_up(): lax.ppermute(x, AXES, [(i, (i + 1) % devices) for i in range(devices)])]
    unnamed x22 -> x8, local copies, waits for them, and re-layouts: 2.81 us -> 2.3 us
    all_to_all x2 -> x3, starting transfers between devices: 9.87 us -> 9.86 us  [exchange(): return lax.all_to_all(row, AXES, 0, 0, tiled=True)]
  transfers between devices with their start and end apart: 10 -> 9, of which waited for: 1 -> 0; matrix products, arithmetic and copies ran while one was open for 1% -> 2% of each run, Pallas kernels for 28% -> 34%
where the time goes in v1:
time: 90.9 us; the launch traced here: 90.4 us
  Pallas kernels  44.1 us (49%)
  starting transfers between devices  27 us (30%)
  blocking collectives  13.6 us (15%)
  local copies, waits for them, and re-layouts  3.54 us (4%)
  between operations  1.46 us (2%)
    pallas_call x8, Pallas kernels, run(): made(*(pltpu.with_memory_space_constraint(x, pltpu.HBM) if spec.memory_sp...  44.1 us
    all_to_all x1, blocking collectives, exchange(): return lax.all_to_all(row, AXES, 0, 0, tiled=True)  13.6 us
    ppermute x3, starting transfers between devices, shift_down(): lax.ppermute(x, AXES, [((i + 1) % devices, i) for i in range(devices)])  10.6 us
    all_to_all x3, starting transfers between devices, exchange(): return lax.all_to_all(row, AXES, 0, 0, tiled=True)  9.86 us
    ppermute x3, starting transfers between devices, shift_up(): lax.ppermute(x, AXES, [(i, (i + 1) % devices) for i in range(devices)])  6.57 us
    unnamed x8, local copies, waits for them, and re-layouts  2.3 us
  transfers between devices with their start and end apart: 9, of which 0 were waited for; matrix products, arithmetic and copies ran while one was open for 2% of the time, Pallas kernels for 34%

profile of v1, /device:TPU:0, one launch (start us, length us, event | category | flops | bytes accessed | tf_op | source)
XLA Modules:
  0.0 90.4 jit_solution(15592801895396385628)
XLA Ops:
  0.6 0.0 copy-start.3
  0.6 0.0 copy-start.2
  0.7 0.7 copy-done.2
  1.4 2.4 %mark.1 = (bf16[8,128,256]{2,1,0:T(8,128)(2,1)S(1)}, bf16[3,128,256]{2,1,0:T(8,128)(2,1)S(1)}, bf16[3,128,256]{2,1,0:T(8,128)(2,1)S(1)}, f32[8,256]{1,0:T(8,128)S(1)}) custom-call(s32[32]{0:T(128)S(1)} %copy-done.2, bf16[8,128,256]{2,1,0:T(8,128)(2,1)} %features.1, s32[8,128]{1,0:T(8,128)} %mask.1, f32[1,256]{1,0:T(1,128)} %bitcast.32, f32[1,256]{1,0:T(1,128)} %bitcast.33, ...), custom_call_target="tpu_custom_call" | custom-call | tf_op jit(solution)/shard_map/mark/pallas_call | solution.py:49
  3.8 0.0 copy-start
  3.8 0.8 copy-done
  4.6 3.0 %collective-permute-start = (bf16[3,128,256]{2,1,0:T(8,128)(2,1)S(1)}, bf16[3,128,256]{2,1,0:T(8,128)(2,1)S(1)}, u32[]{:S(2)}, u32[]{:S(2)}) collective-permute-start(bf16[3,128,256]{2,1,0:T(8,128)(2,1)S(1)} %get-tuple-element.21), channel_id=1, source_target_pairs={{0,1},{1,2},{2,3},{3,4},{4,5},{5,6},{6,7},{7,8},{8,9},{9,10},{10,1... | collective-permute-start | bytes 589832 | tf_op jit(solution)/shard_map/ppermute | solution.py:558
  7.5 3.4 %collective-permute-start.1 = (bf16[3,128,256]{2,1,0:T(8,128)(2,1)S(1)}, bf16[3,128,256]{2,1,0:T(8,128)(2,1)S(1)}, u32[]{:S(2)}, u32[]{:S(2)}) collective-permute-start(bf16[3,128,256]{2,1,0:T(8,128)(2,1)S(1)} %get-tuple-element.22), channel_id=1, source_target_pairs={{1,0},{2,1},{3,2},{4,3},{5,4},{6,5},{7,6},{8,7},{9,8},{10,9},{11,1... | collective-permute-start | bytes 589832 | tf_op jit(solution)/shard_map/ppermute | solution.py:561
  11.0 3.4 %first_sums.1 = (f32[32,128]{1,0:T(8,128)}, bf16[3,128,256]{2,1,0:T(8,128)(2,1)S(1)}, bf16[3,128,256]{2,1,0:T(8,128)(2,1)S(1)}) custom-call(s32[32]{0:T(128)S(1)} %copy-done.2, bf16[8,128,256]{2,1,0:T(8,128)(2,1)} %copy-done, bf16[8,128,256]{2,1,0:T(8,128)(2,1)} %cotangent.5), custom_call_target="tpu_custom_call" | custom-call | tf_op jit(solution)/shard_map/first_sums/pallas_call | solution.py:49
  14.3 3.0 %all-to-all-start = ((f32[32,1,128]{2,1,0:T(1,128)}), f32[32,1,128]{2,1,0:T(1,128)S(1)}, u32[]{:S(2)}, u32[]{:S(2)}) async-start(f32[32,1,128]{2,1,0:T(1,128)} %bitcast.6), calls=%async_computation | async-start | bytes 32768 | tf_op jit(solution)/shard_map/all_to_all | solution.py:564
  17.3 1.8 %collective-permute-start.2 = (bf16[3,128,256]{2,1,0:T(8,128)(2,1)S(1)}, bf16[3,128,256]{2,1,0:T(8,128)(2,1)S(1)}, u32[]{:S(2)}, u32[]{:S(2)}) collective-permute-start(bf16[3,128,256]{2,1,0:T(8,128)(2,1)S(1)} %get-tuple-element.25), channel_id=1, source_target_pairs={{0,1},{1,2},{2,3},{3,4},{4,5},{5,6},{6,7},{7,8},{8,9},{9,10},{10,1... | collective-permute-start | bytes 589832 | tf_op jit(solution)/shard_map/ppermute | solution.py:558
  19.1 3.6 %collective-permute-start.3 = (bf16[3,128,256]{2,1,0:T(8,128)(2,1)S(1)}, bf16[3,128,256]{2,1,0:T(8,128)(2,1)S(1)}, u32[]{:S(2)}, u32[]{:S(2)}) collective-permute-start(bf16[3,128,256]{2,1,0:T(8,128)(2,1)S(1)} %get-tuple-element.26), channel_id=1, source_target_pairs={{1,0},{2,1},{3,2},{4,3},{5,4},{6,5},{7,6},{8,7},{9,8},{10,9},{11,1... | collective-permute-start | bytes 589832 | tf_op jit(solution)/shard_map/ppermute | solution.py:561
  22.7 1.2 %dynamic_slice.3 = s32[1]{0:T(128)} dynamic-slice(s32[32]{0:T(128)} %counts.5, s32[]{:T(128)S(6)} %max.3), dynamic_slice_sizes={1} | dynamic-slice | bytes 12 | tf_op jit(solution)/shard_map/dynamic_slice | solution.py:537
  24.6 0.7 select_select_fusion.index
  25.3 0.0 all-to-all-done
  25.3 0.0 collective-permute-done.before
  25.3 0.0 collective-permute-done.1.after
  25.3 9.0 %first_conv.1 = (bf16[8,128,256]{2,1,0:T(8,128)(2,1)S(1)}, f32[32,128]{1,0:T(8,128)}, f32[8,256]{1,0:T(8,128)S(1)}) custom-call(s32[8,27]{1,0:T(8,128)S(1)} %select_select_fusion.index, f32[32,128]{1,0:T(8,128)S(1)} %bitcast.23, bf16[8,128,256]{2,1,0:T(8,128)(2,1)} %copy-done, bf16[3,128,256]{2,1,0:T(8,128)(2,1)S(1)} %collective-permute-done.before, ...), custom_call_target="tpu_custom_call" | custom-call | tf_op jit(solution)/shard_map/first_conv/pallas_call | solution.py:49
  34.3 0.0 copy-start.1
  34.3 0.8 copy-done.1
  35.1 2.5 %all-to-all-start.1 = ((f32[32,1,128]{2,1,0:T(1,128)}), f32[32,1,128]{2,1,0:T(1,128)S(1)}, u32[]{:S(2)}, u32[]{:S(2)}) async-start(f32[32,1,128]{2,1,0:T(1,128)} %bitcast.11), calls=%async_computation.1 | async-start | bytes 32768 | tf_op jit(solution)/shard_map/all_to_all | solution.py:564
  37.7 0.0 collective-permute-done.2.before
  37.7 0.0 collective-permute-done.3.after
  37.7 0.0 copy-done.3
  37.7 7.5 %grad_conv.1 = (f32[8,128,256]{2,1,0:T(8,128)S(1)}, bf16[6,128,256]{2,1,0:T(8,128)(2,1)S(1)}, bf16[6,128,256]{2,1,0:T(8,128)(2,1)S(1)}) custom-call(s32[8,27]{1,0:T(8,128)S(1)} %select_select_fusion.index, s32[32]{0:T(128)S(1)} %copy-done.3, bf16[8,128,256]{2,1,0:T(8,128)(2,1)} %cotangent.5, bf16[8,128,256]{2,1,0:T(8,128)(2,1)} %copy-done, ...), custom_call_target="tpu_custom_call" | custom-call | tf_op jit(solution)/shard_map/grad_conv/pallas_call | solution.py:49
  45.2 1.8 %collective-permute-start.4 = (bf16[6,128,256]{2,1,0:T(8,128)(2,1)S(1)}, bf16[6,128,256]{2,1,0:T(8,128)(2,1)S(1)}, u32[]{:S(2)}, u32[]{:S(2)}) collective-permute-start(bf16[6,128,256]{2,1,0:T(8,128)(2,1)S(1)} %get-tuple-element.27), channel_id=1, source_target_pairs={{0,1},{1,2},{2,3},{3,4},{4,5},{5,6},{6,7},{7,8},{8,9},{9,10},{10,1... | collective-permute-start | bytes 1179656 | tf_op jit(solution)/shard_map/ppermute | solution.py:558
  47.0 3.6 %collective-permute-start.5 = (bf16[6,128,256]{2,1,0:T(8,128)(2,1)S(1)}, bf16[6,128,256]{2,1,0:T(8,128)(2,1)S(1)}, u32[]{:S(2)}, u32[]{:S(2)}) collective-permute-start(bf16[6,128,256]{2,1,0:T(8,128)(2,1)S(1)} %get-tuple-element.28), channel_id=1, source_target_pairs={{1,0},{2,1},{3,2},{4,3},{5,4},{6,5},{7,6},{8,7},{9,8},{10,9},{11,1... | collective-permute-start | bytes 1179656 | tf_op jit(solution)/shard_map/ppermute | solution.py:561
  50.6 0.0 all-to-all-done.1
  50.6 2.3 %second_sums.1 = (f32[32,128]{1,0:T(8,128)S(1)}, f32[8,256]{1,0:T(8,128)S(1)}) custom-call(f32[32,128]{1,0:T(8,128)S(1)} %bitcast.26, bf16[8,128,256]{2,1,0:T(8,128)(2,1)} %copy-done.1, f32[8,128,256]{2,1,0:T(8,128)S(1)} %get-tuple-element.30.grad, f32[8,256]{1,0:T(8,128)S(1)} %get-tuple-element.23.vectors), custom_call_target="tpu_custom_call" | custom-call | flops 57500000256 | tf_op jit(solution)/shard_map/second_sums/pallas_call | solution.py:49
  52.9 13.6 %all_to_all.44 = f32[32,1,128]{2,1,0:T(1,128)S(1)} all-to-all(f32[32,1,128]{2,1,0:T(1,128)S(1)} %bitcast.27), channel_id=1, replica_groups=mesh['region'=4,'sub'=8] {'region','sub'}, dimensions={0} | all-to-all | bytes 32768 | tf_op jit(solution)/shard_map/all_to_all | solution.py:564
  66.5 0.0 collective-permute-done.4.before
  66.5 0.0 collective-permute-done.5.after
  66.5 8.9 %back_conv.1 = (f32[8,128,256]{2,1,0:T(8,128)S(1)}, f32[32,128]{1,0:T(8,128)}) custom-call(s32[8,27]{1,0:T(8,128)S(1)} %select_select_fusion.index, f32[32,128]{1,0:T(8,128)S(1)} %bitcast.25, bf16[8,128,256]{2,1,0:T(8,128)(2,1)} %copy-done.1, f32[8,128,256]{2,1,0:T(8,128)S(1)} %get-tuple-element.30.grad, ...), custom_call_target="tpu_custom_call" | custom-call | tf_op jit(solution)/shard_map/back_conv/pallas_call | solution.py:49
  75.4 4.4 %all-to-all-start.3 = ((f32[32,1,128]{2,1,0:T(1,128)}), f32[32,1,128]{2,1,0:T(1,128)S(1)}, u32[]{:S(2)}, u32[]{:S(2)}) async-start(f32[32,1,128]{2,1,0:T(1,128)} %bitcast.17), calls=%async_computation.3 | async-start | bytes 32768 | tf_op jit(solution)/shard_map/all_to_all | solution.py:564
  79.8 8.2 %second_conv.1 = bf16[8,128,256]{2,1,0:T(8,128)(2,1)} custom-call(s32[8,27]{1,0:T(8,128)S(1)} %select_select_fusion.index, bf16[8,128,256]{2,1,0:T(8,128)(2,1)} %copy-done.1, bf16[6,128,256]{2,1,0:T(8,128)(2,1)S(1)} %collective-permute-done.4.before, bf16[6,128,256]{2,1,0:T(8,128)(2,1)S(1)} %collective-permute-done.5.after, ...), custom_call_target="tpu_custom_call" | custom-call | flops 9200000000 | tf_op jit(solution)/shard_map/second_conv/pallas_call | solution.py:49
  88.0 0.0 all-to-all-done.3
  88.0 2.4 %end.1 = bf16[8,128,256]{2,1,0:T(8,128)(2,1)} custom-call(f32[32,128]{1,0:T(8,128)S(1)} %bitcast.24, f32[8,128,256]{2,1,0:T(8,128)S(1)} %get-tuple-element.35.scaled, bf16[8,128,256]{2,1,0:T(8,128)(2,1)} %copy-done, f32[8,256]{1,0:T(8,128)S(1)} %get-tuple-element.33.stats_first.stats, bf16[8,128,256]{2,1,0:T(8,128)(2,1)} %cotangent.5), custom_call_target="tpu_custom_call" | custom-call | tf_op jit(solution)/shard_map/end/pallas_call | solution.py:49
Async XLA Ops:
  0.6 37.1 %copy-start.3 = (s32[32]{0:T(128)S(1)}, s32[32]{0:T(128)}, u32[]{:S(2)}) copy-start(s32[32]{0:T(128)} %counts.5) | copy-start | bytes 388
  0.6 0.7 copy-start.2
  3.8 0.8 copy-start
  4.6 20.7 %collective-permute-start = (bf16[3,128,256]{2,1,0:T(8,128)(2,1)S(1)}, bf16[3,128,256]{2,1,0:T(8,128)(2,1)S(1)}, u32[]{:S(2)}, u32[]{:S(2)}) collective-permute-start(bf16[3,128,256]{2,1,0:T(8,128)(2,1)S(1)} %get-tuple-element.21), channel_id=1, source_target_pairs={{0,1},{1,2},{2,3},{3,4},{4,5},{5,6},{6,7},{7,8},{8,9},{9,10},{10,1... | collective-permute-start | bytes 589832 | tf_op jit(solution)/shard_map/ppermute | solution.py:558
  7.5 17.8 %collective-permute-start.1 = (bf16[3,128,256]{2,1,0:T(8,128)(2,1)S(1)}, bf16[3,128,256]{2,1,0:T(8,128)(2,1)S(1)}, u32[]{:S(2)}, u32[]{:S(2)}) collective-permute-start(bf16[3,128,256]{2,1,0:T(8,128)(2,1)S(1)} %get-tuple-element.22), channel_id=1, source_target_pairs={{1,0},{2,1},{3,2},{4,3},{5,4},{6,5},{7,6},{8,7},{9,8},{10,9},{11,1... | collective-permute-start | bytes 589832 | tf_op jit(solution)/shard_map/ppermute | solution.py:561
  14.3 11.0 %all-to-all-start = ((f32[32,1,128]{2,1,0:T(1,128)}), f32[32,1,128]{2,1,0:T(1,128)S(1)}, u32[]{:S(2)}, u32[]{:S(2)}) async-start(f32[32,1,128]{2,1,0:T(1,128)} %bitcast.6), calls=%async_computation | async-start | bytes 32768 | tf_op jit(solution)/shard_map/all_to_all | solution.py:564
  17.3 20.4 %collective-permute-start.2 = (bf16[3,128,256]{2,1,0:T(8,128)(2,1)S(1)}, bf16[3,128,256]{2,1,0:T(8,128)(2,1)S(1)}, u32[]{:S(2)}, u32[]{:S(2)}) collective-permute-start(bf16[3,128,256]{2,1,0:T(8,128)(2,1)S(1)} %get-tuple-element.25), channel_id=1, source_target_pairs={{0,1},{1,2},{2,3},{3,4},{4,5},{5,6},{6,7},{7,8},{8,9},{9,10},{10,1... | collective-permute-start | bytes 589832 | tf_op jit(solution)/shard_map/ppermute | solution.py:558
  19.1 18.6 %collective-permute-start.3 = (bf16[3,128,256]{2,1,0:T(8,128)(2,1)S(1)}, bf16[3,128,256]{2,1,0:T(8,128)(2,1)S(1)}, u32[]{:S(2)}, u32[]{:S(2)}) collective-permute-start(bf16[3,128,256]{2,1,0:T(8,128)(2,1)S(1)} %get-tuple-element.26), channel_id=1, source_target_pairs={{1,0},{2,1},{3,2},{4,3},{5,4},{6,5},{7,6},{8,7},{9,8},{10,9},{11,1... | collective-permute-start | bytes 589832 | tf_op jit(solution)/shard_map/ppermute | solution.py:561
  34.3 0.8 copy-start.1
  35.1 15.5 %all-to-all-start.1 = ((f32[32,1,128]{2,1,0:T(1,128)}), f32[32,1,128]{2,1,0:T(1,128)S(1)}, u32[]{:S(2)}, u32[]{:S(2)}) async-start(f32[32,1,128]{2,1,0:T(1,128)} %bitcast.11), calls=%async_computation.1 | async-start | bytes 32768 | tf_op jit(solution)/shard_map/all_to_all | solution.py:564
  45.2 21.3 %collective-permute-start.4 = (bf16[6,128,256]{2,1,0:T(8,128)(2,1)S(1)}, bf16[6,128,256]{2,1,0:T(8,128)(2,1)S(1)}, u32[]{:S(2)}, u32[]{:S(2)}) collective-permute-start(bf16[6,128,256]{2,1,0:T(8,128)(2,1)S(1)} %get-tuple-element.27), channel_id=1, source_target_pairs={{0,1},{1,2},{2,3},{3,4},{4,5},{5,6},{6,7},{7,8},{8,9},{9,10},{10,1... | collective-permute-start | bytes 1179656 | tf_op jit(solution)/shard_map/ppermute | solution.py:558
  47.0 19.6 %collective-permute-start.5 = (bf16[6,128,256]{2,1,0:T(8,128)(2,1)S(1)}, bf16[6,128,256]{2,1,0:T(8,128)(2,1)S(1)}, u32[]{:S(2)}, u32[]{:S(2)}) collective-permute-start(bf16[6,128,256]{2,1,0:T(8,128)(2,1)S(1)} %get-tuple-element.28), channel_id=1, source_target_pairs={{1,0},{2,1},{3,2},{4,3},{5,4},{6,5},{7,6},{8,7},{9,8},{10,9},{11,1... | collective-permute-start | bytes 1179656 | tf_op jit(solution)/shard_map/ppermute | solution.py:561
  75.4 12.6 %all-to-all-start.3 = ((f32[32,1,128]{2,1,0:T(1,128)}), f32[32,1,128]{2,1,0:T(1,128)S(1)}, u32[]{:S(2)}, u32[]{:S(2)}) async-start(f32[32,1,128]{2,1,0:T(1,128)} %bitcast.17), calls=%async_computation.3 | async-start | bytes 32768 | tf_op jit(solution)/shard_map/all_to_all | solution.py:564

commit v2 on v1

v2 whole, which is shorter than its diff:
```python
import functools

import jax
import jax.numpy as jnp
from jax import lax
from jax.experimental import pallas as pl
from jax.experimental.pallas import tpu as pltpu
from jax.sharding import PartitionSpec as P

GC = 8
EDGE = 3
AXES = ("region", "sub")
eps_norm = 1e-05
MARK = 2.0**100
MARK_LIMIT = 2.0**90
VMEM_LIMIT = 20 * 2**20
COSTS = {"second_sums": 50, "second_conv": 8, "first_conv": 8}
f32 = jnp.float32
bf16 = jnp.bfloat16


def vmem():
    return pl.BlockSpec(memory_space=pltpu.VMEM)


def hbm():
    return pl.BlockSpec(memory_space=pltpu.HBM)


def call(kernel, name, in_specs, outs, scratch=()):
    made = pl.pallas_call(
        kernel,
        name=name,
        in_specs=in_specs,
        out_specs=[hbm() if len(o) == 3 else vmem() for o in outs],
        out_shape=[pltpu.HBM(*o[:2]) if len(o) == 3 else jax.ShapeDtypeStruct(*o) for o in outs],
        scratch_shapes=list(scratch),
        cost_estimate=pl.CostEstimate(flops=int(COSTS[name] * 1.15e9), bytes_accessed=0, transcendentals=0)
        if name in COSTS
        else None,
        compiler_params=pltpu.CompilerParams(vmem_limit_bytes=VMEM_LIMIT),
    )

    def run(*operands):
        return made(
            *(
                pltpu.with_memory_space_constraint(x, pltpu.HBM)
                if spec.memory_space == pltpu.HBM
                else x
                for spec, x in zip(in_specs, operands)
            )
        )

    return run


class Fetched:
    def __init__(self, source, target, sem):
        self.copy = pltpu.make_async_copy(source, target, sem)
        self.copy.start()
        self.target = target

    def ready(self):
        self.copy.wait()
        return self.target


def lane_of(shape):
    return lax.broadcasted_iota(jnp.int32, shape, len(shape) - 1) % GC


def spread_first(x):
    x = jnp.where(lane_of(x.shape) == 0, x, 0.0)
    for s in (1, 2, 4):
        x = x + pltpu.roll(x, s, 1)
    return x


def group_total(x):
    for s in (1, 2, 4):
        x = x + pltpu.roll(x, 128 - s, 1)
    return spread_first(x)


def halves(x):
    return x[:, :128], x[:, 128:]


def pack_row(values):
    lane = lane_of((1, 128))
    row = jnp.zeros((1, 128), f32)
    for k, value in enumerate(values):
        row = jnp.where(lane == k, value, row)
    return row


def unpack_row(rows, k):
    return spread_first(pltpu.roll(rows, 128 - k, 1) if k else rows)


def join(pair):
    return jnp.concatenate(pair, axis=1)


def column_sum(x):
    return jnp.sum(x, axis=0, keepdims=True)


def no_moments():
    zero = jnp.zeros((8, 256), f32)
    return zero, zero, zero, zero[:, :128]


def add_moments(moments, values, on, first):
    base, sums, squares, count = moments
    here = eight_rows(jnp.where(on[:, :128], 1.0, 0.0))
    number = jnp.maximum(here, 1.0)
    base = jnp.where(first, eight_rows(jnp.where(on, values, 0.0)) / join([number, number]), base)
    apart = jnp.where(on.reshape(16, 8, 256), values.reshape(16, 8, 256) - base, 0.0)
    sums = sums + jnp.sum(apart, axis=0)
    squares = squares + jnp.sum(apart * apart, axis=0)
    return base, sums, squares, count + here


def moments_row(moments):
    base, total, square, count = moments
    safe = jnp.maximum(count, 1.0)
    number = column_sum(count)
    sums, squares = [], []
    for base, total, square in zip(halves(base), halves(total), halves(square)):
        apart = total / safe
        mean = base + apart
        group_sum = group_total(column_sum(count * mean))
        group_mean = group_sum / jnp.maximum(number * float(GC), 1.0)
        about = square - total * apart + count * ((mean - group_mean) * (mean - group_mean))
        sums.append(group_sum)
        squares.append(group_total(column_sum(about)))
    return pack_row([*sums, *squares, number * float(GC)])


def combine_moments(rows):
    count = unpack_row(rows, 4)
    total = column_sum(count)
    safe = jnp.maximum(count, 1.0)
    means, scales = [], []
    for k in (0, 1):
        sums = unpack_row(rows, k)
        mean = column_sum(sums) / total
        apart = sums / safe - mean
        spread = column_sum(unpack_row(rows, 2 + k) + count * (apart * apart)) / total
        means.append(mean)
        scales.append(lax.rsqrt(spread + eps_norm))
    return join(means), join(scales), join([total, total])


def combine_pairs(rows, total):
    summed = column_sum(rows)
    first = join([unpack_row(summed, 0), unpack_row(summed, 1)]) / total
    second = join([unpack_row(summed, 2), unpack_row(summed, 3)]) / total
    return first, second


def pairs_row(first, second):
    return pack_row([group_total(h) for h in (*halves(first), *halves(second))])


def eight_rows(x):
    return jnp.sum(x.reshape(16, 8, x.shape[-1]), axis=0)


def put_slot(source, slot, values):
    tile = values.reshape(16, 8, 256)
    source[1, slot] = tile
    source[0, slot] = pltpu.roll(tile, 1, 1)
    source[2, slot] = pltpu.roll(tile, 7, 1)


def build(index, brick, source, windows):
    z = lax.broadcasted_iota(jnp.int32, (1, 8, 256), 1)
    for slab in range(6):
        dx, x = (0, 3) if slab == 0 else (2, 0) if slab == 5 else (1, slab - 1)
        for l in range(3):
            parts = []
            for dy, y, n in ((0, 3, 1), (1, 0, 4), (2, 0, 1)):
                at = pl.ds(x * 4 + y, n)
                part = source[l, index[brick, dx * 9 + dy * 3 + 1], at]
                if l != 1:
                    edge = source[l, index[brick, dx * 9 + dy * 3 + l], at]
                    part = jnp.where(z == (0 if l == 0 else 7), edge, part)
                parts.append(part)
            columns = jnp.concatenate(parts, axis=0)
            for j in range(3):
                windows[j * 3 + l, slab * 32 : slab * 32 + 32, :] = (
                    columns[j : j + 4].reshape(32, 256).astype(bf16)
                )


def product(pair, weights, backward):
    total = None
    for i in range(3):
        for j in range(3):
            for l in range(3):
                o = i * 9 + j * 3 + l
                taken = jnp.concatenate(
                    [pair[k, j * 3 + l, i * 32 : i * 32 + 128, :] for k in range(2)], axis=0
                )
                if backward:
                    part = lax.dot_general(
                        taken, weights[26 - o], (((1,), (1,)), ((), ())), preferred_element_type=f32
                    )
                else:
                    part = jnp.dot(taken, weights[o], preferred_element_type=f32)
                total = part if total is None else total + part
    return total


def conv(index, source, pair, weights, backward, capacity, finish, carry):
    def two(step, carry):
        first = 2 * step
        for k in range(2):
            build(index, first + k, source, pair.at[k])
        both = product(pair, weights, backward)
        carry = finish(first, both[:128], carry)
        return finish(first + 1, both[128:], carry)

    return lax.fori_loop(0, capacity // 2, two, carry)


def conv_scratch(slots, capacity):
    return [
        pltpu.VMEM((3, slots, 16, 8, 256), f32),
        pltpu.VMEM((2, 9, 192, 256), bf16),
        pltpu.VMEM((27, 256, 256), bf16),
        pltpu.SemaphoreType.DMA,
        pltpu.SMEM((capacity, 27), jnp.int32),
        pltpu.SemaphoreType.DMA,
    ]


def each_slot(capacity, own, before, after, body):
    def run(refs, start, count):
        def step(k, _):
            body(refs, k, start + k)
            return 0

        lax.fori_loop(0, count, step, 0)

    run(before, capacity, EDGE)
    run(after, capacity + EDGE, EDGE)
    run([x.ready() if isinstance(x, Fetched) else x for x in own], 0, capacity)


def sigmoid(x):
    return 1.0 / (1.0 + jnp.exp(-x))


def mark_kernel(
    counts_hbm, features, mask, cotangent, gain_first, bias_first, gain_second, bias_second,
    marked_hbm, marked, feat_up, feat_down, cot_up, cot_down, vectors,
    stage, cot_stage, cot_sem, mask_stage, vector_stage, feature_sem, small_sem, counts, counts_sem, out_sem,
):
    capacity = marked.shape[0]
    counting = Fetched(counts_hbm, counts, counts_sem)
    small = [pltpu.make_async_copy(mask, mask_stage, small_sem.at[0])]
    for k, vector in enumerate((gain_first, bias_first, gain_second, bias_second)):
        small.append(pltpu.make_async_copy(vector, vector_stage.at[k], small_sem.at[k + 1]))

    def arriving(b):
        return pltpu.make_async_copy(features.at[b], stage.at[b], feature_sem.at[b])

    def kept(b):
        return pltpu.make_async_copy(marked.at[b], marked_hbm.at[b], out_sem.at[b])

    for copy in small + [arriving(b) for b in range(capacity)]:
        copy.start()
    live = counting.ready()[lax.axis_index(AXES)]
    edges = []
    for k in range(EDGE):
        for at, brick in ((k, live - EDGE + k), (EDGE + k, k)):
            edges.append(pltpu.make_async_copy(cotangent.at[brick], cot_stage.at[at], cot_sem.at[at]))
    for copy in edges:
        copy.start()
    small[0].wait()
    def step(b, _):
        wide = jnp.broadcast_to(mask_stage[pl.ds(b, 1), :].astype(f32), (128, 128)).T
        wide = wide * jnp.where(b < live, 1.0, 0.0)
        arriving(b).wait()
        marked[b] = jnp.where(join([wide, wide]) > 0.5, stage[b].astype(f32), MARK).astype(bf16)
        kept(b).start()
        return 0

    lax.fori_loop(0, capacity, step, 0, unroll=4)
    for copy in edges:
        copy.wait()
    for k in range(EDGE):
        for feat, cot, at, brick in (
            (feat_up, cot_up, k, live - EDGE + k), (feat_down, cot_down, EDGE + k, k)
        ):
            values = marked[brick]
            feat[k] = values
            on = values.astype(f32) < MARK_LIMIT
            cot[k] = jnp.where(on, cot_stage[at].astype(f32), 0.0).astype(bf16)
    for copy in small[1:] + [kept(b) for b in range(capacity)]:
        copy.wait()
    for k in range(4):
        vectors[k : k + 1, :] = vector_stage[k]
    vectors[4:8, :] = jnp.zeros((4, 256), f32)


def first_sums_kernel(
    counts_hbm, marked, neighbors_hbm, row, index_hbm,
    counts, counts_sem, neighbors, neighbors_sem, index, index_sem,
):
    counting = Fetched(counts_hbm, counts, counts_sem)
    naming = Fetched(neighbors_hbm, neighbors, neighbors_sem)
    device = lax.axis_index(AXES)
    counting.ready()

    capacity = marked.shape[0]
    live_before = counts[jnp.maximum(device - 1, 0)]
    named = naming.ready()[...]
    owner = lax.div(named, capacity)
    within = named - owner * capacity
    slot = jnp.where(
        owner == device,
        within,
        jnp.where(
            owner == device - 1, within + (capacity + EDGE - live_before), within + (capacity + EDGE)
        ),
    )
    index[...] = jnp.where(named < 0, capacity + 2 * EDGE, slot)
    indexed = pltpu.make_async_copy(index, index_hbm, index_sem)
    indexed.start()


    def step(b, moments):
        values = marked[b].astype(f32)
        return add_moments(moments, values, values < MARK_LIMIT, b == 0)

    moments = lax.fori_loop(0, capacity, step, no_moments(), unroll=2)
    row[...] = jnp.broadcast_to(moments_row(moments), row.shape)
    indexed.wait()


def grad_conv_kernel(
    index_hbm, cotangent, marked_hbm, before, after, weights_hbm,
    grad, source, windows, weights, sem, index, index_sem, stage, stage_sem, marked, marked_sem,
):
    capacity = marked.shape[0]
    indexing = Fetched(index_hbm, index, index_sem)
    own = Fetched(cotangent, stage, stage_sem)
    marked = Fetched(marked_hbm, marked, marked_sem)
    fetch = pltpu.make_async_copy(weights_hbm, weights, sem)
    fetch.start()
    for k in range(EDGE):
        put_slot(source, capacity + k, before[k].astype(f32))
        put_slot(source, capacity + EDGE + k, after[k].astype(f32))
    put_slot(source, capacity + 2 * EDGE, jnp.zeros((128, 256), f32))
    marked, stage = marked.ready(), own.ready()

    def own_slot(b, _):
        values = stage[b].astype(f32)
        put_slot(source, b, jnp.where(marked[b].astype(f32) < MARK_LIMIT, values, 0.0))
        return 0

    lax.fori_loop(0, capacity, own_slot, 0)
    indexing.ready()
    fetch.wait()

    def finish(b, total, carry):
        grad[b] = total
        return carry

    conv(index, source, windows, weights, True, capacity, finish, 0)


def first_conv_kernel(
    index_hbm, counts_hbm, rows, marked_hbm, before, after, vectors, weights_hbm,
    hidden_hbm, hidden, row, up, down, stats, source, windows, weights, sem, index, index_sem,
    marked_stage, marked_sem, counts, counts_sem, out_sem,
):
    capacity = hidden.shape[0]
    indexing = Fetched(index_hbm, index, index_sem)
    counting = Fetched(counts_hbm, counts, counts_sem)
    marked = Fetched(marked_hbm, marked_stage, marked_sem)
    fetch = pltpu.make_async_copy(weights_hbm, weights, sem)
    fetch.start()
    mean, inv_scale, voxel_total = combine_moments(rows[...])
    stats[...] = jnp.concatenate(
        [mean, inv_scale, voxel_total, jnp.zeros((5, 256), f32)], axis=0
    )
    slope = inv_scale * vectors[0:1, :]
    shift = vectors[1:2, :] - mean * slope

    def prepare(refs, k, slot):
        values = refs[0][k].astype(f32)
        pre = values * slope + shift
        put_slot(source, slot, jnp.where(values < MARK_LIMIT, pre * sigmoid(pre), 0.0))

    each_slot(capacity, (marked,), (before,), (after,), prepare)
    put_slot(source, capacity + 2 * EDGE, jnp.zeros((128, 256), f32))
    indexing.ready()
    fetch.wait()

    def kept(b):
        return pltpu.make_async_copy(hidden.at[b], hidden_hbm.at[b], out_sem.at[b])

    def finish(b, total, carry):
        on = marked_stage[b].astype(f32) < MARK_LIMIT
        rounded = total.astype(bf16).astype(f32)
        hidden[b] = jnp.where(on, rounded, MARK).astype(bf16)
        kept(b).start()
        return add_moments(carry, rounded, on, b == 0)

    moments = conv(index, source, windows, weights, False, capacity, finish, no_moments())
    live = counting.ready()[lax.axis_index(AXES)]
    for k in range(EDGE):
        up[k] = hidden[live - EDGE + k]
        down[k] = hidden[k]
    row[...] = jnp.broadcast_to(moments_row(moments), row.shape)
    for b in range(capacity):
        kept(b).wait()


def slope_of(pre):
    part = sigmoid(pre)
    return part * (1.0 + pre * (1.0 - part))


def second_sums_kernel(counts_hbm, rows, hidden, grad, vectors, row, stats, up, down, counts, counts_sem):
    counting = Fetched(counts_hbm, counts, counts_sem)
    capacity = hidden.shape[0]
    mean, inv_scale, voxel_total = combine_moments(rows[...])
    stats[...] = jnp.concatenate(
        [mean, inv_scale, voxel_total, jnp.zeros((5, 256), f32)], axis=0
    )
    gains, biases = vectors[2:3, :], vectors[3:4, :]

    def step(b, carry):
        values = hidden[b].astype(f32)
        normed = (values - mean) * inv_scale
        scaled = grad[b] * slope_of(normed * gains + biases) * gains
        on = values < MARK_LIMIT
        scaled = jnp.where(on, scaled, 0.0)
        normed = jnp.where(on, normed, 0.0)
        return carry[0] + eight_rows(scaled), carry[1] + eight_rows(scaled * normed)

    zero = jnp.zeros((8, 256), f32)
    first, second = lax.fori_loop(0, capacity, step, (zero, zero), unroll=2)
    live = counting.ready()[lax.axis_index(AXES)]
    for k in range(EDGE):
        up[k] = grad[live - EDGE + k].astype(bf16)
        down[k] = grad[k].astype(bf16)
    row[...] = jnp.broadcast_to(pairs_row(column_sum(first), column_sum(second)), row.shape)


def second_conv_kernel(
    index_hbm, hidden_hbm, before, after, stats, vectors, marked_hbm, weights_hbm,
    out, done, source, windows, weights, sem, index, index_sem, hidden_stage, hidden_sem, marked, marked_sem,
):
    capacity = marked.shape[0]
    indexing = Fetched(index_hbm, index, index_sem)
    hidden = Fetched(hidden_hbm, hidden_stage, hidden_sem)
    marking = Fetched(marked_hbm, marked, marked_sem)
    fetch = pltpu.make_async_copy(weights_hbm, weights, sem)
    fetch.start()
    done[...] = jnp.zeros(done.shape, f32)
    slope = stats[1:2, :] * vectors[2:3, :]
    shift = vectors[3:4, :] - stats[0:1, :] * slope

    def prepare(refs, k, slot):
        values = refs[0][k].astype(f32)
        pre = values * slope + shift
        put_slot(source, slot, jnp.where(values < MARK_LIMIT, pre * sigmoid(pre), 0.0))

    each_slot(capacity, (hidden,), (before,), (after,), prepare)
    put_slot(source, capacity + 2 * EDGE, jnp.zeros((128, 256), f32))
    marking.ready()
    indexing.ready()
    fetch.wait()

    def finish(b, total, carry):
        inputs = marked[b].astype(f32)
        out[b] = jnp.where(inputs < MARK_LIMIT, inputs + total, 0.0).astype(bf16)
        return carry

    conv(index, source, windows, weights, False, capacity, finish, 0)


def back_conv_kernel(
    index_hbm, rows, hidden_hbm, hid_before, hid_after, grad, grad_before, grad_after,
    stats_second, marked_hbm, stats_first, vectors, cotangent, weights_hbm, after_conv,
    partial, normed_out, row, source, windows, weights, sem, index, index_sem, hidden_stage, hidden_sem, marked, marked_sem,
    stage, stage_sem,
):
    capacity = marked.shape[0]
    indexing = Fetched(index_hbm, index, index_sem)
    hidden = Fetched(hidden_hbm, hidden_stage, hidden_sem)
    marking = Fetched(marked_hbm, marked, marked_sem)
    fetch = pltpu.make_async_copy(weights_hbm, weights, sem)
    fetch.start()
    own = Fetched(cotangent, stage, stage_sem)
    mean, inv_scale, voxel_total = (stats_second[k : k + 1, :] for k in range(3))
    first, second = combine_pairs(rows[...], voxel_total)
    gains, biases = vectors[2:3, :], vectors[3:4, :]

    def prepare(refs, k, slot):
        values = refs[0][k].astype(f32)
        normed = (values - mean) * inv_scale
        scaled = refs[1][k].astype(f32) * slope_of(normed * gains + biases) * gains
        result = inv_scale * (scaled - first - normed * second)
        put_slot(source, slot, jnp.where(values < MARK_LIMIT, result, 0.0))

    each_slot(capacity, (hidden, grad), (hid_before, grad_before), (hid_after, grad_after), prepare)
    put_slot(source, capacity + 2 * EDGE, jnp.zeros((128, 256), f32))
    marking.ready()
    indexing.ready()
    fetch.wait()
    own.ready()
    mean_first, inv_first = stats_first[0:1, :], stats_first[1:2, :]
    gains_first, biases_first = vectors[0:1, :], vectors[1:2, :]

    def finish(b, total, carry):
        values = marked[b].astype(f32)
        normed = (values - mean_first) * inv_first
        on = values < MARK_LIMIT
        scaled = total * slope_of(normed * gains_first + biases_first) * gains_first
        scaled = jnp.where(on, scaled, 0.0)
        normed = jnp.where(on, normed, 0.0)
        whole = stage[b].astype(f32) + inv_first * scaled
        partial[b] = jnp.where(on, whole, MARK)
        normed_out[b] = normed
        return carry[0] + eight_rows(scaled), carry[1] + eight_rows(scaled * normed)

    zero = jnp.zeros((8, 256), f32)
    sums = conv(index, source, windows, weights, True, capacity, finish, (zero, zero))
    row[...] = jnp.broadcast_to(pairs_row(column_sum(sums[0]), column_sum(sums[1])), row.shape)


def end_kernel(rows, partial, normed, stats, out_hbm, out, sem):
    capacity = partial.shape[0]
    inv_scale, voxel_total = stats[1:2, :], stats[2:3, :]
    first, second = combine_pairs(rows[...], voxel_total)
    first, second = inv_scale * first, inv_scale * second

    def done(b):
        return pltpu.make_async_copy(out.at[b], out_hbm.at[b], sem.at[b])

    def step(b, carry):
        whole = partial[b]
        out[b] = jnp.where(whole < MARK_LIMIT, whole - first - normed[b] * second, 0.0).astype(bf16)
        done(b).start()
        return carry

    lax.fori_loop(0, capacity, step, 0)
    for b in range(capacity):
        done(b).wait()


def on_device(
    features, voxel_mask, counts, neighbors, w_first, w_second,
    gain_first, bias_first, gain_second, bias_second, cotangent,
):
    capacity, voxels, channels = features.shape
    devices = counts.shape[0]
    vectors = [v.reshape(1, channels) for v in (gain_first, bias_first, gain_second, bias_second)]
    gain_first, bias_first, gain_second, bias_second = vectors
    w_first = w_first.reshape(27, channels, channels)
    w_second = w_second.reshape(27, channels, channels)

    def shift_up(x):
        return lax.ppermute(x, AXES, [(i, (i + 1) % devices) for i in range(devices)])

    def shift_down(x):
        return lax.ppermute(x, AXES, [((i + 1) % devices, i) for i in range(devices)])

    def exchange(row):
        return lax.all_to_all(row, AXES, 0, 0, tiled=True)

    whole = ((capacity, voxels, channels), bf16)
    whole_wide = ((capacity, voxels, channels), f32)
    table = (neighbors.shape, jnp.int32)
    edge = ((EDGE, voxels, channels), bf16)
    packed = ((devices, 128), f32)
    vector = ((8, channels), f32)
    slots = capacity + 2 * EDGE + 1

    dma = pltpu.SemaphoreType.DMA
    marked, marked_near, feat_up, feat_down, cot_up, cot_down, vectors = call(
        mark_kernel, "mark", [hbm()] * 8, [(*whole, "hbm"), whole, edge, edge, edge, edge, vector],
        [
            pltpu.VMEM(*whole), pltpu.VMEM((2 * EDGE, voxels, channels), bf16), dma((2 * EDGE,)),
            pltpu.VMEM((capacity, voxels), jnp.int32),
            pltpu.VMEM((4, 1, channels), f32),
            dma((capacity,)), dma((5,)), pltpu.SMEM(counts.shape, jnp.int32), dma, dma((capacity,)),
        ],
    )(counts, features, voxel_mask, cotangent, gain_first, bias_first, gain_second, bias_second)
    cot_before, cot_after = shift_up(cot_up), shift_down(cot_down)
    feat_before, feat_after = shift_up(feat_up), shift_down(feat_down)
    row, index = call(
        first_sums_kernel, "first_sums", [hbm(), vmem(), hbm()], [packed, (*table, "hbm")],
        [
            pltpu.SMEM(counts.shape, jnp.int32), dma, pltpu.VMEM(*table), dma, pltpu.VMEM(*table), dma,
        ],
    )(counts, marked_near, neighbors)
    rows_first = exchange(row)

    (grad,) = call(
        grad_conv_kernel, "grad_conv", [hbm(), hbm(), hbm(), vmem(), vmem(), hbm()],
        [whole_wide], conv_scratch(slots, capacity) + [pltpu.VMEM(*whole), dma] * 2,
    )(index, cotangent, marked, cot_before, cot_after, w_second)

    hidden, hidden_near, row, hid_up, hid_down, stats_first = call(
        first_conv_kernel, "first_conv",
        [hbm(), hbm(), vmem(), hbm(), vmem(), vmem(), vmem(), hbm()],
        [(*whole, "hbm"), whole, packed, edge, edge, vector],
        conv_scratch(slots, capacity)
        + [
            pltpu.VMEM(*whole), dma, pltpu.SMEM(counts.shape, jnp.int32), dma, dma((capacity,)),
        ],
    )(index, counts, rows_first, marked, feat_before, feat_after, vectors, w_first)
    rows_second = exchange(row)
    hid_before, hid_after = shift_up(hid_up), shift_down(hid_down)

    row, stats_second, grad_up, grad_down = call(
        second_sums_kernel, "second_sums", [hbm()] + [vmem()] * 4, [packed, vector, edge, edge],
        [pltpu.SMEM(counts.shape, jnp.int32), dma],
    )(
        counts, rows_second, hidden_near, grad, vectors
    )
    grad_before, grad_after = shift_up(grad_up), shift_down(grad_down)
    rows_third = exchange(row)

    output, done = call(
        second_conv_kernel, "second_conv", [hbm(), hbm(), vmem(), vmem(), vmem(), vmem(), hbm(), hbm()],
        [whole, ((8, 128), f32)],
        conv_scratch(slots, capacity) + [pltpu.VMEM(*whole), dma, pltpu.VMEM(*whole), dma],
    )(index, hidden, hid_before, hid_after, stats_second, vectors, marked, w_second)

    partial, normed, row = call(
        back_conv_kernel, "back_conv", [hbm(), vmem(), hbm()] + [vmem()] * 6 + [hbm(), vmem(), vmem(), hbm(), hbm(), vmem()],
        [whole_wide, whole_wide, packed],
        conv_scratch(slots, capacity) + [pltpu.VMEM(*whole), dma] * 3,
    )(
        index, rows_third, hidden, hid_before, hid_after, grad, grad_before, grad_after,
        stats_second, marked, stats_first, vectors, cotangent, w_first, done,
    )
    rows_fourth = exchange(row)

    (grad_features,) = call(
        end_kernel, "end", [vmem()] * 4, [(*whole, "hbm")], [pltpu.VMEM(*whole), dma((capacity,))]
    )(rows_fourth, partial, normed, stats_first)
    return (output, grad_features)


def solution(mesh):
    split = P(AXES, None, None)
    placed = (split, P(AXES, None), P(), P(AXES, None), P(), P(), P(), P(), P(), P(), split)
    return jax.shard_map(
        on_device, mesh=mesh, in_specs=placed, out_specs=(split, split), check_vma=False
    )
```

time: 90.9 us -> 84.2 us (0.926)
  Pallas kernels: 44.1 us -> 39.4 us
  starting transfers between devices: 27 us -> 30.7 us
  local copies, waits for them, and re-layouts: 3.54 us -> 0 us
  blocking collectives: 13.6 us -> 11 us
  waiting for transfers between devices: 0.02 us -> 2.04 us
    pallas_call x8, Pallas kernels: 44.1 us -> 39.4 us  [run(): made(*(pltpu.with_memory_space_constraint(x, pltpu.HBM) if spec.memory_sp...]
    ppermute x3 -> x4, starting transfers between devices: 10.6 us -> 14.3 us  [shift_down(): lax.ppermute(x, AXES, [((i + 1) % devices, i) for i in range(devices)])]
    all_to_all x1, blocking collectives: 13.6 us -> 11 us  [exchange(): return lax.all_to_all(row, AXES, 0, 0, tiled=True)]
    unnamed x8 -> x0, local copies, waits for them, and re-layouts: 2.3 us -> none
    all_to_all x3, waiting for transfers between devices: 0.01 us -> 2.02 us  [exchange(): return lax.all_to_all(row, AXES, 0, 0, tiled=True)]
    all_to_all x3, starting transfers between devices: 9.86 us -> 7.98 us  [exchange(): return lax.all_to_all(row, AXES, 0, 0, tiled=True)]
    ppermute x3 -> x4, starting transfers between devices: 6.57 us -> 8.37 us  [shift_up(): lax.ppermute(x, AXES, [(i, (i + 1) % devices) for i in range(devices)])]
    dynamic_slice x1 -> x0, local copies, waits for them, and re-layouts: 1.24 us -> none  [on_device(): live_before = counts[jnp.maximum(device - 1, 0)]]
  transfers between devices with their start and end apart: 9 -> 11, of which waited for: 0 -> 1; matrix products, arithmetic and copies ran while one was open for 2% -> 0% of each run, Pallas kernels for 34% -> 33%
where the time goes in v2:
time: 84.2 us; the launch traced here: 83.9 us
  Pallas kernels  39.4 us (47%)
  starting transfers between devices  30.7 us (36%)
  blocking collectives  11 us (13%)
  waiting for transfers between devices  2.04 us (2%)
    pallas_call x8, Pallas kernels, run(): made(*(pltpu.with_memory_space_constraint(x, pltpu.HBM) if spec.memory_sp...  39.4 us
    ppermute x4, starting transfers between devices, shift_down(): lax.ppermute(x, AXES, [((i + 1) % devices, i) for i in range(devices)])  14.3 us
    all_to_all x1, blocking collectives, exchange(): return lax.all_to_all(row, AXES, 0, 0, tiled=True)  11 us
    ppermute x4, starting transfers between devices, shift_up(): lax.ppermute(x, AXES, [(i, (i + 1) % devices) for i in range(devices)])  8.37 us
    all_to_all x3, starting transfers between devices, exchange(): return lax.all_to_all(row, AXES, 0, 0, tiled=True)  7.98 us
    all_to_all x3, waiting for transfers between devices, exchange(): return lax.all_to_all(row, AXES, 0, 0, tiled=True)  2.02 us
  transfers between devices with their start and end apart: 11, of which 1 were waited for; matrix products, arithmetic and copies ran while one was open for 0% of the time, Pallas kernels for 33%

profile of v2, /device:TPU:0, one launch (start us, length us, event | category | flops | bytes accessed | tf_op | source)
XLA Modules:
  0.0 83.9 jit_solution(14712311920388715849)
XLA Ops:
  0.6 2.6 %mark.1 = (bf16[8,128,256]{2,1,0:T(8,128)(2,1)}, bf16[8,128,256]{2,1,0:T(8,128)(2,1)S(1)}, bf16[3,128,256]{2,1,0:T(8,128)(2,1)S(1)}, bf16[3,128,256]{2,1,0:T(8,1...) custom-call(s32[32]{0:T(128)} %counts_hbm.7, ...), custom_call_target="tpu_custom_call" | custom-call | tf_op jit(solution)/shard_map/mark/pallas_call | solution.py:45
  3.2 3.0 %collective-permute-start = (bf16[3,128,256]{2,1,0:T(8,128)(2,1)S(1)}, bf16[3,128,256]{2,1,0:T(8,128)(2,1)S(1)}, u32[]{:S(2)}, u32[]{:S(2)}) collective-permute-start(bf16[3,128,256]{2,1,0:T(8,128)(2,1)S(1)} %get-tuple-element.30), channel_id=1, source_target_pairs={{0,1},{1,2},{2,3},{3,4},{4,5},{5,6},{6,7},{7,8},{8,9},{9,10},{10,1... | collective-permute-start | bytes 589832 | tf_op jit(solution)/shard_map/ppermute | solution.py:572
  6.2 3.5 %collective-permute-start.1 = (bf16[3,128,256]{2,1,0:T(8,128)(2,1)S(1)}, bf16[3,128,256]{2,1,0:T(8,128)(2,1)S(1)}, u32[]{:S(2)}, u32[]{:S(2)}) collective-permute-start(bf16[3,128,256]{2,1,0:T(8,128)(2,1)S(1)} %get-tuple-element.31), channel_id=1, source_target_pairs={{1,0},{2,1},{3,2},{4,3},{5,4},{6,5},{7,6},{8,7},{9,8},{10,9},{11,1... | collective-permute-start | bytes 589832 | tf_op jit(solution)/shard_map/ppermute | solution.py:575
  9.7 2.6 %first_sums.1 = (f32[32,128]{1,0:T(8,128)}, s32[8,27]{1,0:T(8,128)}) custom-call(s32[32]{0:T(128)} %counts_hbm.7, bf16[8,128,256]{2,1,0:T(8,128)(2,1)S(1)} %get-tuple-element.26.marked, s32[8,27]{1,0:T(8,128)} %neighbors_hbm.1), custom_call_target="tpu_custom_call" | custom-call | tf_op jit(solution)/shard_map/first_sums/pallas_call | solution.py:45
  12.3 2.9 %all-to-all-start = ((f32[32,1,128]{2,1,0:T(1,128)}), f32[32,1,128]{2,1,0:T(1,128)S(1)}, u32[]{:S(2)}, u32[]{:S(2)}) async-start(f32[32,1,128]{2,1,0:T(1,128)} %bitcast.5), calls=%async_computation | async-start | bytes 32768 | tf_op jit(solution)/shard_map/all_to_all | solution.py:578
  15.2 1.8 %collective-permute-start.4 = (bf16[3,128,256]{2,1,0:T(8,128)(2,1)S(1)}, bf16[3,128,256]{2,1,0:T(8,128)(2,1)S(1)}, u32[]{:S(2)}, u32[]{:S(2)}) collective-permute-start(bf16[3,128,256]{2,1,0:T(8,128)(2,1)S(1)} %get-tuple-element.38), channel_id=1, source_target_pairs={{0,1},{1,2},{2,3},{3,4},{4,5},{5,6},{6,7},{7,8},{8,9},{9,10},{10,1... | collective-permute-start | bytes 589832 | tf_op jit(solution)/shard_map/ppermute | solution.py:572
  17.0 3.6 %collective-permute-start.5 = (bf16[3,128,256]{2,1,0:T(8,128)(2,1)S(1)}, bf16[3,128,256]{2,1,0:T(8,128)(2,1)S(1)}, u32[]{:S(2)}, u32[]{:S(2)}) collective-permute-start(bf16[3,128,256]{2,1,0:T(8,128)(2,1)S(1)} %get-tuple-element.39), channel_id=1, source_target_pairs={{1,0},{2,1},{3,2},{4,3},{5,4},{6,5},{7,6},{8,7},{9,8},{10,9},{11,1... | collective-permute-start | bytes 589832 | tf_op jit(solution)/shard_map/ppermute | solution.py:575
  20.6 2.0 %all-to-all-done = f32[32,1,128]{2,1,0:T(1,128)S(1)} async-done(((f32[32,1,128]{2,1,0:T(1,128)}), f32[32,1,128]{2,1,0:T(1,128)S(1)}, u32[]{:S(2)}, u32[]{:S(2)}) %all-to-all-start) | async-done | bytes 16416 | tf_op jit(solution)/shard_map/all_to_all | solution.py:578
  22.6 0.0 collective-permute-done.before
  22.6 0.0 collective-permute-done.1.after
  22.6 8.4 %first_conv.1 = (bf16[8,128,256]{2,1,0:T(8,128)(2,1)}, bf16[8,128,256]{2,1,0:T(8,128)(2,1)S(1)}, f32[32,128]{1,0:T(8,128)}, bf16[3,128,256]{2,1,0:T(8,128)(2,1)S...) custom-call(s32[8,27]{1,0:T(8,128)} %get-tuple-element.27.index_hbm, s32[32]{0:T(128)} %counts_hbm.7, ...), custom_call_target="tpu_custom_call" | custom-call | flops 9200000000 | tf_op jit(solution)/shard_map/first_conv/pallas_call | solution.py:45
  31.0 2.6 %all-to-all-start.1 = ((f32[32,1,128]{2,1,0:T(1,128)}), f32[32,1,128]{2,1,0:T(1,128)S(1)}, u32[]{:S(2)}, u32[]{:S(2)}) async-start(f32[32,1,128]{2,1,0:T(1,128)} %bitcast.9), calls=%async_computation.1 | async-start | bytes 32768 | tf_op jit(solution)/shard_map/all_to_all | solution.py:578
  33.6 1.7 %collective-permute-start.2 = (bf16[3,128,256]{2,1,0:T(8,128)(2,1)S(1)}, bf16[3,128,256]{2,1,0:T(8,128)(2,1)S(1)}, u32[]{:S(2)}, u32[]{:S(2)}) collective-permute-start(bf16[3,128,256]{2,1,0:T(8,128)(2,1)S(1)} %get-tuple-element.34), channel_id=1, source_target_pairs={{0,1},{1,2},{2,3},{3,4},{4,5},{5,6},{6,7},{7,8},{8,9},{9,10},{10,1... | collective-permute-start | bytes 589832 | tf_op jit(solution)/shard_map/ppermute | solution.py:572
  35.3 3.7 %collective-permute-start.3 = (bf16[3,128,256]{2,1,0:T(8,128)(2,1)S(1)}, bf16[3,128,256]{2,1,0:T(8,128)(2,1)S(1)}, u32[]{:S(2)}, u32[]{:S(2)}) collective-permute-start(bf16[3,128,256]{2,1,0:T(8,128)(2,1)S(1)} %get-tuple-element.35), channel_id=1, source_target_pairs={{1,0},{2,1},{3,2},{4,3},{5,4},{6,5},{7,6},{8,7},{9,8},{10,9},{11,1... | collective-permute-start | bytes 589832 | tf_op jit(solution)/shard_map/ppermute | solution.py:575
  39.0 0.0 collective-permute-done.4.before
  39.0 0.0 collective-permute-done.5.after
  39.0 6.8 %grad_conv.1.grad = f32[8,128,256]{2,1,0:T(8,128)S(1)} custom-call(s32[8,27]{1,0:T(8,128)} %get-tuple-element.27.index_hbm, bf16[8,128,256]{2,1,0:T(8,128)(2,1)} %cotangent.5, bf16[8,128,256]{2,1,0:T(8,128)(2,1)} %get-tuple-element.29.marked_hbm, bf16[3,128,256]{2,1,0:T(8,128)(2,1)S(1)} %collective-permute-done.4.before, ...), custom_call_target="tpu_custom_call" | custom-call | tf_op jit(solution)/shard_map/grad_conv/pallas_call | solution.py:45
  45.8 0.0 all-to-all-done.1
  45.9 2.3 %second_sums.1 = (f32[32,128]{1,0:T(8,128)}, f32[8,256]{1,0:T(8,128)S(1)}, bf16[3,128,256]{2,1,0:T(8,128)(2,1)S(1)}, bf16[3,128,256]{2,1,0:T(8,128)(2,1)S(1)}) custom-call(s32[32]{0:T(128)} %counts_hbm.7, f32[32,128]{1,0:T(8,128)S(1)} %bitcast.25, bf16[8,128,256]{2,1,0:T(8,128)(2,1)S(1)} %get-tuple-element.37.hidden, f32[8,128,256]{2,1,0:T(8,128)S(1)} %grad_conv.1.grad, ...), custom_call_target="tpu_custom_call" | custom-call | flops 57500000256 | tf_op jit(solution)/shard_map/second_sums/pallas_call | solution.py:45
  48.1 2.5 %all-to-all-start.2 = ((f32[32,1,128]{2,1,0:T(1,128)}), f32[32,1,128]{2,1,0:T(1,128)S(1)}, u32[]{:S(2)}, u32[]{:S(2)}) async-start(f32[32,1,128]{2,1,0:T(1,128)} %bitcast.13), calls=%async_computation.2 | async-start | bytes 32768 | tf_op jit(solution)/shard_map/all_to_all | solution.py:578
  50.7 1.8 %collective-permute-start.6 = (bf16[3,128,256]{2,1,0:T(8,128)(2,1)S(1)}, bf16[3,128,256]{2,1,0:T(8,128)(2,1)S(1)}, u32[]{:S(2)}, u32[]{:S(2)}) collective-permute-start(bf16[3,128,256]{2,1,0:T(8,128)(2,1)S(1)} %get-tuple-element.43), channel_id=1, source_target_pairs={{0,1},{1,2},{2,3},{3,4},{4,5},{5,6},{6,7},{7,8},{8,9},{9,10},{10,1... | collective-permute-start | bytes 589832 | tf_op jit(solution)/shard_map/ppermute | solution.py:572
  52.5 3.6 %collective-permute-start.7 = (bf16[3,128,256]{2,1,0:T(8,128)(2,1)S(1)}, bf16[3,128,256]{2,1,0:T(8,128)(2,1)S(1)}, u32[]{:S(2)}, u32[]{:S(2)}) collective-permute-start(bf16[3,128,256]{2,1,0:T(8,128)(2,1)S(1)} %get-tuple-element.44), channel_id=1, source_target_pairs={{1,0},{2,1},{3,2},{4,3},{5,4},{6,5},{7,6},{8,7},{9,8},{10,9},{11,1... | collective-permute-start | bytes 589832 | tf_op jit(solution)/shard_map/ppermute | solution.py:575
  56.1 0.0 collective-permute-done.2.before.hid_before
  56.1 0.0 collective-permute-done.3.after.hid_after
  56.1 7.5 %second_conv.1 = (bf16[8,128,256]{2,1,0:T(8,128)(2,1)}, f32[8,128]{1,0:T(8,128)S(1)}) custom-call(s32[8,27]{1,0:T(8,128)} %get-tuple-element.27.index_hbm, bf16[8,128,256]{2,1,0:T(8,128)(2,1)} %get-tuple-element.33.hidden_hbm, bf16[3,128,256]{2,1,0:T(8,128)(2,1)S(1)} %collective-permute-done.2.before.hid_before, ...), custom_call_target="tpu_custom_call" | custom-call | flops 9200000000 | tf_op jit(solution)/shard_map/second_conv/pallas_call | solution.py:45
  63.6 0.0 all-to-all-done.2
  63.6 0.0 collective-permute-done.6.grad_before
  63.6 0.0 collective-permute-done.7.grad_after
  63.6 7.9 %back_conv.1 = (f32[8,128,256]{2,1,0:T(8,128)S(1)}, f32[8,128,256]{2,1,0:T(8,128)S(1)}, f32[32,128]{1,0:T(8,128)S(1)}) custom-call(s32[8,27]{1,0:T(8,128)} %get-tuple-element.27.index_hbm, f32[32,128]{1,0:T(8,128)S(1)} %bitcast.22, bf16[8,128,256]{2,1,0:T(8,128)(2,1)} %get-tuple-element.33.hidden_hbm, ...), custom_call_target="tpu_custom_call" | custom-call | tf_op jit(solution)/shard_map/back_conv/pallas_call | solution.py:45
  71.6 11.0 %all_to_all.44 = f32[32,1,128]{2,1,0:T(1,128)S(1)} all-to-all(f32[32,1,128]{2,1,0:T(1,128)S(1)} %bitcast.26), channel_id=1, replica_groups=mesh['region'=4,'sub'=8] {'region','sub'}, dimensions={0} | all-to-all | bytes 32768 | tf_op jit(solution)/shard_map/all_to_all | solution.py:578
  82.6 1.3 %end.1 = bf16[8,128,256]{2,1,0:T(8,128)(2,1)} custom-call(f32[32,128]{1,0:T(8,128)S(1)} %bitcast.23, f32[8,128,256]{2,1,0:T(8,128)S(1)} %get-tuple-element.48.partial, f32[8,128,256]{2,1,0:T(8,128)S(1)} %get-tuple-element.49.normed, f32[8,256]{1,0:T(8,128)S(1)} %get-tuple-element.45.stats_first.stats), custom_call_target="tpu_custom_call" | custom-call | tf_op jit(solution)/shard_map/end/pallas_call | solution.py:45
Async XLA Ops:
  3.2 19.4 %collective-permute-start = (bf16[3,128,256]{2,1,0:T(8,128)(2,1)S(1)}, bf16[3,128,256]{2,1,0:T(8,128)(2,1)S(1)}, u32[]{:S(2)}, u32[]{:S(2)}) collective-permute-start(bf16[3,128,256]{2,1,0:T(8,128)(2,1)S(1)} %get-tuple-element.30), channel_id=1, source_target_pairs={{0,1},{1,2},{2,3},{3,4},{4,5},{5,6},{6,7},{7,8},{8,9},{9,10},{10,1... | collective-permute-start | bytes 589832 | tf_op jit(solution)/shard_map/ppermute | solution.py:572
  6.2 16.4 %collective-permute-start.1 = (bf16[3,128,256]{2,1,0:T(8,128)(2,1)S(1)}, bf16[3,128,256]{2,1,0:T(8,128)(2,1)S(1)}, u32[]{:S(2)}, u32[]{:S(2)}) collective-permute-start(bf16[3,128,256]{2,1,0:T(8,128)(2,1)S(1)} %get-tuple-element.31), channel_id=1, source_target_pairs={{1,0},{2,1},{3,2},{4,3},{5,4},{6,5},{7,6},{8,7},{9,8},{10,9},{11,1... | collective-permute-start | bytes 589832 | tf_op jit(solution)/shard_map/ppermute | solution.py:575
  12.3 10.3 %all-to-all-start = ((f32[32,1,128]{2,1,0:T(1,128)}), f32[32,1,128]{2,1,0:T(1,128)S(1)}, u32[]{:S(2)}, u32[]{:S(2)}) async-start(f32[32,1,128]{2,1,0:T(1,128)} %bitcast.5), calls=%async_computation | async-start | bytes 32768 | tf_op jit(solution)/shard_map/all_to_all | solution.py:578
  15.2 23.8 %collective-permute-start.4 = (bf16[3,128,256]{2,1,0:T(8,128)(2,1)S(1)}, bf16[3,128,256]{2,1,0:T(8,128)(2,1)S(1)}, u32[]{:S(2)}, u32[]{:S(2)}) collective-permute-start(bf16[3,128,256]{2,1,0:T(8,128)(2,1)S(1)} %get-tuple-element.38), channel_id=1, source_target_pairs={{0,1},{1,2},{2,3},{3,4},{4,5},{5,6},{6,7},{7,8},{8,9},{9,10},{10,1... | collective-permute-start | bytes 589832 | tf_op jit(solution)/shard_map/ppermute | solution.py:572
  17.0 22.0 %collective-permute-start.5 = (bf16[3,128,256]{2,1,0:T(8,128)(2,1)S(1)}, bf16[3,128,256]{2,1,0:T(8,128)(2,1)S(1)}, u32[]{:S(2)}, u32[]{:S(2)}) collective-permute-start(bf16[3,128,256]{2,1,0:T(8,128)(2,1)S(1)} %get-tuple-element.39), channel_id=1, source_target_pairs={{1,0},{2,1},{3,2},{4,3},{5,4},{6,5},{7,6},{8,7},{9,8},{10,9},{11,1... | collective-permute-start | bytes 589832 | tf_op jit(solution)/shard_map/ppermute | solution.py:575
  31.0 14.8 %all-to-all-start.1 = ((f32[32,1,128]{2,1,0:T(1,128)}), f32[32,1,128]{2,1,0:T(1,128)S(1)}, u32[]{:S(2)}, u32[]{:S(2)}) async-start(f32[32,1,128]{2,1,0:T(1,128)} %bitcast.9), calls=%async_computation.1 | async-start | bytes 32768 | tf_op jit(solution)/shard_map/all_to_all | solution.py:578
  33.6 22.5 %collective-permute-start.2 = (bf16[3,128,256]{2,1,0:T(8,128)(2,1)S(1)}, bf16[3,128,256]{2,1,0:T(8,128)(2,1)S(1)}, u32[]{:S(2)}, u32[]{:S(2)}) collective-permute-start(bf16[3,128,256]{2,1,0:T(8,128)(2,1)S(1)} %get-tuple-element.34), channel_id=1, source_target_pairs={{0,1},{1,2},{2,3},{3,4},{4,5},{5,6},{6,7},{7,8},{8,9},{9,10},{10,1... | collective-permute-start | bytes 589832 | tf_op jit(solution)/shard_map/ppermute | solution.py:572
  35.3 20.8 %collective-permute-start.3 = (bf16[3,128,256]{2,1,0:T(8,128)(2,1)S(1)}, bf16[3,128,256]{2,1,0:T(8,128)(2,1)S(1)}, u32[]{:S(2)}, u32[]{:S(2)}) collective-permute-start(bf16[3,128,256]{2,1,0:T(8,128)(2,1)S(1)} %get-tuple-element.35), channel_id=1, source_target_pairs={{1,0},{2,1},{3,2},{4,3},{5,4},{6,5},{7,6},{8,7},{9,8},{10,9},{11,1... | collective-permute-start | bytes 589832 | tf_op jit(solution)/shard_map/ppermute | solution.py:575
  48.1 15.5 %all-to-all-start.2 = ((f32[32,1,128]{2,1,0:T(1,128)}), f32[32,1,128]{2,1,0:T(1,128)S(1)}, u32[]{:S(2)}, u32[]{:S(2)}) async-start(f32[32,1,128]{2,1,0:T(1,128)} %bitcast.13), calls=%async_computation.2 | async-start | bytes 32768 | tf_op jit(solution)/shard_map/all_to_all | solution.py:578
  50.7 12.9 %collective-permute-start.6 = (bf16[3,128,256]{2,1,0:T(8,128)(2,1)S(1)}, bf16[3,128,256]{2,1,0:T(8,128)(2,1)S(1)}, u32[]{:S(2)}, u32[]{:S(2)}) collective-permute-start(bf16[3,128,256]{2,1,0:T(8,128)(2,1)S(1)} %get-tuple-element.43), channel_id=1, source_target_pairs={{0,1},{1,2},{2,3},{3,4},{4,5},{5,6},{6,7},{7,8},{8,9},{9,10},{10,1... | collective-permute-start | bytes 589832 | tf_op jit(solution)/shard_map/ppermute | solution.py:572
  52.5 11.1 %collective-permute-start.7 = (bf16[3,128,256]{2,1,0:T(8,128)(2,1)S(1)}, bf16[3,128,256]{2,1,0:T(8,128)(2,1)S(1)}, u32[]{:S(2)}, u32[]{:S(2)}) collective-permute-start(bf16[3,128,256]{2,1,0:T(8,128)(2,1)S(1)} %get-tuple-element.44), channel_id=1, source_target_pairs={{1,0},{2,1},{3,2},{4,3},{5,4},{6,5},{7,6},{8,7},{9,8},{10,9},{11,1... | collective-permute-start | bytes 589832 | tf_op jit(solution)/shard_map/ppermute | solution.py:575

commit v3 on v2

--- a/solution.py
+++ b/solution.py
@@ -214,21 +214,35 @@
     return total
 
 
-def conv(index, source, pair, weights, backward, capacity, finish, carry):
-    def two(step, carry):
-        first = 2 * step
+def conv(index, source, pairs, weights, backward, capacity, finish, carry):
+    even, odd = pairs
+
+    def build_pair(first, pair):
+        first = jnp.minimum(first, capacity - 2)
         for k in range(2):
             build(index, first + k, source, pair.at[k])
+
+    def finish_pair(first, pair, carry):
         both = product(pair, weights, backward)
         carry = finish(first, both[:128], carry)
         return finish(first + 1, both[128:], carry)
 
-    return lax.fori_loop(0, capacity // 2, two, carry)
+    build_pair(0, even)
+
+    def four(step, carry):
+        first = 4 * step
+        build_pair(first + 2, odd)
+        carry = finish_pair(first, even, carry)
+        build_pair(first + 4, even)
+        return finish_pair(first + 2, odd, carry)
+
+    return lax.fori_loop(0, capacity // 4, four, carry)
 
 
 def conv_scratch(slots, capacity):
     return [
         pltpu.VMEM((3, slots, 16, 8, 256), f32),
+        pltpu.VMEM((2, 9, 192, 256), bf16),
         pltpu.VMEM((2, 9, 192, 256), bf16),
         pltpu.VMEM((27, 256, 256), bf16),
         pltpu.SemaphoreType.DMA,
@@ -256,8 +270,8 @@
 
 def mark_kernel(
     counts_hbm, features, mask, cotangent, gain_first, bias_first, gain_second, bias_second,
-    marked_hbm, marked, feat_up, feat_down, cot_up, cot_down, vectors,
-    stage, cot_stage, cot_sem, mask_stage, vector_stage, feature_sem, small_sem, counts, counts_sem, out_sem,
+    marked, feat_up, feat_down, cot_up, cot_down, vectors,
+    stage, cot_stage, cot_sem, mask_stage, vector_stage, feature_sem, small_sem, counts, counts_sem,
 ):
     capacity = marked.shape[0]
     counting = Fetched(counts_hbm, counts, counts_sem)
@@ -267,9 +281,6 @@
 
     def arriving(b):
         return pltpu.make_async_copy(features.at[b], stage.at[b], feature_sem.at[b])
-
-    def kept(b):
-        return pltpu.make_async_copy(marked.at[b], marked_hbm.at[b], out_sem.at[b])
 
     for copy in small + [arriving(b) for b in range(capacity)]:
         copy.start()
@@ -286,7 +297,6 @@
         wide = wide * jnp.where(b < live, 1.0, 0.0)
         arriving(b).wait()
         marked[b] = jnp.where(join([wide, wide]) > 0.5, stage[b].astype(f32), MARK).astype(bf16)
-        kept(b).start()
         return 0
 
     lax.fori_loop(0, capacity, step, 0, unroll=4)
@@ -300,7 +310,7 @@
             feat[k] = values
             on = values.astype(f32) < MARK_LIMIT
             cot[k] = jnp.where(on, cot_stage[at].astype(f32), 0.0).astype(bf16)
-    for copy in small[1:] + [kept(b) for b in range(capacity)]:
+    for copy in small[1:]:
         copy.wait()
     for k in range(4):
         vectors[k : k + 1, :] = vector_stage[k]
@@ -308,11 +318,13 @@
 
 
 def first_sums_kernel(
-    counts_hbm, marked, neighbors_hbm, row, index_hbm,
+    counts_hbm, marked, neighbors_hbm, row, index_hbm, marked_hbm, out_sem,
     counts, counts_sem, neighbors, neighbors_sem, index, index_sem,
 ):
     counting = Fetched(counts_hbm, counts, counts_sem)
     naming = Fetched(neighbors_hbm, neighbors, neighbors_sem)
+    kept = pltpu.make_async_copy(marked, marked_hbm, out_sem)
+    kept.start()
     device = lax.axis_index(AXES)
     counting.ready()
 
@@ -340,11 +352,12 @@
     moments = lax.fori_loop(0, capacity, step, no_moments(), unroll=2)
     row[...] = jnp.broadcast_to(moments_row(moments), row.shape)
     indexed.wait()
+    kept.wait()
 
 
 def grad_conv_kernel(
     index_hbm, cotangent, marked_hbm, before, after, weights_hbm,
-    grad, source, windows, weights, sem, index, index_sem, stage, stage_sem, marked, marked_sem,
+    grad, source, even, odd, weights, sem, index, index_sem, stage, stage_sem, marked, marked_sem,
 ):
     capacity = marked.shape[0]
     indexing = Fetched(index_hbm, index, index_sem)
@@ -371,13 +384,13 @@
         grad[b] = total
         return carry
 
-    conv(index, source, windows, weights, True, capacity, finish, 0)
+    conv(index, source, (even, odd), weights, True, capacity, finish, 0)
 
 
 def first_conv_kernel(
     index_hbm, counts_hbm, rows, marked_hbm, before, after, vectors, weights_hbm,
-    hidden_hbm, hidden, row, up, down, stats, source, windows, weights, sem, index, index_sem,
-    marked_stage, marked_sem, counts, counts_sem, out_sem,
+    hidden, row, up, down, stats, source, even, odd, weights, sem, index, index_sem,
+    marked_stage, marked_sem, counts, counts_sem,
 ):
     capacity = hidden.shape[0]
     indexing = Fetched(index_hbm, index, index_sem)
@@ -402,24 +415,18 @@
     indexing.ready()
     fetch.wait()
 
-    def kept(b):
-        return pltpu.make_async_copy(hidden.at[b], hidden_hbm.at[b], out_sem.at[b])
-
     def finish(b, total, carry):
         on = marked_stage[b].astype(f32) < MARK_LIMIT
         rounded = total.astype(bf16).astype(f32)
         hidden[b] = jnp.where(on, rounded, MARK).astype(bf16)
-        kept(b).start()
         return add_moments(carry, rounded, on, b == 0)
 
-    moments = conv(index, source, windows, weights, False, capacity, finish, no_moments())
+    moments = conv(index, source, (even, odd), weights, False, capacity, finish, no_moments())
     live = counting.ready()[lax.axis_index(AXES)]
     for k in range(EDGE):
         up[k] = hidden[live - EDGE + k]
         down[k] = hidden[k]
     row[...] = jnp.broadcast_to(moments_row(moments), row.shape)
-    for b in range(capacity):
-        kept(b).wait()
 
 
 def slope_of(pre):
@@ -427,8 +434,10 @@
     return part * (1.0 + pre * (1.0 - part))
 
 
-def second_sums_kernel(counts_hbm, rows, hidden, grad, vectors, row, stats, up, down, counts, counts_sem):
+def second_sums_kernel(counts_hbm, rows, hidden, grad, vectors, row, stats, up, down, hidden_hbm, counts, counts_sem, out_sem):
     counting = Fetched(counts_hbm, counts, counts_sem)
+    kept = pltpu.make_async_copy(hidden, hidden_hbm, out_sem)
+    kept.start()
     capacity = hidden.shape[0]
     mean, inv_scale, voxel_total = combine_moments(rows[...])
     stats[...] = jnp.concatenate(
@@ -451,12 +460,13 @@
     for k in range(EDGE):
         up[k] = grad[live - EDGE + k].astype(bf16)
         down[k] = grad[k].astype(bf16)
+    kept.wait()
     row[...] = jnp.broadcast_to(pairs_row(column_sum(first), column_sum(second)), row.shape)
 
 
 def second_conv_kernel(
     index_hbm, hidden_hbm, before, after, stats, vectors, marked_hbm, weights_hbm,
-    out, done, source, windows, weights, sem, index, index_sem, hidden_stage, hidden_sem, marked, marked_sem,
+    out, done, source, even, odd, weights, sem, index, index_sem, hidden_stage, hidden_sem, marked, marked_sem,
 ):
     capacity = marked.shape[0]
     indexing = Fetched(index_hbm, index, index_sem)
@@ -484,13 +494,13 @@
         out[b] = jnp.where(inputs < MARK_LIMIT, inputs + total, 0.0).astype(bf16)
         return carry
 
-    conv(index, source, windows, weights, False, capacity, finish, 0)
+    conv(index, source, (even, odd), weights, False, capacity, finish, 0)
 
 
 def back_conv_kernel(
     index_hbm, rows, hidden_hbm, hid_before, hid_after, grad, grad_before, grad_after,
     stats_second, marked_hbm, stats_first, vectors, cotangent, weights_hbm, after_conv,
-    partial, normed_out, row, source, windows, weights, sem, index, index_sem, hidden_stage, hidden_sem, marked, marked_sem,
+    partial, normed_out, row, source, even, odd, weights, sem, index, index_sem, hidden_stage, hidden_sem, marked, marked_sem,
     stage, stage_sem,
 ):
     capacity = marked.shape[0]
@@ -533,7 +543,7 @@
         return carry[0] + eight_rows(scaled), carry[1] + eight_rows(scaled * normed)
 
     zero = jnp.zeros((8, 256), f32)
-    sums = conv(index, source, windows, weights, True, capacity, finish, (zero, zero))
+    sums = conv(index, source, (even, odd), weights, True, capacity, finish, (zero, zero))
     row[...] = jnp.broadcast_to(pairs_row(column_sum(sums[0]), column_sum(sums[1])), row.shape)
 
 
@@ -586,20 +596,21 @@
     slots = capacity + 2 * EDGE + 1
 
     dma = pltpu.SemaphoreType.DMA
-    marked, marked_near, feat_up, feat_down, cot_up, cot_down, vectors = call(
-        mark_kernel, "mark", [hbm()] * 8, [(*whole, "hbm"), whole, edge, edge, edge, edge, vector],
+    marked_near, feat_up, feat_down, cot_up, cot_down, vectors = call(
+        mark_kernel, "mark", [hbm()] * 8, [whole, edge, edge, edge, edge, vector],
         [
             pltpu.VMEM(*whole), pltpu.VMEM((2 * EDGE, voxels, channels), bf16), dma((2 * EDGE,)),
             pltpu.VMEM((capacity, voxels), jnp.int32),
             pltpu.VMEM((4, 1, channels), f32),
-            dma((capacity,)), dma((5,)), pltpu.SMEM(counts.shape, jnp.int32), dma, dma((capacity,)),
+            dma((capacity,)), dma((5,)), pltpu.SMEM(counts.shape, jnp.int32), dma,
         ],
     )(counts, features, voxel_mask, cotangent, gain_first, bias_first, gain_second, bias_second)
     cot_before, cot_after = shift_up(cot_up), shift_down(cot_down)
     feat_before, feat_after = shift_up(feat_up), shift_down(feat_down)
-    row, index = call(
-        first_sums_kernel, "first_sums", [hbm(), vmem(), hbm()], [packed, (*table, "hbm")],
+    row, index, marked = call(
+        first_sums_kernel, "first_sums", [hbm(), vmem(), hbm()], [packed, (*table, "hbm"), (*whole, "hbm")],
         [
+            dma,
             pltpu.SMEM(counts.shape, jnp.int32), dma, pltpu.VMEM(*table), dma, pltpu.VMEM(*table), dma,
         ],
     )(counts, marked_near, neighbors)
@@ -610,21 +621,21 @@
         [whole_wide], conv_scratch(slots, capacity) + [pltpu.VMEM(*whole), dma] * 2,
     )(index, cotangent, marked, cot_before, cot_after, w_second)
 
-    hidden, hidden_near, row, hid_up, hid_down, stats_first = call(
+    hidden_near, row, hid_up, hid_down, stats_first = call(
         first_conv_kernel, "first_conv",
         [hbm(), hbm(), vmem(), hbm(), vmem(), vmem(), vmem(), hbm()],
-        [(*whole, "hbm"), whole, packed, edge, edge, vector],
+        [whole, packed, edge, edge, vector],
         conv_scratch(slots, capacity)
         + [
-            pltpu.VMEM(*whole), dma, pltpu.SMEM(counts.shape, jnp.int32), dma, dma((capacity,)),
+            pltpu.VMEM(*whole), dma, pltpu.SMEM(counts.shape, jnp.int32), dma,
         ],
     )(index, counts, rows_first, marked, feat_before, feat_after, vectors, w_first)
     rows_second = exchange(row)
     hid_before, hid_after = shift_up(hid_up), shift_down(hid_down)
 
-    row, stats_second, grad_up, grad_down = call(
-        second_sums_kernel, "second_sums", [hbm()] + [vmem()] * 4, [packed, vector, edge, edge],
-        [pltpu.SMEM(counts.shape, jnp.int32), dma],
+    row, stats_second, grad_up, grad_down, hidden = call(
+        second_sums_kernel, "second_sums", [hbm()] + [vmem()] * 4, [packed, vector, edge, edge, (*whole, "hbm")],
+        [pltpu.SMEM(counts.shape, jnp.int32), dma, dma],
     )(
         counts, rows_second, hidden_near, grad, vectors
     )

time: 84.2 us -> 83.2 us (0.988)
  Pallas kernels: 39.4 us -> 38.1 us
    pallas_call x8, Pallas kernels: 39.4 us -> 38.1 us  [run(): made(*(pltpu.with_memory_space_constraint(x, pltpu.HBM) if spec.memory_sp...]
  transfers between devices with their start and end apart: 11 -> 11, of which waited for: 1 -> 2; matrix products, arithmetic and copies ran while one was open for 0% -> 0% of each run, Pallas kernels for 33% -> 33%
where the time goes in v3:
time: 83.2 us; the launch traced here: 82.8 us
  Pallas kernels  38.1 us (46%)
  starting transfers between devices  30.7 us (37%)
  blocking collectives  11.1 us (13%)
  waiting for transfers between devices  2.13 us (3%)
    pallas_call x8, Pallas kernels, run(): made(*(pltpu.with_memory_space_constraint(x, pltpu.HBM) if spec.memory_sp...  38.1 us
    ppermute x4, starting transfers between devices, shift_down(): lax.ppermute(x, AXES, [((i + 1) % devices, i) for i in range(devices)])  14.3 us
    all_to_all x1, blocking collectives, exchange(): return lax.all_to_all(row, AXES, 0, 0, tiled=True)  11.1 us
    ppermute x4, starting transfers between devices, shift_up(): lax.ppermute(x, AXES, [(i, (i + 1) % devices) for i in range(devices)])  8.37 us
    all_to_all x3, starting transfers between devices, exchange(): return lax.all_to_all(row, AXES, 0, 0, tiled=True)  7.98 us
    all_to_all x3, waiting for transfers between devices, exchange(): return lax.all_to_all(row, AXES, 0, 0, tiled=True)  2.02 us
  transfers between devices with their start and end apart: 11, of which 2 were waited for; matrix products, arithmetic and copies ran while one was open for 0% of the time, Pallas kernels for 33%

profile of v3, /device:TPU:0, one launch (start us, length us, event | category | flops | bytes accessed | tf_op | source)
XLA Modules:
  0.0 82.8 jit_solution(12875634654828002495)
XLA Ops:
  0.6 2.1 %mark.1 = (bf16[8,128,256]{2,1,0:T(8,128)(2,1)S(1)}, bf16[3,128,256]{2,1,0:T(8,128)(2,1)S(1)}, bf16[3,128,256]{2,1,0:T(8,128)(2,1)S(1)}, bf16[3,128,256]{2,1,0:T...) custom-call(s32[32]{0:T(128)} %counts_hbm.7, bf16[8,128,256]{2,1,0:T(8,128)(2,1)} %features.1, ...), custom_call_target="tpu_custom_call" | custom-call | tf_op jit(solution)/shard_map/mark/pallas_call | solution.py:45
  2.8 3.0 %collective-permute-start = (bf16[3,128,256]{2,1,0:T(8,128)(2,1)S(1)}, bf16[3,128,256]{2,1,0:T(8,128)(2,1)S(1)}, u32[]{:S(2)}, u32[]{:S(2)}) collective-permute-start(bf16[3,128,256]{2,1,0:T(8,128)(2,1)S(1)} %get-tuple-element.30), channel_id=1, source_target_pairs={{0,1},{1,2},{2,3},{3,4},{4,5},{5,6},{6,7},{7,8},{8,9},{9,10},{10,1... | collective-permute-start | bytes 589832 | tf_op jit(solution)/shard_map/ppermute | solution.py:582
  5.8 3.5 %collective-permute-start.1 = (bf16[3,128,256]{2,1,0:T(8,128)(2,1)S(1)}, bf16[3,128,256]{2,1,0:T(8,128)(2,1)S(1)}, u32[]{:S(2)}, u32[]{:S(2)}) collective-permute-start(bf16[3,128,256]{2,1,0:T(8,128)(2,1)S(1)} %get-tuple-element.31), channel_id=1, source_target_pairs={{1,0},{2,1},{3,2},{4,3},{5,4},{6,5},{7,6},{8,7},{9,8},{10,9},{11,1... | collective-permute-start | bytes 589832 | tf_op jit(solution)/shard_map/ppermute | solution.py:585
  9.3 2.6 %first_sums.1 = (f32[32,128]{1,0:T(8,128)}, s32[8,27]{1,0:T(8,128)}, bf16[8,128,256]{2,1,0:T(8,128)(2,1)}) custom-call(s32[32]{0:T(128)} %counts_hbm.7, bf16[8,128,256]{2,1,0:T(8,128)(2,1)S(1)} %get-tuple-element.26.marked, s32[8,27]{1,0:T(8,128)} %neighbors_hbm.1), custom_call_target="tpu_custom_call" | custom-call | tf_op jit(solution)/shard_map/first_sums/pallas_call | solution.py:45
  11.9 2.9 %all-to-all-start = ((f32[32,1,128]{2,1,0:T(1,128)}), f32[32,1,128]{2,1,0:T(1,128)S(1)}, u32[]{:S(2)}, u32[]{:S(2)}) async-start(f32[32,1,128]{2,1,0:T(1,128)} %bitcast.5), calls=%async_computation | async-start | bytes 32768 | tf_op jit(solution)/shard_map/all_to_all | solution.py:588
  14.8 1.8 %collective-permute-start.2 = (bf16[3,128,256]{2,1,0:T(8,128)(2,1)S(1)}, bf16[3,128,256]{2,1,0:T(8,128)(2,1)S(1)}, u32[]{:S(2)}, u32[]{:S(2)}) collective-permute-start(bf16[3,128,256]{2,1,0:T(8,128)(2,1)S(1)} %get-tuple-element.35), channel_id=1, source_target_pairs={{0,1},{1,2},{2,3},{3,4},{4,5},{5,6},{6,7},{7,8},{8,9},{9,10},{10,1... | collective-permute-start | bytes 589832 | tf_op jit(solution)/shard_map/ppermute | solution.py:582
  16.6 3.6 %collective-permute-start.3 = (bf16[3,128,256]{2,1,0:T(8,128)(2,1)S(1)}, bf16[3,128,256]{2,1,0:T(8,128)(2,1)S(1)}, u32[]{:S(2)}, u32[]{:S(2)}) collective-permute-start(bf16[3,128,256]{2,1,0:T(8,128)(2,1)S(1)} %get-tuple-element.36), channel_id=1, source_target_pairs={{1,0},{2,1},{3,2},{4,3},{5,4},{6,5},{7,6},{8,7},{9,8},{10,9},{11,1... | collective-permute-start | bytes 589832 | tf_op jit(solution)/shard_map/ppermute | solution.py:585
  20.1 2.0 %all-to-all-done = f32[32,1,128]{2,1,0:T(1,128)S(1)} async-done(((f32[32,1,128]{2,1,0:T(1,128)}), f32[32,1,128]{2,1,0:T(1,128)S(1)}, u32[]{:S(2)}, u32[]{:S(2)}) %all-to-all-start) | async-done | bytes 16416 | tf_op jit(solution)/shard_map/all_to_all | solution.py:588
  22.2 0.0 collective-permute-done.before
  22.2 0.0 collective-permute-done.1.after
  22.2 8.2 %first_conv.1 = (bf16[8,128,256]{2,1,0:T(8,128)(2,1)S(1)}, f32[32,128]{1,0:T(8,128)}, bf16[3,128,256]{2,1,0:T(8,128)(2,1)S(1)}, bf16[3,128,256]{2,1,0:T(8,128)(2,1)S(1)}, f32[8,256]{1,0:T(8,128)S(1)}) custom-call(s32[8,27]{1,0:T(8,128)} %get-tuple-element.27.index_hbm, s32[32]{0:T(128)} %counts_hbm.7, f32[32,128]{1,0:T(8,128)S(1)} %bitcast.24, ...), custom_call_target="tpu_custom_call" | custom-call | flops 9200000000 | tf_op jit(solution)/shard_map/first_conv/pallas_call | solution.py:45
  30.4 2.6 %all-to-all-start.1 = ((f32[32,1,128]{2,1,0:T(1,128)}), f32[32,1,128]{2,1,0:T(1,128)S(1)}, u32[]{:S(2)}, u32[]{:S(2)}) async-start(f32[32,1,128]{2,1,0:T(1,128)} %bitcast.9), calls=%async_computation.1 | async-start | bytes 32768 | tf_op jit(solution)/shard_map/all_to_all | solution.py:588
  32.9 1.7 %collective-permute-start.4 = (bf16[3,128,256]{2,1,0:T(8,128)(2,1)S(1)}, bf16[3,128,256]{2,1,0:T(8,128)(2,1)S(1)}, u32[]{:S(2)}, u32[]{:S(2)}) collective-permute-start(bf16[3,128,256]{2,1,0:T(8,128)(2,1)S(1)} %get-tuple-element.38), channel_id=1, source_target_pairs={{0,1},{1,2},{2,3},{3,4},{4,5},{5,6},{6,7},{7,8},{8,9},{9,10},{10,1... | collective-permute-start | bytes 589832 | tf_op jit(solution)/shard_map/ppermute | solution.py:582
  34.7 3.7 %collective-permute-start.5 = (bf16[3,128,256]{2,1,0:T(8,128)(2,1)S(1)}, bf16[3,128,256]{2,1,0:T(8,128)(2,1)S(1)}, u32[]{:S(2)}, u32[]{:S(2)}) collective-permute-start(bf16[3,128,256]{2,1,0:T(8,128)(2,1)S(1)} %get-tuple-element.39), channel_id=1, source_target_pairs={{1,0},{2,1},{3,2},{4,3},{5,4},{6,5},{7,6},{8,7},{9,8},{10,9},{11,1... | collective-permute-start | bytes 589832 | tf_op jit(solution)/shard_map/ppermute | solution.py:585
  38.3 0.0 collective-permute-done.2.before
  38.3 0.0 collective-permute-done.3.after
  38.4 6.6 %grad_conv.1.grad = f32[8,128,256]{2,1,0:T(8,128)S(1)} custom-call(s32[8,27]{1,0:T(8,128)} %get-tuple-element.27.index_hbm, bf16[8,128,256]{2,1,0:T(8,128)(2,1)} %cotangent.5, bf16[8,128,256]{2,1,0:T(8,128)(2,1)} %get-tuple-element.29.marked_hbm, bf16[3,128,256]{2,1,0:T(8,128)(2,1)S(1)} %collective-permute-done.2.before, ...), custom_call_target="tpu_custom_call" | custom-call | tf_op jit(solution)/shard_map/grad_conv/pallas_call | solution.py:45
  44.9 0.0 all-to-all-done.1
  44.9 2.3 %second_sums.1 = (f32[32,128]{1,0:T(8,128)}, f32[8,256]{1,0:T(8,128)S(1)}, bf16[3,128,256]{2,1,0:T(8,128)(2,1)S(1)}, bf16[3,128,256]{2,1,0:T(8,128)(2,1)S(1)}, bf16[8,128,256]{2,1,0:T(8,128)(2,1)}) custom-call(s32[32]{0:T(128)} %counts_hbm.7, f32[32,128]{1,0:T(8,128)S(1)} %bitcast.25, bf16[8,128,256]{2,1,0:T(8,128)(2,1)S(1)} %get-tuple-element.34.hidden, ...), custom_call_target="tpu_custom_call" | custom-call | flops 57500000256 | tf_op jit(solution)/shard_map/second_sums/pallas_call | solution.py:45
  47.3 2.5 %all-to-all-start.2 = ((f32[32,1,128]{2,1,0:T(1,128)}), f32[32,1,128]{2,1,0:T(1,128)S(1)}, u32[]{:S(2)}, u32[]{:S(2)}) async-start(f32[32,1,128]{2,1,0:T(1,128)} %bitcast.13), calls=%async_computation.2 | async-start | bytes 32768 | tf_op jit(solution)/shard_map/all_to_all | solution.py:588
  49.8 1.8 %collective-permute-start.6 = (bf16[3,128,256]{2,1,0:T(8,128)(2,1)S(1)}, bf16[3,128,256]{2,1,0:T(8,128)(2,1)S(1)}, u32[]{:S(2)}, u32[]{:S(2)}) collective-permute-start(bf16[3,128,256]{2,1,0:T(8,128)(2,1)S(1)} %get-tuple-element.43), channel_id=1, source_target_pairs={{0,1},{1,2},{2,3},{3,4},{4,5},{5,6},{6,7},{7,8},{8,9},{9,10},{10,1... | collective-permute-start | bytes 589832 | tf_op jit(solution)/shard_map/ppermute | solution.py:582
  51.6 3.6 %collective-permute-start.7 = (bf16[3,128,256]{2,1,0:T(8,128)(2,1)S(1)}, bf16[3,128,256]{2,1,0:T(8,128)(2,1)S(1)}, u32[]{:S(2)}, u32[]{:S(2)}) collective-permute-start(bf16[3,128,256]{2,1,0:T(8,128)(2,1)S(1)} %get-tuple-element.44), channel_id=1, source_target_pairs={{1,0},{2,1},{3,2},{4,3},{5,4},{6,5},{7,6},{8,7},{9,8},{10,9},{11,1... | collective-permute-start | bytes 589832 | tf_op jit(solution)/shard_map/ppermute | solution.py:585
  55.2 0.0 collective-permute-done.4.before.hid_before
  55.2 0.0 collective-permute-done.5.after.hid_after
  55.2 7.3 %second_conv.1 = (bf16[8,128,256]{2,1,0:T(8,128)(2,1)}, f32[8,128]{1,0:T(8,128)S(1)}) custom-call(s32[8,27]{1,0:T(8,128)} %get-tuple-element.27.index_hbm, bf16[8,128,256]{2,1,0:T(8,128)(2,1)} %get-tuple-element.37.hidden_hbm, bf16[3,128,256]{2,1,0:T(8,128)(2,1)S(1)} %collective-permute-done.4.before.hid_before, ...), custom_call_target="tpu_custom_call" | custom-call | flops 9200000000 | tf_op jit(solution)/shard_map/second_conv/pallas_call | solution.py:45
  62.5 0.0 all-to-all-done.2
  62.5 0.0 collective-permute-done.6.grad_before
  62.6 0.1 collective-permute-done.7.grad_after
  62.7 7.7 %back_conv.1 = (f32[8,128,256]{2,1,0:T(8,128)S(1)}, f32[8,128,256]{2,1,0:T(8,128)S(1)}, f32[32,128]{1,0:T(8,128)S(1)}) custom-call(s32[8,27]{1,0:T(8,128)} %get-tuple-element.27.index_hbm, f32[32,128]{1,0:T(8,128)S(1)} %bitcast.22, bf16[8,128,256]{2,1,0:T(8,128)(2,1)} %get-tuple-element.37.hidden_hbm, ...), custom_call_target="tpu_custom_call" | custom-call | tf_op jit(solution)/shard_map/back_conv/pallas_call | solution.py:45
  70.4 11.1 %all_to_all.44 = f32[32,1,128]{2,1,0:T(1,128)S(1)} all-to-all(f32[32,1,128]{2,1,0:T(1,128)S(1)} %bitcast.26), channel_id=1, replica_groups=mesh['region'=4,'sub'=8] {'region','sub'}, dimensions={0} | all-to-all | bytes 32768 | tf_op jit(solution)/shard_map/all_to_all | solution.py:588
  81.5 1.3 %end.1 = bf16[8,128,256]{2,1,0:T(8,128)(2,1)} custom-call(f32[32,128]{1,0:T(8,128)S(1)} %bitcast.23, f32[8,128,256]{2,1,0:T(8,128)S(1)} %get-tuple-element.48.partial, f32[8,128,256]{2,1,0:T(8,128)S(1)} %get-tuple-element.49.normed, f32[8,256]{1,0:T(8,128)S(1)} %get-tuple-element.45.stats_first.stats), custom_call_target="tpu_custom_call" | custom-call | tf_op jit(solution)/shard_map/end/pallas_call | solution.py:45
Async XLA Ops:
  2.8 19.4 %collective-permute-start = (bf16[3,128,256]{2,1,0:T(8,128)(2,1)S(1)}, bf16[3,128,256]{2,1,0:T(8,128)(2,1)S(1)}, u32[]{:S(2)}, u32[]{:S(2)}) collective-permute-start(bf16[3,128,256]{2,1,0:T(8,128)(2,1)S(1)} %get-tuple-element.30), channel_id=1, source_target_pairs={{0,1},{1,2},{2,3},{3,4},{4,5},{5,6},{6,7},{7,8},{8,9},{9,10},{10,1... | collective-permute-start | bytes 589832 | tf_op jit(solution)/shard_map/ppermute | solution.py:582
  5.8 16.4 %collective-permute-start.1 = (bf16[3,128,256]{2,1,0:T(8,128)(2,1)S(1)}, bf16[3,128,256]{2,1,0:T(8,128)(2,1)S(1)}, u32[]{:S(2)}, u32[]{:S(2)}) collective-permute-start(bf16[3,128,256]{2,1,0:T(8,128)(2,1)S(1)} %get-tuple-element.31), channel_id=1, source_target_pairs={{1,0},{2,1},{3,2},{4,3},{5,4},{6,5},{7,6},{8,7},{9,8},{10,9},{11,1... | collective-permute-start | bytes 589832 | tf_op jit(solution)/shard_map/ppermute | solution.py:585
  11.9 10.3 %all-to-all-start = ((f32[32,1,128]{2,1,0:T(1,128)}), f32[32,1,128]{2,1,0:T(1,128)S(1)}, u32[]{:S(2)}, u32[]{:S(2)}) async-start(f32[32,1,128]{2,1,0:T(1,128)} %bitcast.5), calls=%async_computation | async-start | bytes 32768 | tf_op jit(solution)/shard_map/all_to_all | solution.py:588
  14.8 23.6 %collective-permute-start.2 = (bf16[3,128,256]{2,1,0:T(8,128)(2,1)S(1)}, bf16[3,128,256]{2,1,0:T(8,128)(2,1)S(1)}, u32[]{:S(2)}, u32[]{:S(2)}) collective-permute-start(bf16[3,128,256]{2,1,0:T(8,128)(2,1)S(1)} %get-tuple-element.35), channel_id=1, source_target_pairs={{0,1},{1,2},{2,3},{3,4},{4,5},{5,6},{6,7},{7,8},{8,9},{9,10},{10,1... | collective-permute-start | bytes 589832 | tf_op jit(solution)/shard_map/ppermute | solution.py:582
  16.6 21.8 %collective-permute-start.3 = (bf16[3,128,256]{2,1,0:T(8,128)(2,1)S(1)}, bf16[3,128,256]{2,1,0:T(8,128)(2,1)S(1)}, u32[]{:S(2)}, u32[]{:S(2)}) collective-permute-start(bf16[3,128,256]{2,1,0:T(8,128)(2,1)S(1)} %get-tuple-element.36), channel_id=1, source_target_pairs={{1,0},{2,1},{3,2},{4,3},{5,4},{6,5},{7,6},{8,7},{9,8},{10,9},{11,1... | collective-permute-start | bytes 589832 | tf_op jit(solution)/shard_map/ppermute | solution.py:585
  30.4 14.6 %all-to-all-start.1 = ((f32[32,1,128]{2,1,0:T(1,128)}), f32[32,1,128]{2,1,0:T(1,128)S(1)}, u32[]{:S(2)}, u32[]{:S(2)}) async-start(f32[32,1,128]{2,1,0:T(1,128)} %bitcast.9), calls=%async_computation.1 | async-start | bytes 32768 | tf_op jit(solution)/shard_map/all_to_all | solution.py:588
  32.9 22.3 %collective-permute-start.4 = (bf16[3,128,256]{2,1,0:T(8,128)(2,1)S(1)}, bf16[3,128,256]{2,1,0:T(8,128)(2,1)S(1)}, u32[]{:S(2)}, u32[]{:S(2)}) collective-permute-start(bf16[3,128,256]{2,1,0:T(8,128)(2,1)S(1)} %get-tuple-element.38), channel_id=1, source_target_pairs={{0,1},{1,2},{2,3},{3,4},{4,5},{5,6},{6,7},{7,8},{8,9},{9,10},{10,1... | collective-permute-start | bytes 589832 | tf_op jit(solution)/shard_map/ppermute | solution.py:582
  34.7 20.6 %collective-permute-start.5 = (bf16[3,128,256]{2,1,0:T(8,128)(2,1)S(1)}, bf16[3,128,256]{2,1,0:T(8,128)(2,1)S(1)}, u32[]{:S(2)}, u32[]{:S(2)}) collective-permute-start(bf16[3,128,256]{2,1,0:T(8,128)(2,1)S(1)} %get-tuple-element.39), channel_id=1, source_target_pairs={{1,0},{2,1},{3,2},{4,3},{5,4},{6,5},{7,6},{8,7},{9,8},{10,9},{11,1... | collective-permute-start | bytes 589832 | tf_op jit(solution)/shard_map/ppermute | solution.py:585
  47.3 15.3 %all-to-all-start.2 = ((f32[32,1,128]{2,1,0:T(1,128)}), f32[32,1,128]{2,1,0:T(1,128)S(1)}, u32[]{:S(2)}, u32[]{:S(2)}) async-start(f32[32,1,128]{2,1,0:T(1,128)} %bitcast.13), calls=%async_computation.2 | async-start | bytes 32768 | tf_op jit(solution)/shard_map/all_to_all | solution.py:588
  49.8 12.7 %collective-permute-start.6 = (bf16[3,128,256]{2,1,0:T(8,128)(2,1)S(1)}, bf16[3,128,256]{2,1,0:T(8,128)(2,1)S(1)}, u32[]{:S(2)}, u32[]{:S(2)}) collective-permute-start(bf16[3,128,256]{2,1,0:T(8,128)(2,1)S(1)} %get-tuple-element.43), channel_id=1, source_target_pairs={{0,1},{1,2},{2,3},{3,4},{4,5},{5,6},{6,7},{7,8},{8,9},{9,10},{10,1... | collective-permute-start | bytes 589832 | tf_op jit(solution)/shard_map/ppermute | solution.py:582
  51.6 11.0 %collective-permute-start.7 = (bf16[3,128,256]{2,1,0:T(8,128)(2,1)S(1)}, bf16[3,128,256]{2,1,0:T(8,128)(2,1)S(1)}, u32[]{:S(2)}, u32[]{:S(2)}) collective-permute-start(bf16[3,128,256]{2,1,0:T(8,128)(2,1)S(1)} %get-tuple-element.44), channel_id=1, source_target_pairs={{1,0},{2,1},{3,2},{4,3},{5,4},{6,5},{7,6},{8,7},{9,8},{10,9},{11,1... | collective-permute-start | bytes 589832 | tf_op jit(solution)/shard_map/ppermute | solution.py:585

commit v4 on v3

--- a/solution.py
+++ b/solution.py
@@ -269,12 +269,14 @@
 
 
 def mark_kernel(
-    counts_hbm, features, mask, cotangent, gain_first, bias_first, gain_second, bias_second,
-    marked, feat_up, feat_down, cot_up, cot_down, vectors,
+    counts_hbm, neighbors_hbm, features, mask, cotangent, gain_first, bias_first, gain_second, bias_second,
+    marked, feat_up, feat_down, cot_up, cot_down, vectors, index_hbm,
+    neighbors, neighbors_sem, index, index_sem,
     stage, cot_stage, cot_sem, mask_stage, vector_stage, feature_sem, small_sem, counts, counts_sem,
 ):
     capacity = marked.shape[0]
     counting = Fetched(counts_hbm, counts, counts_sem)
+    naming = Fetched(neighbors_hbm, neighbors, neighbors_sem)
     small = [pltpu.make_async_copy(mask, mask_stage, small_sem.at[0])]
     for k, vector in enumerate((gain_first, bias_first, gain_second, bias_second)):
         small.append(pltpu.make_async_copy(vector, vector_stage.at[k], small_sem.at[k + 1]))
@@ -284,51 +286,15 @@
 
     for copy in small + [arriving(b) for b in range(capacity)]:
         copy.start()
-    live = counting.ready()[lax.axis_index(AXES)]
+    device = lax.axis_index(AXES)
+    live = counting.ready()[device]
     edges = []
     for k in range(EDGE):
         for at, brick in ((k, live - EDGE + k), (EDGE + k, k)):
             edges.append(pltpu.make_async_copy(cotangent.at[brick], cot_stage.at[at], cot_sem.at[at]))
     for copy in edges:
         copy.start()
-    small[0].wait()
-    def step(b, _):
-        wide = jnp.broadcast_to(mask_stage[pl.ds(b, 1), :].astype(f32), (128, 128)).T
-        wide = wide * jnp.where(b < live, 1.0, 0.0)
-        arriving(b).wait()
-        marked[b] = jnp.where(join([wide, wide]) > 0.5, stage[b].astype(f32), MARK).astype(bf16)
-        return 0
-
-    lax.fori_loop(0, capacity, step, 0, unroll=4)
-    for copy in edges:
-        copy.wait()
-    for k in range(EDGE):
-        for feat, cot, at, brick in (
-            (feat_up, cot_up, k, live - EDGE + k), (feat_down, cot_down, EDGE + k, k)
-        ):
-            values = marked[brick]
-            feat[k] = values
-            on = values.astype(f32) < MARK_LIMIT
-            cot[k] = jnp.where(on, cot_stage[at].astype(f32), 0.0).astype(bf16)
-    for copy in small[1:]:
-        copy.wait()
-    for k in range(4):
-        vectors[k : k + 1, :] = vector_stage[k]
-    vectors[4:8, :] = jnp.zeros((4, 256), f32)
-
-
-def first_sums_kernel(
-    counts_hbm, marked, neighbors_hbm, row, index_hbm, marked_hbm, out_sem,
-    counts, counts_sem, neighbors, neighbors_sem, index, index_sem,
-):
-    counting = Fetched(counts_hbm, counts, counts_sem)
-    naming = Fetched(neighbors_hbm, neighbors, neighbors_sem)
-    kept = pltpu.make_async_copy(marked, marked_hbm, out_sem)
-    kept.start()
-    device = lax.axis_index(AXES)
-    counting.ready()
-
-    capacity = marked.shape[0]
+
     live_before = counts[jnp.maximum(device - 1, 0)]
     named = naming.ready()[...]
     owner = lax.div(named, capacity)
@@ -344,14 +310,45 @@
     indexed = pltpu.make_async_copy(index, index_hbm, index_sem)
     indexed.start()
 
+    small[0].wait()
+    def step(b, _):
+        wide = jnp.broadcast_to(mask_stage[pl.ds(b, 1), :].astype(f32), (128, 128)).T
+        wide = wide * jnp.where(b < live, 1.0, 0.0)
+        arriving(b).wait()
+        marked[b] = jnp.where(join([wide, wide]) > 0.5, stage[b].astype(f32), MARK).astype(bf16)
+        return 0
+
+    lax.fori_loop(0, capacity, step, 0, unroll=4)
+    for copy in edges:
+        copy.wait()
+    for k in range(EDGE):
+        for feat, cot, at, brick in (
+            (feat_up, cot_up, k, live - EDGE + k), (feat_down, cot_down, EDGE + k, k)
+        ):
+            values = marked[brick]
+            feat[k] = values
+            on = values.astype(f32) < MARK_LIMIT
+            cot[k] = jnp.where(on, cot_stage[at].astype(f32), 0.0).astype(bf16)
+    indexed.wait()
+    for copy in small[1:]:
+        copy.wait()
+    for k in range(4):
+        vectors[k : k + 1, :] = vector_stage[k]
+    vectors[4:8, :] = jnp.zeros((4, 256), f32)
+
+
+def first_sums_kernel(marked, row, marked_hbm, out_sem):
+    kept = pltpu.make_async_copy(marked, marked_hbm, out_sem)
+    kept.start()
+    capacity = marked.shape[0]
+
 
     def step(b, moments):
         values = marked[b].astype(f32)
         return add_moments(moments, values, values < MARK_LIMIT, b == 0)
 
-    moments = lax.fori_loop(0, capacity, step, no_moments(), unroll=2)
+    moments = lax.fori_loop(0, capacity, step, no_moments(), unroll=4)
     row[...] = jnp.broadcast_to(moments_row(moments), row.shape)
-    indexed.wait()
     kept.wait()
 
 
@@ -596,24 +593,22 @@
     slots = capacity + 2 * EDGE + 1
 
     dma = pltpu.SemaphoreType.DMA
-    marked_near, feat_up, feat_down, cot_up, cot_down, vectors = call(
-        mark_kernel, "mark", [hbm()] * 8, [whole, edge, edge, edge, edge, vector],
+    marked_near, feat_up, feat_down, cot_up, cot_down, vectors, index = call(
+        mark_kernel, "mark", [hbm()] * 9,
+        [whole, edge, edge, edge, edge, vector, (*table, "hbm")],
         [
+            pltpu.VMEM(*table), dma, pltpu.VMEM(*table), dma,
             pltpu.VMEM(*whole), pltpu.VMEM((2 * EDGE, voxels, channels), bf16), dma((2 * EDGE,)),
             pltpu.VMEM((capacity, voxels), jnp.int32),
             pltpu.VMEM((4, 1, channels), f32),
             dma((capacity,)), dma((5,)), pltpu.SMEM(counts.shape, jnp.int32), dma,
         ],
-    )(counts, features, voxel_mask, cotangent, gain_first, bias_first, gain_second, bias_second)
+    )(counts, neighbors, features, voxel_mask, cotangent, gain_first, bias_first, gain_second, bias_second)
     cot_before, cot_after = shift_up(cot_up), shift_down(cot_down)
     feat_before, feat_after = shift_up(feat_up), shift_down(feat_down)
-    row, index, marked = call(
-        first_sums_kernel, "first_sums", [hbm(), vmem(), hbm()], [packed, (*table, "hbm"), (*whole, "hbm")],
-        [
-            dma,
-            pltpu.SMEM(counts.shape, jnp.int32), dma, pltpu.VMEM(*table), dma, pltpu.VMEM(*table), dma,
-        ],
-    )(counts, marked_near, neighbors)
+    row, marked = call(
+        first_sums_kernel, "first_sums", [vmem()], [packed, (*whole, "hbm")], [dma]
+    )(marked_near)
     rows_first = exchange(row)
 
     (grad,) = call(

time: 83.2 us -> 82.5 us (level)
  transfers between devices with their start and end apart: 11 -> 11, of which waited for: 2 -> 2; matrix products, arithmetic and copies ran while one was open for 0% -> 0% of each run, Pallas kernels for 33% -> 32%
where the time goes in v4:
time: 82.5 us; the launch traced here: 82.2 us
  Pallas kernels  37.5 us (45%)
  starting transfers between devices  30.7 us (37%)
  blocking collectives  11.2 us (14%)
  waiting for transfers between devices  2.13 us (3%)
    pallas_call x8, Pallas kernels, run(): made(*(pltpu.with_memory_space_constraint(x, pltpu.HBM) if spec.memory_sp...  37.5 us
    ppermute x4, starting transfers between devices, shift_down(): lax.ppermute(x, AXES, [((i + 1) % devices, i) for i in range(devices)])  14.3 us
    all_to_all x1, blocking collectives, exchange(): return lax.all_to_all(row, AXES, 0, 0, tiled=True)  11.2 us
    ppermute x4, starting transfers between devices, shift_up(): lax.ppermute(x, AXES, [(i, (i + 1) % devices) for i in range(devices)])  8.37 us
    all_to_all x3, starting transfers between devices, exchange(): return lax.all_to_all(row, AXES, 0, 0, tiled=True)  7.98 us
    all_to_all x3, waiting for transfers between devices, exchange(): return lax.all_to_all(row, AXES, 0, 0, tiled=True)  2.02 us
  transfers between devices with their start and end apart: 11, of which 2 were waited for; matrix products, arithmetic and copies ran while one was open for 0% of the time, Pallas kernels for 32%

profile of v4, /device:TPU:0, one launch (start us, length us, event | category | flops | bytes accessed | tf_op | source)
XLA Modules:
  0.0 82.2 jit_solution(2175610404940692299)
XLA Ops:
  0.6 2.2 %mark.1 = (bf16[8,128,256]{2,1,0:T(8,128)(2,1)S(1)}, bf16[3,128,256]{2,1,0:T(8,128)(2,1)S(1)}, bf16[3,128,256]{2,1,0:T(8,128)(2,1)S(1)}, bf16[3,128,256]{2,1,0:T...) custom-call(s32[32]{0:T(128)} %counts_hbm.5, s32[8,27]{1,0:T(8,128)} %neighbors_hbm.1, ...), custom_call_target="tpu_custom_call" | custom-call | tf_op jit(solution)/shard_map/mark/pallas_call | solution.py:45
  2.9 3.0 %collective-permute-start = (bf16[3,128,256]{2,1,0:T(8,128)(2,1)S(1)}, bf16[3,128,256]{2,1,0:T(8,128)(2,1)S(1)}, u32[]{:S(2)}, u32[]{:S(2)}) collective-permute-start(bf16[3,128,256]{2,1,0:T(8,128)(2,1)S(1)} %get-tuple-element.30), channel_id=1, source_target_pairs={{0,1},{1,2},{2,3},{3,4},{4,5},{5,6},{6,7},{7,8},{8,9},{9,10},{10,1... | collective-permute-start | bytes 589832 | tf_op jit(solution)/shard_map/ppermute | solution.py:579
  5.9 3.5 %collective-permute-start.1 = (bf16[3,128,256]{2,1,0:T(8,128)(2,1)S(1)}, bf16[3,128,256]{2,1,0:T(8,128)(2,1)S(1)}, u32[]{:S(2)}, u32[]{:S(2)}) collective-permute-start(bf16[3,128,256]{2,1,0:T(8,128)(2,1)S(1)} %get-tuple-element.31), channel_id=1, source_target_pairs={{1,0},{2,1},{3,2},{4,3},{5,4},{6,5},{7,6},{8,7},{9,8},{10,9},{11,1... | collective-permute-start | bytes 589832 | tf_op jit(solution)/shard_map/ppermute | solution.py:582
  9.4 1.9 %first_sums.1 = (f32[32,128]{1,0:T(8,128)}, bf16[8,128,256]{2,1,0:T(8,128)(2,1)}) custom-call(bf16[8,128,256]{2,1,0:T(8,128)(2,1)S(1)} %get-tuple-element.27.marked), custom_call_target="tpu_custom_call" | custom-call | tf_op jit(solution)/shard_map/first_sums/pallas_call | solution.py:45
  11.2 2.9 %all-to-all-start = ((f32[32,1,128]{2,1,0:T(1,128)}), f32[32,1,128]{2,1,0:T(1,128)S(1)}, u32[]{:S(2)}, u32[]{:S(2)}) async-start(f32[32,1,128]{2,1,0:T(1,128)} %bitcast.5), calls=%async_computation | async-start | bytes 32768 | tf_op jit(solution)/shard_map/all_to_all | solution.py:585
  14.1 1.8 %collective-permute-start.2 = (bf16[3,128,256]{2,1,0:T(8,128)(2,1)S(1)}, bf16[3,128,256]{2,1,0:T(8,128)(2,1)S(1)}, u32[]{:S(2)}, u32[]{:S(2)}) collective-permute-start(bf16[3,128,256]{2,1,0:T(8,128)(2,1)S(1)} %get-tuple-element.35), channel_id=1, source_target_pairs={{0,1},{1,2},{2,3},{3,4},{4,5},{5,6},{6,7},{7,8},{8,9},{9,10},{10,1... | collective-permute-start | bytes 589832 | tf_op jit(solution)/shard_map/ppermute | solution.py:579
  15.9 3.6 %collective-permute-start.3 = (bf16[3,128,256]{2,1,0:T(8,128)(2,1)S(1)}, bf16[3,128,256]{2,1,0:T(8,128)(2,1)S(1)}, u32[]{:S(2)}, u32[]{:S(2)}) collective-permute-start(bf16[3,128,256]{2,1,0:T(8,128)(2,1)S(1)} %get-tuple-element.36), channel_id=1, source_target_pairs={{1,0},{2,1},{3,2},{4,3},{5,4},{6,5},{7,6},{8,7},{9,8},{10,9},{11,1... | collective-permute-start | bytes 589832 | tf_op jit(solution)/shard_map/ppermute | solution.py:582
  19.5 2.0 %all-to-all-done = f32[32,1,128]{2,1,0:T(1,128)S(1)} async-done(((f32[32,1,128]{2,1,0:T(1,128)}), f32[32,1,128]{2,1,0:T(1,128)S(1)}, u32[]{:S(2)}, u32[]{:S(2)}) %all-to-all-start) | async-done | bytes 16416 | tf_op jit(solution)/shard_map/all_to_all | solution.py:585
  21.5 0.0 collective-permute-done.before
  21.5 0.0 collective-permute-done.1.after
  21.5 8.2 %first_conv.1 = (bf16[8,128,256]{2,1,0:T(8,128)(2,1)S(1)}, f32[32,128]{1,0:T(8,128)}, bf16[3,128,256]{2,1,0:T(8,128)(2,1)S(1)}, bf16[3,128,256]{2,1,0:T(8,128)(2,1)S(1)}, f32[8,256]{1,0:T(8,128)S(1)}) custom-call(s32[8,27]{1,0:T(8,128)} %get-tuple-element.26.index_hbm, s32[32]{0:T(128)} %counts_hbm.5, f32[32,128]{1,0:T(8,128)S(1)} %bitcast.24, ...), custom_call_target="tpu_custom_call" | custom-call | flops 9200000000 | tf_op jit(solution)/shard_map/first_conv/pallas_call | solution.py:45
  29.7 2.6 %all-to-all-start.1 = ((f32[32,1,128]{2,1,0:T(1,128)}), f32[32,1,128]{2,1,0:T(1,128)S(1)}, u32[]{:S(2)}, u32[]{:S(2)}) async-start(f32[32,1,128]{2,1,0:T(1,128)} %bitcast.9), calls=%async_computation.1 | async-start | bytes 32768 | tf_op jit(solution)/shard_map/all_to_all | solution.py:585
  32.3 1.7 %collective-permute-start.4 = (bf16[3,128,256]{2,1,0:T(8,128)(2,1)S(1)}, bf16[3,128,256]{2,1,0:T(8,128)(2,1)S(1)}, u32[]{:S(2)}, u32[]{:S(2)}) collective-permute-start(bf16[3,128,256]{2,1,0:T(8,128)(2,1)S(1)} %get-tuple-element.38), channel_id=1, source_target_pairs={{0,1},{1,2},{2,3},{3,4},{4,5},{5,6},{6,7},{7,8},{8,9},{9,10},{10,1... | collective-permute-start | bytes 589832 | tf_op jit(solution)/shard_map/ppermute | solution.py:579
  34.0 3.7 %collective-permute-start.5 = (bf16[3,128,256]{2,1,0:T(8,128)(2,1)S(1)}, bf16[3,128,256]{2,1,0:T(8,128)(2,1)S(1)}, u32[]{:S(2)}, u32[]{:S(2)}) collective-permute-start(bf16[3,128,256]{2,1,0:T(8,128)(2,1)S(1)} %get-tuple-element.39), channel_id=1, source_target_pairs={{1,0},{2,1},{3,2},{4,3},{5,4},{6,5},{7,6},{8,7},{9,8},{10,9},{11,1... | collective-permute-start | bytes 589832 | tf_op jit(solution)/shard_map/ppermute | solution.py:582
  37.7 0.0 collective-permute-done.2.before
  37.7 0.0 collective-permute-done.3.after
  37.7 6.6 %grad_conv.1.grad = f32[8,128,256]{2,1,0:T(8,128)S(1)} custom-call(s32[8,27]{1,0:T(8,128)} %get-tuple-element.26.index_hbm, bf16[8,128,256]{2,1,0:T(8,128)(2,1)} %cotangent.5, bf16[8,128,256]{2,1,0:T(8,128)(2,1)} %get-tuple-element.29.marked_hbm, bf16[3,128,256]{2,1,0:T(8,128)(2,1)S(1)} %collective-permute-done.2.before, ...), custom_call_target="tpu_custom_call" | custom-call | tf_op jit(solution)/shard_map/grad_conv/pallas_call | solution.py:45
  44.3 0.0 all-to-all-done.1
  44.3 2.3 %second_sums.1 = (f32[32,128]{1,0:T(8,128)}, f32[8,256]{1,0:T(8,128)S(1)}, bf16[3,128,256]{2,1,0:T(8,128)(2,1)S(1)}, bf16[3,128,256]{2,1,0:T(8,128)(2,1)S(1)}, bf16[8,128,256]{2,1,0:T(8,128)(2,1)}) custom-call(s32[32]{0:T(128)} %counts_hbm.5, f32[32,128]{1,0:T(8,128)S(1)} %bitcast.25, bf16[8,128,256]{2,1,0:T(8,128)(2,1)S(1)} %get-tuple-element.34.hidden, ...), custom_call_target="tpu_custom_call" | custom-call | flops 57500000256 | tf_op jit(solution)/shard_map/second_sums/pallas_call | solution.py:45
  46.7 2.5 %all-to-all-start.2 = ((f32[32,1,128]{2,1,0:T(1,128)}), f32[32,1,128]{2,1,0:T(1,128)S(1)}, u32[]{:S(2)}, u32[]{:S(2)}) async-start(f32[32,1,128]{2,1,0:T(1,128)} %bitcast.13), calls=%async_computation.2 | async-start | bytes 32768 | tf_op jit(solution)/shard_map/all_to_all | solution.py:585
  49.2 1.8 %collective-permute-start.6 = (bf16[3,128,256]{2,1,0:T(8,128)(2,1)S(1)}, bf16[3,128,256]{2,1,0:T(8,128)(2,1)S(1)}, u32[]{:S(2)}, u32[]{:S(2)}) collective-permute-start(bf16[3,128,256]{2,1,0:T(8,128)(2,1)S(1)} %get-tuple-element.43), channel_id=1, source_target_pairs={{0,1},{1,2},{2,3},{3,4},{4,5},{5,6},{6,7},{7,8},{8,9},{9,10},{10,1... | collective-permute-start | bytes 589832 | tf_op jit(solution)/shard_map/ppermute | solution.py:579
  51.0 3.6 %collective-permute-start.7 = (bf16[3,128,256]{2,1,0:T(8,128)(2,1)S(1)}, bf16[3,128,256]{2,1,0:T(8,128)(2,1)S(1)}, u32[]{:S(2)}, u32[]{:S(2)}) collective-permute-start(bf16[3,128,256]{2,1,0:T(8,128)(2,1)S(1)} %get-tuple-element.44), channel_id=1, source_target_pairs={{1,0},{2,1},{3,2},{4,3},{5,4},{6,5},{7,6},{8,7},{9,8},{10,9},{11,1... | collective-permute-start | bytes 589832 | tf_op jit(solution)/shard_map/ppermute | solution.py:582
  54.6 0.0 collective-permute-done.4.before.hid_before
  54.6 0.0 collective-permute-done.5.after.hid_after
  54.6 7.3 %second_conv.1 = (bf16[8,128,256]{2,1,0:T(8,128)(2,1)}, f32[8,128]{1,0:T(8,128)S(1)}) custom-call(s32[8,27]{1,0:T(8,128)} %get-tuple-element.26.index_hbm, bf16[8,128,256]{2,1,0:T(8,128)(2,1)} %get-tuple-element.37.hidden_hbm, bf16[3,128,256]{2,1,0:T(8,128)(2,1)S(1)} %collective-permute-done.4.before.hid_before, ...), custom_call_target="tpu_custom_call" | custom-call | flops 9200000000 | tf_op jit(solution)/shard_map/second_conv/pallas_call | solution.py:45
  61.9 0.0 all-to-all-done.2
  61.9 0.0 collective-permute-done.6.grad_before
  61.9 0.1 collective-permute-done.7.grad_after
  62.0 7.8 %back_conv.1 = (f32[8,128,256]{2,1,0:T(8,128)S(1)}, f32[8,128,256]{2,1,0:T(8,128)S(1)}, f32[32,128]{1,0:T(8,128)S(1)}) custom-call(s32[8,27]{1,0:T(8,128)} %get-tuple-element.26.index_hbm, f32[32,128]{1,0:T(8,128)S(1)} %bitcast.22, bf16[8,128,256]{2,1,0:T(8,128)(2,1)} %get-tuple-element.37.hidden_hbm, ...), custom_call_target="tpu_custom_call" | custom-call | tf_op jit(solution)/shard_map/back_conv/pallas_call | solution.py:45
  69.8 11.2 %all_to_all.44 = f32[32,1,128]{2,1,0:T(1,128)S(1)} all-to-all(f32[32,1,128]{2,1,0:T(1,128)S(1)} %bitcast.26), channel_id=1, replica_groups=mesh['region'=4,'sub'=8] {'region','sub'}, dimensions={0} | all-to-all | bytes 32768 | tf_op jit(solution)/shard_map/all_to_all | solution.py:585
  81.0 1.3 %end.1 = bf16[8,128,256]{2,1,0:T(8,128)(2,1)} custom-call(f32[32,128]{1,0:T(8,128)S(1)} %bitcast.23, f32[8,128,256]{2,1,0:T(8,128)S(1)} %get-tuple-element.48.partial, f32[8,128,256]{2,1,0:T(8,128)S(1)} %get-tuple-element.49.normed, f32[8,256]{1,0:T(8,128)S(1)} %get-tuple-element.45.stats_first.stats), custom_call_target="tpu_custom_call" | custom-call | tf_op jit(solution)/shard_map/end/pallas_call | solution.py:45
Async XLA Ops:
  2.9 18.7 %collective-permute-start = (bf16[3,128,256]{2,1,0:T(8,128)(2,1)S(1)}, bf16[3,128,256]{2,1,0:T(8,128)(2,1)S(1)}, u32[]{:S(2)}, u32[]{:S(2)}) collective-permute-start(bf16[3,128,256]{2,1,0:T(8,128)(2,1)S(1)} %get-tuple-element.30), channel_id=1, source_target_pairs={{0,1},{1,2},{2,3},{3,4},{4,5},{5,6},{6,7},{7,8},{8,9},{9,10},{10,1... | collective-permute-start | bytes 589832 | tf_op jit(solution)/shard_map/ppermute | solution.py:579
  5.9 15.6 %collective-permute-start.1 = (bf16[3,128,256]{2,1,0:T(8,128)(2,1)S(1)}, bf16[3,128,256]{2,1,0:T(8,128)(2,1)S(1)}, u32[]{:S(2)}, u32[]{:S(2)}) collective-permute-start(bf16[3,128,256]{2,1,0:T(8,128)(2,1)S(1)} %get-tuple-element.31), channel_id=1, source_target_pairs={{1,0},{2,1},{3,2},{4,3},{5,4},{6,5},{7,6},{8,7},{9,8},{10,9},{11,1... | collective-permute-start | bytes 589832 | tf_op jit(solution)/shard_map/ppermute | solution.py:582
  11.2 10.3 %all-to-all-start = ((f32[32,1,128]{2,1,0:T(1,128)}), f32[32,1,128]{2,1,0:T(1,128)S(1)}, u32[]{:S(2)}, u32[]{:S(2)}) async-start(f32[32,1,128]{2,1,0:T(1,128)} %bitcast.5), calls=%async_computation | async-start | bytes 32768 | tf_op jit(solution)/shard_map/all_to_all | solution.py:585
  14.1 23.6 %collective-permute-start.2 = (bf16[3,128,256]{2,1,0:T(8,128)(2,1)S(1)}, bf16[3,128,256]{2,1,0:T(8,128)(2,1)S(1)}, u32[]{:S(2)}, u32[]{:S(2)}) collective-permute-start(bf16[3,128,256]{2,1,0:T(8,128)(2,1)S(1)} %get-tuple-element.35), channel_id=1, source_target_pairs={{0,1},{1,2},{2,3},{3,4},{4,5},{5,6},{6,7},{7,8},{8,9},{9,10},{10,1... | collective-permute-start | bytes 589832 | tf_op jit(solution)/shard_map/ppermute | solution.py:579
  15.9 21.8 %collective-permute-start.3 = (bf16[3,128,256]{2,1,0:T(8,128)(2,1)S(1)}, bf16[3,128,256]{2,1,0:T(8,128)(2,1)S(1)}, u32[]{:S(2)}, u32[]{:S(2)}) collective-permute-start(bf16[3,128,256]{2,1,0:T(8,128)(2,1)S(1)} %get-tuple-element.36), channel_id=1, source_target_pairs={{1,0},{2,1},{3,2},{4,3},{5,4},{6,5},{7,6},{8,7},{9,8},{10,9},{11,1... | collective-permute-start | bytes 589832 | tf_op jit(solution)/shard_map/ppermute | solution.py:582
  29.7 14.6 %all-to-all-start.1 = ((f32[32,1,128]{2,1,0:T(1,128)}), f32[32,1,128]{2,1,0:T(1,128)S(1)}, u32[]{:S(2)}, u32[]{:S(2)}) async-start(f32[32,1,128]{2,1,0:T(1,128)} %bitcast.9), calls=%async_computation.1 | async-start | bytes 32768 | tf_op jit(solution)/shard_map/all_to_all | solution.py:585
  32.3 22.3 %collective-permute-start.4 = (bf16[3,128,256]{2,1,0:T(8,128)(2,1)S(1)}, bf16[3,128,256]{2,1,0:T(8,128)(2,1)S(1)}, u32[]{:S(2)}, u32[]{:S(2)}) collective-permute-start(bf16[3,128,256]{2,1,0:T(8,128)(2,1)S(1)} %get-tuple-element.38), channel_id=1, source_target_pairs={{0,1},{1,2},{2,3},{3,4},{4,5},{5,6},{6,7},{7,8},{8,9},{9,10},{10,1... | collective-permute-start | bytes 589832 | tf_op jit(solution)/shard_map/ppermute | solution.py:579
  34.0 20.6 %collective-permute-start.5 = (bf16[3,128,256]{2,1,0:T(8,128)(2,1)S(1)}, bf16[3,128,256]{2,1,0:T(8,128)(2,1)S(1)}, u32[]{:S(2)}, u32[]{:S(2)}) collective-permute-start(bf16[3,128,256]{2,1,0:T(8,128)(2,1)S(1)} %get-tuple-element.39), channel_id=1, source_target_pairs={{1,0},{2,1},{3,2},{4,3},{5,4},{6,5},{7,6},{8,7},{9,8},{10,9},{11,1... | collective-permute-start | bytes 589832 | tf_op jit(solution)/shard_map/ppermute | solution.py:582
  46.7 15.3 %all-to-all-start.2 = ((f32[32,1,128]{2,1,0:T(1,128)}), f32[32,1,128]{2,1,0:T(1,128)S(1)}, u32[]{:S(2)}, u32[]{:S(2)}) async-start(f32[32,1,128]{2,1,0:T(1,128)} %bitcast.13), calls=%async_computation.2 | async-start | bytes 32768 | tf_op jit(solution)/shard_map/all_to_all | solution.py:585
  49.2 12.7 %collective-permute-start.6 = (bf16[3,128,256]{2,1,0:T(8,128)(2,1)S(1)}, bf16[3,128,256]{2,1,0:T(8,128)(2,1)S(1)}, u32[]{:S(2)}, u32[]{:S(2)}) collective-permute-start(bf16[3,128,256]{2,1,0:T(8,128)(2,1)S(1)} %get-tuple-element.43), channel_id=1, source_target_pairs={{0,1},{1,2},{2,3},{3,4},{4,5},{5,6},{6,7},{7,8},{8,9},{9,10},{10,1... | collective-permute-start | bytes 589832 | tf_op jit(solution)/shard_map/ppermute | solution.py:579
  51.0 11.0 %collective-permute-start.7 = (bf16[3,128,256]{2,1,0:T(8,128)(2,1)S(1)}, bf16[3,128,256]{2,1,0:T(8,128)(2,1)S(1)}, u32[]{:S(2)}, u32[]{:S(2)}) collective-permute-start(bf16[3,128,256]{2,1,0:T(8,128)(2,1)S(1)} %get-tuple-element.44), channel_id=1, source_target_pairs={{1,0},{2,1},{3,2},{4,3},{5,4},{6,5},{7,6},{8,7},{9,8},{10,9},{11,1... | collective-permute-start | bytes 589832 | tf_op jit(solution)/shard_map/ppermute | solution.py:582

commit v5 on v4

--- a/solution.py
+++ b/solution.py
@@ -353,20 +353,19 @@
 
 
 def grad_conv_kernel(
-    index_hbm, cotangent, marked_hbm, before, after, weights_hbm,
-    grad, source, even, odd, weights, sem, index, index_sem, stage, stage_sem, marked, marked_sem,
+    index_hbm, cotangent, marked, before, after, weights_hbm,
+    grad, source, even, odd, weights, sem, index, index_sem, stage, stage_sem,
 ):
     capacity = marked.shape[0]
     indexing = Fetched(index_hbm, index, index_sem)
     own = Fetched(cotangent, stage, stage_sem)
-    marked = Fetched(marked_hbm, marked, marked_sem)
     fetch = pltpu.make_async_copy(weights_hbm, weights, sem)
     fetch.start()
     for k in range(EDGE):
         put_slot(source, capacity + k, before[k].astype(f32))
         put_slot(source, capacity + EDGE + k, after[k].astype(f32))
     put_slot(source, capacity + 2 * EDGE, jnp.zeros((128, 256), f32))
-    marked, stage = marked.ready(), own.ready()
+    own.ready()
 
     def own_slot(b, _):
         values = stage[b].astype(f32)
@@ -385,14 +384,13 @@
 
 
 def first_conv_kernel(
-    index_hbm, counts_hbm, rows, marked_hbm, before, after, vectors, weights_hbm,
+    index_hbm, counts_hbm, rows, marked, before, after, vectors, weights_hbm,
     hidden, row, up, down, stats, source, even, odd, weights, sem, index, index_sem,
-    marked_stage, marked_sem, counts, counts_sem,
+    counts, counts_sem,
 ):
     capacity = hidden.shape[0]
     indexing = Fetched(index_hbm, index, index_sem)
     counting = Fetched(counts_hbm, counts, counts_sem)
-    marked = Fetched(marked_hbm, marked_stage, marked_sem)
     fetch = pltpu.make_async_copy(weights_hbm, weights, sem)
     fetch.start()
     mean, inv_scale, voxel_total = combine_moments(rows[...])
@@ -413,7 +411,7 @@
     fetch.wait()
 
     def finish(b, total, carry):
-        on = marked_stage[b].astype(f32) < MARK_LIMIT
+        on = marked[b].astype(f32) < MARK_LIMIT
         rounded = total.astype(bf16).astype(f32)
         hidden[b] = jnp.where(on, rounded, MARK).astype(bf16)
         return add_moments(carry, rounded, on, b == 0)
@@ -612,19 +610,19 @@
     rows_first = exchange(row)
 
     (grad,) = call(
-        grad_conv_kernel, "grad_conv", [hbm(), hbm(), hbm(), vmem(), vmem(), hbm()],
-        [whole_wide], conv_scratch(slots, capacity) + [pltpu.VMEM(*whole), dma] * 2,
-    )(index, cotangent, marked, cot_before, cot_after, w_second)
+        grad_conv_kernel, "grad_conv", [hbm(), hbm(), vmem(), vmem(), vmem(), hbm()],
+        [whole_wide], conv_scratch(slots, capacity) + [pltpu.VMEM(*whole), dma],
+    )(index, cotangent, marked_near, cot_before, cot_after, w_second)
 
     hidden_near, row, hid_up, hid_down, stats_first = call(
         first_conv_kernel, "first_conv",
-        [hbm(), hbm(), vmem(), hbm(), vmem(), vmem(), vmem(), hbm()],
+        [hbm(), hbm(), vmem(), vmem(), vmem(), vmem(), vmem(), hbm()],
         [whole, packed, edge, edge, vector],
         conv_scratch(slots, capacity)
         + [
-            pltpu.VMEM(*whole), dma, pltpu.SMEM(counts.shape, jnp.int32), dma,
+            pltpu.SMEM(counts.shape, jnp.int32), dma,
         ],
-    )(index, counts, rows_first, marked, feat_before, feat_after, vectors, w_first)
+    )(index, counts, rows_first, marked_near, feat_before, feat_after, vectors, w_first)
     rows_second = exchange(row)
     hid_before, hid_after = shift_up(hid_up), shift_down(hid_down)
 

time: 82.5 us -> 82.2 us (level)
  no operation moved by 1% of the time
where the time goes in v5:
time: 82.2 us; the launch traced here: 81.9 us
  Pallas kernels  37.2 us (45%)
  starting transfers between devices  30.7 us (37%)
  blocking collectives  11.1 us (14%)
  waiting for transfers between devices  2.13 us (3%)
    pallas_call x8, Pallas kernels, run(): made(*(pltpu.with_memory_space_constraint(x, pltpu.HBM) if spec.memory_sp...  37.2 us
    ppermute x4, starting transfers between devices, shift_down(): lax.ppermute(x, AXES, [((i + 1) % devices, i) for i in range(devices)])  14.3 us
    all_to_all x1, blocking collectives, exchange(): return lax.all_to_all(row, AXES, 0, 0, tiled=True)  11.1 us
    ppermute x4, starting transfers between devices, shift_up(): lax.ppermute(x, AXES, [(i, (i + 1) % devices) for i in range(devices)])  8.37 us
    all_to_all x3, starting transfers between devices, exchange(): return lax.all_to_all(row, AXES, 0, 0, tiled=True)  7.98 us
    all_to_all x3, waiting for transfers between devices, exchange(): return lax.all_to_all(row, AXES, 0, 0, tiled=True)  2.02 us
  transfers between devices with their start and end apart: 11, of which 2 were waited for; matrix products, arithmetic and copies ran while one was open for 0% of the time, Pallas kernels for 32%

profile of v5, /device:TPU:0, one launch (start us, length us, event | category | flops | bytes accessed | tf_op | source)
XLA Modules:
  0.0 81.9 jit_solution(10617862257787986013)
XLA Ops:
  0.6 2.2 %mark.1 = (bf16[8,128,256]{2,1,0:T(8,128)(2,1)S(1)}, bf16[3,128,256]{2,1,0:T(8,128)(2,1)S(1)}, bf16[3,128,256]{2,1,0:T(8,128)(2,1)S(1)}, bf16[3,128,256]{2,1,0:T...) custom-call(s32[32]{0:T(128)} %counts_hbm.5, s32[8,27]{1,0:T(8,128)} %neighbors_hbm.1, ...), custom_call_target="tpu_custom_call" | custom-call | tf_op jit(solution)/shard_map/mark/pallas_call | solution.py:45
  2.9 3.0 %collective-permute-start = (bf16[3,128,256]{2,1,0:T(8,128)(2,1)S(1)}, bf16[3,128,256]{2,1,0:T(8,128)(2,1)S(1)}, u32[]{:S(2)}, u32[]{:S(2)}) collective-permute-start(bf16[3,128,256]{2,1,0:T(8,128)(2,1)S(1)} %get-tuple-element.29), channel_id=1, source_target_pairs={{0,1},{1,2},{2,3},{3,4},{4,5},{5,6},{6,7},{7,8},{8,9},{9,10},{10,1... | collective-permute-start | bytes 589832 | tf_op jit(solution)/shard_map/ppermute | solution.py:577
  5.9 3.5 %collective-permute-start.1 = (bf16[3,128,256]{2,1,0:T(8,128)(2,1)S(1)}, bf16[3,128,256]{2,1,0:T(8,128)(2,1)S(1)}, u32[]{:S(2)}, u32[]{:S(2)}) collective-permute-start(bf16[3,128,256]{2,1,0:T(8,128)(2,1)S(1)} %get-tuple-element.30), channel_id=1, source_target_pairs={{1,0},{2,1},{3,2},{4,3},{5,4},{6,5},{7,6},{8,7},{9,8},{10,9},{11,1... | collective-permute-start | bytes 589832 | tf_op jit(solution)/shard_map/ppermute | solution.py:580
  9.4 1.9 %first_sums.1 = (f32[32,128]{1,0:T(8,128)}, bf16[8,128,256]{2,1,0:T(8,128)(2,1)}) custom-call(bf16[8,128,256]{2,1,0:T(8,128)(2,1)S(1)} %get-tuple-element.27.marked), custom_call_target="tpu_custom_call" | custom-call | tf_op jit(solution)/shard_map/first_sums/pallas_call | solution.py:45
  11.2 2.9 %all-to-all-start = ((f32[32,1,128]{2,1,0:T(1,128)}), f32[32,1,128]{2,1,0:T(1,128)S(1)}, u32[]{:S(2)}, u32[]{:S(2)}) async-start(f32[32,1,128]{2,1,0:T(1,128)} %bitcast.5), calls=%async_computation | async-start | bytes 32768 | tf_op jit(solution)/shard_map/all_to_all | solution.py:583
  14.1 1.8 %collective-permute-start.2 = (bf16[3,128,256]{2,1,0:T(8,128)(2,1)S(1)}, bf16[3,128,256]{2,1,0:T(8,128)(2,1)S(1)}, u32[]{:S(2)}, u32[]{:S(2)}) collective-permute-start(bf16[3,128,256]{2,1,0:T(8,128)(2,1)S(1)} %get-tuple-element.34), channel_id=1, source_target_pairs={{0,1},{1,2},{2,3},{3,4},{4,5},{5,6},{6,7},{7,8},{8,9},{9,10},{10,1... | collective-permute-start | bytes 589832 | tf_op jit(solution)/shard_map/ppermute | solution.py:577
  15.9 3.6 %collective-permute-start.3 = (bf16[3,128,256]{2,1,0:T(8,128)(2,1)S(1)}, bf16[3,128,256]{2,1,0:T(8,128)(2,1)S(1)}, u32[]{:S(2)}, u32[]{:S(2)}) collective-permute-start(bf16[3,128,256]{2,1,0:T(8,128)(2,1)S(1)} %get-tuple-element.35), channel_id=1, source_target_pairs={{1,0},{2,1},{3,2},{4,3},{5,4},{6,5},{7,6},{8,7},{9,8},{10,9},{11,1... | collective-permute-start | bytes 589832 | tf_op jit(solution)/shard_map/ppermute | solution.py:580
  19.5 2.0 %all-to-all-done = f32[32,1,128]{2,1,0:T(1,128)S(1)} async-done(((f32[32,1,128]{2,1,0:T(1,128)}), f32[32,1,128]{2,1,0:T(1,128)S(1)}, u32[]{:S(2)}, u32[]{:S(2)}) %all-to-all-start) | async-done | bytes 16416 | tf_op jit(solution)/shard_map/all_to_all | solution.py:583
  21.5 0.0 collective-permute-done.before
  21.5 0.0 collective-permute-done.1.after
  21.5 8.0 %first_conv.1 = (bf16[8,128,256]{2,1,0:T(8,128)(2,1)S(1)}, f32[32,128]{1,0:T(8,128)}, bf16[3,128,256]{2,1,0:T(8,128)(2,1)S(1)}, bf16[3,128,256]{2,1,0:T(8,128)(2,1)S(1)}, f32[8,256]{1,0:T(8,128)S(1)}) custom-call(s32[8,27]{1,0:T(8,128)} %get-tuple-element.26.index_hbm, s32[32]{0:T(128)} %counts_hbm.5, f32[32,128]{1,0:T(8,128)S(1)} %bitcast.25, ...), custom_call_target="tpu_custom_call" | custom-call | flops 9200000000 | tf_op jit(solution)/shard_map/first_conv/pallas_call | solution.py:45
  29.6 2.6 %all-to-all-start.1 = ((f32[32,1,128]{2,1,0:T(1,128)}), f32[32,1,128]{2,1,0:T(1,128)S(1)}, u32[]{:S(2)}, u32[]{:S(2)}) async-start(f32[32,1,128]{2,1,0:T(1,128)} %bitcast.9), calls=%async_computation.1 | async-start | bytes 32768 | tf_op jit(solution)/shard_map/all_to_all | solution.py:583
  32.2 1.7 %collective-permute-start.4 = (bf16[3,128,256]{2,1,0:T(8,128)(2,1)S(1)}, bf16[3,128,256]{2,1,0:T(8,128)(2,1)S(1)}, u32[]{:S(2)}, u32[]{:S(2)}) collective-permute-start(bf16[3,128,256]{2,1,0:T(8,128)(2,1)S(1)} %get-tuple-element.37), channel_id=1, source_target_pairs={{0,1},{1,2},{2,3},{3,4},{4,5},{5,6},{6,7},{7,8},{8,9},{9,10},{10,1... | collective-permute-start | bytes 589832 | tf_op jit(solution)/shard_map/ppermute | solution.py:577
  33.9 3.7 %collective-permute-start.5 = (bf16[3,128,256]{2,1,0:T(8,128)(2,1)S(1)}, bf16[3,128,256]{2,1,0:T(8,128)(2,1)S(1)}, u32[]{:S(2)}, u32[]{:S(2)}) collective-permute-start(bf16[3,128,256]{2,1,0:T(8,128)(2,1)S(1)} %get-tuple-element.38), channel_id=1, source_target_pairs={{1,0},{2,1},{3,2},{4,3},{5,4},{6,5},{7,6},{8,7},{9,8},{10,9},{11,1... | collective-permute-start | bytes 589832 | tf_op jit(solution)/shard_map/ppermute | solution.py:580
  37.6 0.0 collective-permute-done.2.before
  37.6 0.0 collective-permute-done.3.after
  37.6 6.4 %grad_conv.1.grad = f32[8,128,256]{2,1,0:T(8,128)S(1)} custom-call(s32[8,27]{1,0:T(8,128)} %get-tuple-element.26.index_hbm, bf16[8,128,256]{2,1,0:T(8,128)(2,1)} %cotangent.5, bf16[8,128,256]{2,1,0:T(8,128)(2,1)S(1)} %get-tuple-element.27.marked, bf16[3,128,256]{2,1,0:T(8,128)(2,1)S(1)} %collective-permute-done.2.before, ...), custom_call_target="tpu_custom_call" | custom-call | tf_op jit(solution)/shard_map/grad_conv/pallas_call | solution.py:45
  44.0 0.0 all-to-all-done.1
  44.0 2.3 %second_sums.1 = (f32[32,128]{1,0:T(8,128)}, f32[8,256]{1,0:T(8,128)S(1)}, bf16[3,128,256]{2,1,0:T(8,128)(2,1)S(1)}, bf16[3,128,256]{2,1,0:T(8,128)(2,1)S(1)}, bf16[8,128,256]{2,1,0:T(8,128)(2,1)}) custom-call(s32[32]{0:T(128)} %counts_hbm.5, f32[32,128]{1,0:T(8,128)S(1)} %bitcast.24, bf16[8,128,256]{2,1,0:T(8,128)(2,1)S(1)} %get-tuple-element.33.hidden, ...), custom_call_target="tpu_custom_call" | custom-call | flops 57500000256 | tf_op jit(solution)/shard_map/second_sums/pallas_call | solution.py:45
  46.3 2.5 %all-to-all-start.2 = ((f32[32,1,128]{2,1,0:T(1,128)}), f32[32,1,128]{2,1,0:T(1,128)S(1)}, u32[]{:S(2)}, u32[]{:S(2)}) async-start(f32[32,1,128]{2,1,0:T(1,128)} %bitcast.13), calls=%async_computation.2 | async-start | bytes 32768 | tf_op jit(solution)/shard_map/all_to_all | solution.py:583
  48.9 1.8 %collective-permute-start.6 = (bf16[3,128,256]{2,1,0:T(8,128)(2,1)S(1)}, bf16[3,128,256]{2,1,0:T(8,128)(2,1)S(1)}, u32[]{:S(2)}, u32[]{:S(2)}) collective-permute-start(bf16[3,128,256]{2,1,0:T(8,128)(2,1)S(1)} %get-tuple-element.43), channel_id=1, source_target_pairs={{0,1},{1,2},{2,3},{3,4},{4,5},{5,6},{6,7},{7,8},{8,9},{9,10},{10,1... | collective-permute-start | bytes 589832 | tf_op jit(solution)/shard_map/ppermute | solution.py:577
  50.7 3.6 %collective-permute-start.7 = (bf16[3,128,256]{2,1,0:T(8,128)(2,1)S(1)}, bf16[3,128,256]{2,1,0:T(8,128)(2,1)S(1)}, u32[]{:S(2)}, u32[]{:S(2)}) collective-permute-start(bf16[3,128,256]{2,1,0:T(8,128)(2,1)S(1)} %get-tuple-element.44), channel_id=1, source_target_pairs={{1,0},{2,1},{3,2},{4,3},{5,4},{6,5},{7,6},{8,7},{9,8},{10,9},{11,1... | collective-permute-start | bytes 589832 | tf_op jit(solution)/shard_map/ppermute | solution.py:580
  54.3 0.0 collective-permute-done.4.before.hid_before
  54.3 0.0 collective-permute-done.5.after.hid_after
  54.3 7.3 %second_conv.1 = (bf16[8,128,256]{2,1,0:T(8,128)(2,1)}, f32[8,128]{1,0:T(8,128)S(1)}) custom-call(s32[8,27]{1,0:T(8,128)} %get-tuple-element.26.index_hbm, bf16[8,128,256]{2,1,0:T(8,128)(2,1)} %get-tuple-element.36.hidden_hbm, bf16[3,128,256]{2,1,0:T(8,128)(2,1)S(1)} %collective-permute-done.4.before.hid_before, ...), custom_call_target="tpu_custom_call" | custom-call | flops 9200000000 | tf_op jit(solution)/shard_map/second_conv/pallas_call | solution.py:45
  61.6 0.0 all-to-all-done.2
  61.6 0.0 collective-permute-done.6.grad_before
  61.6 0.1 collective-permute-done.7.grad_after
  61.7 7.8 %back_conv.1 = (f32[8,128,256]{2,1,0:T(8,128)S(1)}, f32[8,128,256]{2,1,0:T(8,128)S(1)}, f32[32,128]{1,0:T(8,128)S(1)}) custom-call(s32[8,27]{1,0:T(8,128)} %get-tuple-element.26.index_hbm, f32[32,128]{1,0:T(8,128)S(1)} %bitcast.22, bf16[8,128,256]{2,1,0:T(8,128)(2,1)} %get-tuple-element.36.hidden_hbm, ...), custom_call_target="tpu_custom_call" | custom-call | tf_op jit(solution)/shard_map/back_conv/pallas_call | solution.py:45
  69.5 11.1 %all_to_all.44 = f32[32,1,128]{2,1,0:T(1,128)S(1)} all-to-all(f32[32,1,128]{2,1,0:T(1,128)S(1)} %bitcast.26), channel_id=1, replica_groups=mesh['region'=4,'sub'=8] {'region','sub'}, dimensions={0} | all-to-all | bytes 32768 | tf_op jit(solution)/shard_map/all_to_all | solution.py:583
  80.6 1.3 %end.1 = bf16[8,128,256]{2,1,0:T(8,128)(2,1)} custom-call(f32[32,128]{1,0:T(8,128)S(1)} %bitcast.23, f32[8,128,256]{2,1,0:T(8,128)S(1)} %get-tuple-element.48.partial, f32[8,128,256]{2,1,0:T(8,128)S(1)} %get-tuple-element.49.normed, f32[8,256]{1,0:T(8,128)S(1)} %get-tuple-element.45.stats_first.stats), custom_call_target="tpu_custom_call" | custom-call | tf_op jit(solution)/shard_map/end/pallas_call | solution.py:45
Async XLA Ops:
  2.9 18.7 %collective-permute-start = (bf16[3,128,256]{2,1,0:T(8,128)(2,1)S(1)}, bf16[3,128,256]{2,1,0:T(8,128)(2,1)S(1)}, u32[]{:S(2)}, u32[]{:S(2)}) collective-permute-start(bf16[3,128,256]{2,1,0:T(8,128)(2,1)S(1)} %get-tuple-element.29), channel_id=1, source_target_pairs={{0,1},{1,2},{2,3},{3,4},{4,5},{5,6},{6,7},{7,8},{8,9},{9,10},{10,1... | collective-permute-start | bytes 589832 | tf_op jit(solution)/shard_map/ppermute | solution.py:577
  5.9 15.6 %collective-permute-start.1 = (bf16[3,128,256]{2,1,0:T(8,128)(2,1)S(1)}, bf16[3,128,256]{2,1,0:T(8,128)(2,1)S(1)}, u32[]{:S(2)}, u32[]{:S(2)}) collective-permute-start(bf16[3,128,256]{2,1,0:T(8,128)(2,1)S(1)} %get-tuple-element.30), channel_id=1, source_target_pairs={{1,0},{2,1},{3,2},{4,3},{5,4},{6,5},{7,6},{8,7},{9,8},{10,9},{11,1... | collective-permute-start | bytes 589832 | tf_op jit(solution)/shard_map/ppermute | solution.py:580
  11.2 10.3 %all-to-all-start = ((f32[32,1,128]{2,1,0:T(1,128)}), f32[32,1,128]{2,1,0:T(1,128)S(1)}, u32[]{:S(2)}, u32[]{:S(2)}) async-start(f32[32,1,128]{2,1,0:T(1,128)} %bitcast.5), calls=%async_computation | async-start | bytes 32768 | tf_op jit(solution)/shard_map/all_to_all | solution.py:583
  14.1 23.4 %collective-permute-start.2 = (bf16[3,128,256]{2,1,0:T(8,128)(2,1)S(1)}, bf16[3,128,256]{2,1,0:T(8,128)(2,1)S(1)}, u32[]{:S(2)}, u32[]{:S(2)}) collective-permute-start(bf16[3,128,256]{2,1,0:T(8,128)(2,1)S(1)} %get-tuple-element.34), channel_id=1, source_target_pairs={{0,1},{1,2},{2,3},{3,4},{4,5},{5,6},{6,7},{7,8},{8,9},{9,10},{10,1... | collective-permute-start | bytes 589832 | tf_op jit(solution)/shard_map/ppermute | solution.py:577
  15.9 21.6 %collective-permute-start.3 = (bf16[3,128,256]{2,1,0:T(8,128)(2,1)S(1)}, bf16[3,128,256]{2,1,0:T(8,128)(2,1)S(1)}, u32[]{:S(2)}, u32[]{:S(2)}) collective-permute-start(bf16[3,128,256]{2,1,0:T(8,128)(2,1)S(1)} %get-tuple-element.35), channel_id=1, source_target_pairs={{1,0},{2,1},{3,2},{4,3},{5,4},{6,5},{7,6},{8,7},{9,8},{10,9},{11,1... | collective-permute-start | bytes 589832 | tf_op jit(solution)/shard_map/ppermute | solution.py:580
  29.6 14.4 %all-to-all-start.1 = ((f32[32,1,128]{2,1,0:T(1,128)}), f32[32,1,128]{2,1,0:T(1,128)S(1)}, u32[]{:S(2)}, u32[]{:S(2)}) async-start(f32[32,1,128]{2,1,0:T(1,128)} %bitcast.9), calls=%async_computation.1 | async-start | bytes 32768 | tf_op jit(solution)/shard_map/all_to_all | solution.py:583
  32.2 22.1 %collective-permute-start.4 = (bf16[3,128,256]{2,1,0:T(8,128)(2,1)S(1)}, bf16[3,128,256]{2,1,0:T(8,128)(2,1)S(1)}, u32[]{:S(2)}, u32[]{:S(2)}) collective-permute-start(bf16[3,128,256]{2,1,0:T(8,128)(2,1)S(1)} %get-tuple-element.37), channel_id=1, source_target_pairs={{0,1},{1,2},{2,3},{3,4},{4,5},{5,6},{6,7},{7,8},{8,9},{9,10},{10,1... | collective-permute-start | bytes 589832 | tf_op jit(solution)/shard_map/ppermute | solution.py:577
  33.9 20.4 %collective-permute-start.5 = (bf16[3,128,256]{2,1,0:T(8,128)(2,1)S(1)}, bf16[3,128,256]{2,1,0:T(8,128)(2,1)S(1)}, u32[]{:S(2)}, u32[]{:S(2)}) collective-permute-start(bf16[3,128,256]{2,1,0:T(8,128)(2,1)S(1)} %get-tuple-element.38), channel_id=1, source_target_pairs={{1,0},{2,1},{3,2},{4,3},{5,4},{6,5},{7,6},{8,7},{9,8},{10,9},{11,1... | collective-permute-start | bytes 589832 | tf_op jit(solution)/shard_map/ppermute | solution.py:580
  46.3 15.3 %all-to-all-start.2 = ((f32[32,1,128]{2,1,0:T(1,128)}), f32[32,1,128]{2,1,0:T(1,128)S(1)}, u32[]{:S(2)}, u32[]{:S(2)}) async-start(f32[32,1,128]{2,1,0:T(1,128)} %bitcast.13), calls=%async_computation.2 | async-start | bytes 32768 | tf_op jit(solution)/shard_map/all_to_all | solution.py:583
  48.9 12.7 %collective-permute-start.6 = (bf16[3,128,256]{2,1,0:T(8,128)(2,1)S(1)}, bf16[3,128,256]{2,1,0:T(8,128)(2,1)S(1)}, u32[]{:S(2)}, u32[]{:S(2)}) collective-permute-start(bf16[3,128,256]{2,1,0:T(8,128)(2,1)S(1)} %get-tuple-element.43), channel_id=1, source_target_pairs={{0,1},{1,2},{2,3},{3,4},{4,5},{5,6},{6,7},{7,8},{8,9},{9,10},{10,1... | collective-permute-start | bytes 589832 | tf_op jit(solution)/shard_map/ppermute | solution.py:577
  50.7 11.0 %collective-permute-start.7 = (bf16[3,128,256]{2,1,0:T(8,128)(2,1)S(1)}, bf16[3,128,256]{2,1,0:T(8,128)(2,1)S(1)}, u32[]{:S(2)}, u32[]{:S(2)}) collective-permute-start(bf16[3,128,256]{2,1,0:T(8,128)(2,1)S(1)} %get-tuple-element.44), channel_id=1, source_target_pairs={{1,0},{2,1},{3,2},{4,3},{5,4},{6,5},{7,6},{8,7},{9,8},{10,9},{11,1... | collective-permute-start | bytes 589832 | tf_op jit(solution)/shard_map/ppermute | solution.py:580
